TPU v7x, 32 devices: a whole 2x2x4 slice. The times are simulated.
32 devices in a mesh: groups: 2 (over x), seq: 16 (over z, y, core).
Axes of the slice: x: 2, y: 2, z: 4, core: 2. Of those that a mesh axis runs over, the one named last changes fastest.
Arguments:
- queries: bfloat16 [1024, 4096], P(('groups', 'seq')), parts along dimension 0, may hold values from -10 to 10
- visual_keys: bfloat16 [16384, 512], P(('groups', 'seq')), parts along dimension 0, may hold values from -6 to 6
- hidden: bfloat16 [16384, 8192], P(('groups', 'seq')), parts along dimension 0, may hold values from -6 to 6
- keep_count: int32 [32], P(('groups', 'seq')), parts along dimension 0, may hold values from 0 to 512, as said below
- keep_index: int32 [16384], P(('groups', 'seq')), parts along dimension 0, may hold values from 0 to 511, as said below
- norm_gain: float32 [8192], replicated, may hold values from 0.25 to 1.75
- kv_weight: bfloat16 [8192, 1024], replicated, may hold values from -0.0625 to 0.0625
- kv_bias: float32 [1024], replicated, may hold values from -3 to 3
Outputs:
- importance: float32 [16384], P(('groups', 'seq')), parts along dimension 0
- layer_kv: bfloat16 [8192, 1024], P(('groups', 'seq')), parts along dimension 0
There are 2 independent parts, one for each index of `groups`. A program takes and returns all parts, laid end to end along the dimension named above; an argument that names none is the same for every part. Nothing has to cross between parts.
Inputs may be any that keep to these rules, and one draw needn't show every extreme that they name: keep_count sums to 16 * 256 over one part; some device keeps all its rows and some none. `keep_index`: each device's block of 512 entries lists first its kept rows, distinct and ascending, as many as its count, then its other rows; entries are row numbers within the device's block.
All inputs are finite; a program needn't handle non-finite values.
Results may differ from a plain program's by a relative error of at most 0.0046.
Values may be sent and summed in bfloat16 or wider, within the bound.
No kernel may reach another device: no remote copies, remote signals or barrier semaphores. Data moves between devices by JAX's collectives and lax.ppermute only.
A program may use at most 192 MiB of HBM per device.

v0:
```python
import jax
import jax.numpy as jnp
from jax import lax
from jax.sharding import PartitionSpec as P

HD = 128


def merged(x, axis, combine):
    everything = jax.tree.map(lambda part: lax.all_gather(part, axis), x)
    leading = jax.tree.map(lambda part: part[0], everything)

    def turn(k, so_far):
        return combine(so_far, jax.tree.map(lambda part: part[k], everything))

    return lax.fori_loop(1, lax.axis_size(axis), turn, leading)


def combine_totals(left_pair, right_pair):
    row_top = jnp.maximum(left_pair[0], right_pair[0])
    row_total = left_pair[1] * jnp.exp(left_pair[0] - row_top) + right_pair[1] * jnp.exp(
        right_pair[0] - row_top
    )
    return (row_top, row_total)


def rms_project(row_block, norm_gain, kv_weight, kv_bias):
    values = row_block.astype(jnp.float32)
    mean_sq = jnp.mean(values * values, axis=-1, keepdims=True)
    normed = (values * lax.rsqrt(mean_sq + 1e-06) * norm_gain).astype(jnp.bfloat16)
    return (jnp.dot(normed, kv_weight, preferred_element_type=jnp.float32) + kv_bias).astype(
        jnp.bfloat16
    )


def shards(queries, visual_keys, hidden, keep_count, keep_index, norm_gain, kv_weight, kv_bias):
    seq_size = lax.axis_size("seq")
    my_index = lax.axis_index("seq")
    key_rows = visual_keys.shape[0]
    kv_heads = visual_keys.shape[1] // HD
    all_queries = lax.all_gather(queries, "seq", axis=0, tiled=True)
    total_q = all_queries.shape[0]
    head_count = all_queries.shape[1] // HD
    group_size = head_count // kv_heads
    q_split = all_queries.reshape(total_q, kv_heads, group_size, HD)
    k_split = visual_keys.reshape(key_rows, kv_heads, HD)
    scores = jnp.einsum(
        "tkgd,vkd->kgtv", q_split, k_split, preferred_element_type=jnp.float32
    ) * HD ** (-0.5)
    local_top = jnp.max(scores, axis=-1)
    local_total = jnp.sum(jnp.exp(scores - local_top[..., None]), axis=-1)
    row_top, row_total = merged((local_top, local_total), "seq", combine_totals)
    weights = jnp.exp(scores - row_top[..., None]) / row_total[..., None]
    importance = jnp.sum(weights, axis=(0, 1, 2)) * (key_rows * seq_size / (head_count * total_q))
    counts = lax.all_gather(keep_count, "seq", axis=0, tiled=True)
    run_ends = jnp.cumsum(counts)
    starts = run_ends - counts
    slot_cap = key_rows // seq_size
    keep_rows = key_rows // 2
    my_start = starts[my_index]
    owners = jnp.arange(seq_size, dtype=jnp.int32)[:, None]
    column = jnp.arange(slot_cap, dtype=jnp.int32)[None, :]
    send_pos = jnp.minimum(
        (owners - my_start) % seq_size + column * seq_size, key_rows - 1
    ).reshape(-1)
    recv_pos = (my_index - starts[:, None]) % seq_size + column * seq_size
    recv_slot = jnp.where(
        recv_pos < counts[:, None], (starts[:, None] + recv_pos) // seq_size, keep_rows
    ).reshape(-1)
    gathered = jnp.take(hidden, keep_index, axis=0)
    projected = rms_project(gathered, norm_gain, kv_weight, kv_bias)
    picked = jnp.take(projected, send_pos, axis=0).reshape(seq_size, slot_cap, projected.shape[1])
    arrived = lax.all_to_all(picked, "seq", split_axis=0, concat_axis=0, tiled=True)
    layer_kv = (
        jnp.zeros((keep_rows, projected.shape[1]), jnp.bfloat16)
        .at[recv_slot]
        .set(arrived.reshape(seq_size * slot_cap, projected.shape[1]), mode="drop")
    )
    return (importance, layer_kv)


def solution(mesh):
    placed = (
        P(("groups", "seq"), None),
        P(("groups", "seq"), None),
        P(("groups", "seq"), None),
        P(("groups", "seq")),
        P(("groups", "seq")),
        P(),
        P(),
        P(),
    )
    return jax.shard_map(
        shards,
        mesh=mesh,
        in_specs=placed,
        out_specs=(P(("groups", "seq")), P(("groups", "seq"), None)),
        check_vma=False,
    )
```

profile of v0, /device:TPU:0, one launch (start us, length us, event | category | flops | bytes accessed | tf_op | source)
XLA Modules:
  0.0 210.4 jit_solution(15245506369441247073)
XLA Ops:
  7.2 0.0 all-gather.6.cloned.1.call-start
  7.2 0.7 all-gather.6.cloned.1.call-update
  7.9 0.0 all-gather.8.cloned.1.call-start
  8.6 1.2 dynamic-slice
  9.8 0.8 dynamic-update-slice
  10.6 13.8 %all-reduce = s32[16]{0:T(128)S(1)} all-reduce(s32[16]{0:T(128)S(1)} %dynamic-update-slice), channel_id=1, replica_groups=mesh['groups'=2,'seq'=16] {'seq'}, use_global_device_ids=true, to_apply=%add | all-reduce | flops 16 | bytes 128
  24.4 1.2 reshape.245
  25.6 0.1 copy.19
  25.7 0.1 reduce
  25.8 0.6 dynamic_slice.23
  26.4 0.7 and_select_fusion.1
  27.1 0.1 add_minimum_fusion
  27.2 0.1 min.25
  27.3 0.7 compare_select_fusion.3
  27.9 0.0 copy-start
  28.0 0.0 copy-start.1
  28.0 0.0 copy-start.2
  28.0 20.0 %gather_fusion = bf16[512,8192]{1,0:T(8,128)(2,1)} fusion(bf16[512,8192]{1,0:T(8,128)(2,1)} %param.12, s32[1024]{0:T(1024)S(1)} %pad_clamp_fusion.1), kind=kCustom, calls=%fused_computation | custom fusion | bytes 16779264 | tf_op jit(solution)/shard_map/jit(_take)/gather | solution.py:70
  48.0 0.0 copy-done
  48.0 5.8 %fusion.7 = f32[512]{0:T(512)S(1)} fusion(bf16[512,8192]{1,0:T(8,128)(2,1)} %gather_fusion, pred[512]{0:T(512)(128)(4,1)S(1)} %compare_and_fusion.1), kind=kLoop, calls=%fused_computation.18 | loop fusion | flops 16776704 | bytes 8391168 | tf_op jit(solution)/shard_map/reduce_sum | solution.py:29
  53.8 0.0 copy-done.1
  53.8 0.0 copy-done.2
  53.8 15.3 %add_convert_fusion = bf16[512,1024]{1,0:T(8,128)(2,1)S(1)} fusion(bf16[8192,1024]{1,0:T(8,128)(2,1)} %param.16, f32[8192]{0:T(1024)S(1)} %copy-done.1, f32[512]{0:T(512)S(1)} %add_rsqrt_fusion, bf16[512,8192]{1,0:T(8,128)(2,1)} %gather_fusion, pred[512]{0:T(512)(128)(4,1)S(1)} %compare_and_fusion.1, f32[1024]{0:T(1024)S(1)} %copy-done.2), kind=kOutput, calls=%fused_computation.25 | convolution fusion | flops 8611954688 | bytes 26253824 | tf_op jit(solution)/shard_map/dot_general | solution.py:31
  69.0 2.1 gather_fusion.1
  71.1 0.1 compare_and_fusion
  71.2 0.0 all-gather.6.cloned.1.call-done
  71.2 6.4 %copy.16 = bf16[512,4096]{0,1:T(8,128)(2,1)} copy(bf16[512,4096]{1,0:T(8,128)(2,1)} %all-gather.6.cloned.1.call-done) | data formatting | bytes 8388608 | tf_op jit(solution)/shard_map/all_gather | solution.py:41
  77.7 15.9 %bitcast_reduce_fusion = (f32[4,8,512]{2,1,0:T(8,128)}, f32[4,512,512,8]{2,1,3,0:T(8,128)}) fusion(bf16[512,4,8,128]{0,3,2,1:T(8,128)(2,1)} %bitcast.41, bf16[512,4,128,1]{2,1,0,3:T(4,128)(2,1)S(1)} %bitcast.43), kind=kOutput, calls=%fused_computation.10 | convolution fusion | flops 2164244480 | bytes 38338560 | tf_op jit(solution)/shard_map/tkgd,vkd->kgtv/dot_general | solution.py:47
  93.6 0.0 all-gather.8.cloned.1.call-update
  93.6 1.1 broadcast_select_fusion.2
  94.8 3.7 %all-to-all-start = ((bf16[16,32,1024]{2,1,0:T(8,128)(2,1)}), bf16[16,32,1024]{2,1,0:T(8,128)(2,1)S(1)}, u32[]{:S(2)}, u32[]{:S(2)}) async-start(bf16[16,32,1024]{2,1,0:T(8,128)(2,1)} %broadcast_select_fusion.2), calls=%async_computation | async-start | bytes 2097152 | tf_op jit(solution)/shard_map/all_to_all | solution.py:73
  98.4 0.0 all-gather.10.cloned.1.call-start
  98.5 14.2 %fusion.3 = f32[4,8,512]{2,1,0:T(8,128)} fusion(f32[4,512,512,8]{2,1,3,0:T(8,128)} %get-tuple-element.156, f32[4,8,512]{2,1,0:T(8,128)} %get-tuple-element.155), kind=kLoop, calls=%fused_computation.12 | loop fusion | flops 25149440 | bytes 33685504 | tf_op jit(solution)/shard_map/reduce_sum | solution.py:51
  112.7 0.0 all-gather.10.cloned.1.call-update
  112.7 0.1 lt.92
  112.8 0.1 add.204
  112.9 10.5 %all-to-all-done = bf16[16,32,1024]{2,1,0:T(8,128)(2,1)S(1)} async-done(((bf16[16,32,1024]{2,1,0:T(8,128)(2,1)}), bf16[16,32,1024]{2,1,0:T(8,128)(2,1)S(1)}, u32[]{:S(2)}, u32[]{:S(2)}) %all-to-all-start) | async-done | bytes 1048608 | tf_op jit(solution)/shard_map/all_to_all | solution.py:73
  123.5 3.4 %scatter_custom_fusion = bf16[256,1024]{1,0:T(8,128)(2,1)} fusion(s32[512]{0:T(512)S(1)} %bitcast.49, bf16[512,1024]{1,0:T(8,128)(2,1)S(1)} %bitcast.44, bf16[]{:T(256)} %constant.112.clone.1), kind=kCustom, calls=%fused_computation.29 | custom fusion | bytes 524290 | tf_op jit(solution)/shard_map/scatter | solution.py:77
  126.9 7.6 %all-gather.8.cloned.1.call-done = f32[64,8,512]{2,1,0:T(8,128)} async-done(((f32[4,8,512]{2,1,0:T(8,128)}), f32[64,8,512]{2,1,0:T(8,128)}) %all-gather.8.cloned.1.call-update) | async-done | bytes 1048592 | tf_op jit(solution)/shard_map/all_gather | solution.py:10
  134.5 0.8 slice.14
  135.4 38.3 %all-gather.10.cloned.1.call-done = f32[64,8,512]{2,1,0:T(8,128)} async-done(((f32[4,8,512]{2,1,0:T(8,128)}), f32[64,8,512]{2,1,0:T(8,128)}) %all-gather.10.cloned.1.call-update) | async-done | bytes 1048592 | tf_op jit(solution)/shard_map/all_gather | solution.py:10
  173.6 0.8 slice.15
  174.5 14.4 %while.17 = (s32[]{:T(128)}, f32[4,8,512]{2,1,0:T(8,128)S(1)}, f32[4,8,512]{2,1,0:T(8,128)S(1)}, f32[16,4,8,512]{3,2,1,0:T(8,128)}, f32[16,4,8,512]{3,2,1,0:T(8,128)}, /*index=5*/s32[]{:T(128)}, s32[]{:T(128)}, s32[]{:T(128)}) while((s32[]{:T(128)}, f32[4,8,512]{2,1,0:T(8,128)S(1)}, f32[4,8,512]{2,1,0:T(8,128)S(1)}, ...), condition=%wide.region_3.0_spmd, body=%wide.region_2.0_spmd.sunk | while | flops 98309 | bytes 393347 | solution.py:16
  174.5 0.9 fusion.26
  175.4 0.9 fusion.26
  176.4 0.9 fusion.26
  177.4 0.9 fusion.26
  178.3 0.9 fusion.26
  179.3 0.9 fusion.26
  180.2 0.9 fusion.26
  181.2 0.9 fusion.26
  182.2 0.9 fusion.26
  183.1 0.9 fusion.26
  184.1 0.9 fusion.26
  185.1 0.9 fusion.26
  186.0 0.9 fusion.26
  187.0 0.9 fusion.26
  187.9 0.9 fusion.26
  188.9 14.4 %fusion.6 = f32[512]{0:T(512)S(1)} fusion(f32[4,512,512,8]{2,1,3,0:T(8,128)} %get-tuple-element.156, f32[4,8,512]{2,1,0:T(8,128)S(1)} %get-tuple-element.136, f32[4,8,512]{2,1,0:T(8,128)S(1)} %get-tuple-element.135), kind=kLoop, calls=%fused_computation.15 | loop fusion | flops 33553920 | bytes 33687552 | tf_op jit(solution)/shard_map/reduce_sum | solution.py:54
  203.2 0.6 broadcast_multiply_fusion
  (10 shorter events, 0.1 us)
Async XLA Ops:
  7.2 64.0 %all-gather.6.cloned.1.call-start = ((), (), s32[]{:S(2)}) async-start(), calls=%async_computation.1 | async-start | bytes 4456448 | tf_op jit(solution)/shard_map/all_gather | solution.py:41
  7.9 126.6 %all-gather.8.cloned.1.call-start = ((), (), s32[]{:S(2)}) async-start(), calls=%async_computation.2 | async-start | bytes 1114112 | tf_op jit(solution)/shard_map/all_gather | solution.py:10
  27.9 20.0 %copy-start = (s32[512]{0:T(512)S(1)}, s32[512]{0:T(512)}, u32[]{:S(2)}) copy-start(s32[512]{0:T(512)} %param.14) | copy-start | bytes 6148
  28.0 25.8 %copy-start.1 = (f32[8192]{0:T(1024)S(1)}, f32[8192]{0:T(1024)}, u32[]{:S(2)}) copy-start(f32[8192]{0:T(1024)} %param.15) | copy-start | bytes 98308
  28.0 25.8 %copy-start.2 = (f32[1024]{0:T(1024)S(1)}, f32[1024]{0:T(1024)}, u32[]{:S(2)}) copy-start(f32[1024]{0:T(1024)} %param.17) | copy-start | bytes 12292
  94.8 28.7 %all-to-all-start = ((bf16[16,32,1024]{2,1,0:T(8,128)(2,1)}), bf16[16,32,1024]{2,1,0:T(8,128)(2,1)S(1)}, u32[]{:S(2)}, u32[]{:S(2)}) async-start(bf16[16,32,1024]{2,1,0:T(8,128)(2,1)} %broadcast_select_fusion.2), calls=%async_computation | async-start | bytes 2097152 | tf_op jit(solution)/shard_map/all_to_all | solution.py:73
  98.4 75.2 %all-gather.10.cloned.1.call-start = ((), (), s32[]{:S(2)}) async-start(), calls=%async_computation.3 | async-start | bytes 1114112 | tf_op jit(solution)/shard_map/all_gather | solution.py:10
Sparse Core Ops, SparseCore 0:
  10.2 53.4 all-gather.5
  93.7 40.7 all-gather.7
  136.7 36.8 all-gather.9
where the time goes:
time: 212 us; the launch traced here: 210 us
  waiting for transfers between devices  57.2 us (27%)
  other arithmetic  51.9 us (24%)
  local copies, waits for them, and re-layouts  37.7 us (18%)
  matrix products  31.2 us (15%)
  between operations  14.5 us (7%)
  blocking collectives  13.8 us (7%)
  starting transfers between devices  3.77 us (2%)
    all_gather x2, waiting for transfers between devices, merged(): everything = jax.tree.map(lambda part: lax.all_gather(part, axis), x)  45.9 us
    gather x1, local copies, waits for them, and re-layouts, shards(): gathered = jnp.take(hidden, keep_index, axis=0)  20 us
    dot_general x1, matrix products, shards(): jnp.einsum('tkgd,vkd->kgtv', q_split, k_split, preferred_element_type=jnp...  15.9 us
    dot_general x1, matrix products, rms_project(): jnp.dot(normed, kv_weight, preferred_element_type=jnp.float32) + kv_bias  15.3 us
    reduce_sum x1, other arithmetic, shards(): jnp.sum(weights, axis=(0, 1, 2))  14.4 us
    reduce_sum x1, other arithmetic, shards(): local_total = jnp.sum(jnp.exp(scores - local_top[..., None]), axis=-1)  14.2 us
    add x15, other arithmetic, combine_totals(): left_pair[1] * jnp.exp(left_pair[0] - row_top)  14.1 us
    unnamed x1, blocking collectives  13.8 us
  transfers between devices with their start and end apart: 4, of which 3 were waited for; matrix products, arithmetic and copies ran while one was open for 33% of the time, Pallas kernels for 0%

commit v1 on v0

v1 whole, which is shorter than its diff:
```python
import functools

import jax
import jax.numpy as jnp
from jax import lax
from jax.experimental import pallas as pl
from jax.experimental.pallas import tpu as pltpu
from jax.sharding import PartitionSpec as P

HD = 128
CELL = 8
EPS = 1e-06
F32 = jnp.float32
BF16 = jnp.bfloat16
LOG2E = 1.4426950408889634
MIB = 1024 * 1024


def params(mib):
    return pltpu.CompilerParams(vmem_limit_bytes=mib * MIB)


def cost(flops, bytes_accessed, transcendentals=0):
    return pl.CostEstimate(
        flops=int(flops), bytes_accessed=int(bytes_accessed), transcendentals=int(transcendentals)
    )


def project_kernel(x_ref, gain_ref, weight_ref, bias_ref, out_ref, total, squares):
    step = pl.program_id(0)
    values = x_ref[...].astype(F32)
    scaled = (values * gain_ref[...]).astype(BF16)
    part = jnp.dot(scaled, weight_ref[...], preferred_element_type=F32)
    square = values * values
    lanes = square[:, :128]
    for col in range(128, square.shape[1], 128):
        lanes = lanes + square[:, col : col + 128]

    @pl.when(step == 0)
    def _():
        total[...] = part
        squares[...] = lanes

    @pl.when(step > 0)
    def _():
        total[...] += part
        squares[...] += lanes

    @pl.when(step == pl.num_programs(0) - 1)
    def _():
        width = x_ref.shape[1] * pl.num_programs(0)
        mean_sq = jnp.sum(squares[...], axis=1, keepdims=True) * (1.0 / width)
        out_ref[...] = (total[...] * lax.rsqrt(mean_sq + EPS) + bias_ref[...]).astype(BF16)


def project(hidden, gain, weight, bias, depth=1024):
    rows, width = hidden.shape
    cols = weight.shape[1]
    return pl.pallas_call(
        project_kernel,
        grid=(width // depth,),
        in_specs=[
            pl.BlockSpec((rows, depth), lambda k: (0, k)),
            pl.BlockSpec((1, depth), lambda k: (0, k)),
            pl.BlockSpec((depth, cols), lambda k: (k, 0)),
            pl.BlockSpec((1, cols), lambda k: (0, 0)),
        ],
        out_specs=pl.BlockSpec((rows, cols), lambda k: (0, 0)),
        out_shape=jax.ShapeDtypeStruct((rows, cols), BF16),
        scratch_shapes=[pltpu.VMEM((rows, cols), F32), pltpu.VMEM((rows, 128), F32)],
        compiler_params=params(32),
        cost_estimate=cost(2 * rows * width * cols, 2 * width * (rows + cols)),
        name="project",
    )(hidden, gain.reshape(1, -1), weight, bias.reshape(1, -1))


def start_of(counts_ref, me, upto, size):
    total = jnp.int32(0)
    for r in range(size):
        total += jnp.where((me ^ r) < upto, counts_ref[r], 0)
    return total


def pick_kernel(size, me_ref, counts_ref, keep_ref, rows_ref, out_ref):
    me = me_ref[0]
    start = start_of(counts_ref, me, me, size)
    count = rows_ref.shape[0]
    cap = count // size
    slot = lax.broadcasted_iota(jnp.int32, (count, count), 0)
    entry = lax.broadcasted_iota(jnp.int32, (count, count), 1)
    owner = slot // cap
    wanted = ((owner - start) & (size - 1)) + (slot & (cap - 1)) * size
    chooses = (wanted == entry).astype(F32).astype(BF16)
    row = lax.broadcasted_iota(jnp.int32, (count, count), 0)
    listed = (keep_ref[...] == row).astype(F32).astype(BF16)
    select = lax.dot_general(
        chooses, listed, (((1,), (1,)), ((), ())), preferred_element_type=F32
    ).astype(BF16)
    out_ref[...] = jnp.dot(select, rows_ref[...], preferred_element_type=F32).astype(BF16)


def pick(me, counts, keep_index, rows, size):
    smem = pl.BlockSpec(memory_space=pltpu.SMEM)
    vmem = pl.BlockSpec(memory_space=pltpu.VMEM)
    n = rows.shape[0]
    return pl.pallas_call(
        functools.partial(pick_kernel, size),
        in_specs=[smem, smem, vmem, vmem],
        out_specs=vmem,
        out_shape=jax.ShapeDtypeStruct(rows.shape, BF16),
        compiler_params=params(32),
        cost_estimate=cost(2 * n * n * (n + rows.shape[1]), 4 * rows.size),
        name="pick",
    )(me, counts, keep_index.reshape(1, -1), rows)


def place_kernel(size, me_ref, counts_ref, rows_ref, out_ref):
    me = me_ref[0]
    keep, count = out_ref.shape[0], rows_ref.shape[0]
    cap = count // size
    slot = lax.broadcasted_iota(jnp.int32, (1, count), 1)
    source = slot // cap
    starts = jnp.zeros((1, count), jnp.int32)
    counts = jnp.zeros((1, count), jnp.int32)
    so_far = jnp.int32(0)
    for s in range(size):
        here = counts_ref[me ^ s]
        starts = jnp.where(source == s, so_far, starts)
        counts = jnp.where(source == s, here, counts)
        so_far += here
    pos = ((me - starts) & (size - 1)) + (slot & (cap - 1)) * size
    target = jnp.where(pos < counts, (starts + pos) // size, keep)
    row = lax.broadcasted_iota(jnp.int32, (keep, count), 0)
    select = (row == target).astype(F32).astype(BF16)
    out_ref[...] = jnp.dot(select, rows_ref[...], preferred_element_type=F32).astype(BF16)


def place(me, counts, rows, keep, size):
    smem = pl.BlockSpec(memory_space=pltpu.SMEM)
    vmem = pl.BlockSpec(memory_space=pltpu.VMEM)
    return pl.pallas_call(
        functools.partial(place_kernel, size),
        in_specs=[smem, smem, vmem],
        out_specs=vmem,
        out_shape=jax.ShapeDtypeStruct((keep, rows.shape[1]), BF16),
        compiler_params=params(32),
        cost_estimate=cost(2 * keep * rows.size, 3 * rows.size),
        name="place",
    )(me, counts, rows)


def prepare_kernel(me_ref, keys_ref, *out_refs):
    me = me_ref[0] & (CELL - 1)
    for i, out_ref in enumerate(out_refs):
        head = (me ^ (2 * i)) // 2
        out_ref[...] = keys_ref[:, pl.ds(pl.multiple_of(head * HD, HD), HD)]


def prepare(me, keys):
    n = CELL // 2
    smem = pl.BlockSpec(memory_space=pltpu.SMEM)
    vmem = pl.BlockSpec(memory_space=pltpu.VMEM)
    block = jax.ShapeDtypeStruct((keys.shape[0], HD), BF16)
    return pl.pallas_call(
        prepare_kernel,
        in_specs=[smem, vmem],
        out_specs=[vmem] * n,
        out_shape=[block] * n,
        compiler_params=params(16),
        cost_estimate=cost(0, 4 * keys.size),
        name="prepare",
    )(me, keys)


def score_kernel(chunk, q_ref, even_ref, odd_ref, prob_ref, top_ref, lse_ref):
    scale = HD**-0.5 * LOG2E
    query = q_ref[...]
    tops, sums = [], []
    half = even_ref.shape[0]
    for c in range(2 * half // chunk):
        ref, at = (even_ref, c * chunk) if c * chunk < half else (odd_ref, c * chunk - half)
        s = lax.dot_general(
            ref[at : at + chunk, :], query, (((1,), (1,)), ((), ())), preferred_element_type=F32
        )
        top = jnp.max(s, axis=0, keepdims=True)
        p = jnp.exp2((s - top) * scale)
        sums.append(jnp.sum(p, axis=0, keepdims=True))
        tops.append(top * scale)
        prob_ref[c * chunk : (c + 1) * chunk, :] = p.astype(BF16)
    top_all = functools.reduce(jnp.maximum, tops)
    total = sum(part * jnp.exp2(top - top_all) for part, top in zip(sums, tops))
    top_ref[...] = jnp.concatenate(tops, axis=0)
    lse_ref[...] = top_all + jnp.log2(total)


def score(q, even, odd, chunk=512, tile=256):
    tokens, width = q.shape
    heads = width // HD
    keys = 2 * even.shape[0]
    rows = tokens * heads
    tile = min(tile, tokens)
    per = tokens // tile
    chunks = keys // chunk
    return pl.pallas_call(
        functools.partial(score_kernel, chunk),
        grid=(rows // tile,),
        in_specs=[
            pl.BlockSpec((tile, HD), lambda i: (i % per, i // per)),
            pl.BlockSpec(even.shape, lambda i: (0, 0)),
            pl.BlockSpec(odd.shape, lambda i: (0, 0)),
        ],
        out_specs=[
            pl.BlockSpec((keys, tile), lambda i: (0, i)),
            pl.BlockSpec((chunks, tile), lambda i: (0, i)),
            pl.BlockSpec((1, tile), lambda i: (0, i)),
        ],
        out_shape=[
            jax.ShapeDtypeStruct((keys, rows), BF16),
            jax.ShapeDtypeStruct((chunks, rows), F32),
            jax.ShapeDtypeStruct((1, rows), F32),
        ],
        compiler_params=params(40),
        cost_estimate=cost(2 * rows * keys * HD, 2 * rows * keys, rows * keys),
        name="score",
    )(q, even, odd)


def weigh_kernel(factor, prob_ref, top_ref, lse_ref, *rest):
    others, out_ref = rest[:-1], rest[-1]
    mine = lse_ref[...]
    top = functools.reduce(jnp.maximum, [ref[...] for ref in others], mine)
    total = jnp.exp2(mine - top)
    for ref in others:
        total = total + jnp.exp2(ref[...] - top)
    lse = top + jnp.log2(total)
    c = pl.program_id(0)
    weight = jnp.exp2(top_ref[pl.ds(c, 1), :] - lse) * factor
    high = weight.astype(BF16)
    low = (weight - high.astype(F32)).astype(BF16)
    both = jnp.concatenate([high, low], axis=0)
    got = lax.dot_general(
        both, prob_ref[...], (((1,), (1,)), ((), ())), preferred_element_type=F32
    )
    out_ref[...] = jnp.sum(got, axis=0, keepdims=True)[None]


def weigh(prob, tops, lse, others, factor):
    keys, rows = prob.shape
    chunks = tops.shape[0]
    chunk = keys // chunks
    row = pl.BlockSpec((1, rows), lambda c: (0, 0))
    return pl.pallas_call(
        functools.partial(weigh_kernel, factor),
        grid=(chunks,),
        in_specs=[
            pl.BlockSpec((chunk, rows), lambda c: (c, 0)),
            pl.BlockSpec((chunks, rows), lambda c: (0, 0)),
            row,
            *[row] * len(others),
        ],
        out_specs=pl.BlockSpec((1, 1, chunk), lambda c: (c, 0, 0)),
        out_shape=jax.ShapeDtypeStruct((chunks, 1, chunk), F32),
        compiler_params=params(32),
        cost_estimate=cost(4 * rows * keys, 2 * rows * keys),
        name="weigh",
    )(prob, tops, lse, *others)


def shards(queries, visual_keys, hidden, keep_count, keep_index, norm_gain, kv_weight, kv_bias):
    size = lax.axis_size("seq")
    me = lax.axis_index("seq").astype(jnp.int32).reshape(1)
    own_keys = visual_keys.shape[0]
    tokens = queries.shape[0]

    def swap(x, r):
        return lax.ppermute(x, "seq", [(i, i ^ r) for i in range(size)])

    share = queries.shape[1] // CELL
    by_share = queries.reshape(tokens, CELL, share).transpose(1, 0, 2)
    to_all = jnp.concatenate([by_share] * (size // CELL), axis=0)
    my_q = lax.all_to_all(to_all, "seq", split_axis=0, concat_axis=0, tiled=True)
    my_q = my_q.reshape(size * tokens, share)

    crossed = [keep_count] + [swap(keep_count, CELL * d) for d in range(1, size // CELL)]
    crossed = jnp.concatenate(crossed)
    evens = jnp.stack([crossed] + [swap(crossed, r) for r in range(2, CELL, 2)])
    both = jnp.stack([evens, swap(evens, 1)])
    counts = both.transpose(2, 1, 0).reshape(size)

    blocks = prepare(me, visual_keys)
    even_keys = jnp.concatenate(
        [blocks[0]] + [swap(blocks[r // 2], r) for r in range(2, CELL, 2)], axis=0
    )
    odd_keys = swap(even_keys, 1)

    projected = project(hidden, norm_gain, kv_weight, kv_bias)
    picked = pick(me, counts, keep_index, projected, size)
    cap = own_keys // size
    arrived = lax.all_to_all(
        picked.reshape(size, cap, -1), "seq", split_axis=0, concat_axis=0, tiled=True
    ).reshape(own_keys, -1)
    layer_kv = place(me, counts, arrived, own_keys // 2, size)

    prob, tops, lse = score(my_q, even_keys, odd_keys)
    others = [swap(lse, CELL * d) for d in range(1, size // CELL)]
    total_rows = size * tokens * (queries.shape[1] // HD)
    partial = weigh(prob, tops, lse, others, own_keys * size / total_rows)
    half = CELL // 2
    partial = partial.reshape(2, half, own_keys)
    chip = partial[0] + swap(partial[1], 1)
    importance = chip[0]
    for r in range(1, half):
        importance = importance + swap(chip[r], 2 * r)
    return (importance, layer_kv)


def solution(mesh):
    rows = P(("groups", "seq"), None)
    flat = P(("groups", "seq"))
    return jax.shard_map(
        shards,
        mesh=mesh,
        in_specs=(rows, rows, rows, flat, flat, P(), P(), P()),
        out_specs=(flat, rows),
        check_vma=False,
    )
```

time: 212 us -> 101 us (0.48)
  other arithmetic: 51.9 us -> 2.85 us
  waiting for transfers between devices: 57.2 us -> 14.9 us
  Pallas kernels: 0 us -> 37 us
  matrix products: 31.2 us -> 0 us
  starting transfers between devices: 3.77 us -> 28.7 us
  local copies, waits for them, and re-layouts: 37.7 us -> 15.8 us
  blocking collectives: 13.8 us -> 0 us
  between operations: 14.5 us -> 1.45 us
    all_gather x3 -> x0, waiting for transfers between devices: 45.9 us -> none  [the longest x2 45.9 us: merged(): everything = jax.tree.map(lambda part: lax.all_gather(part, axis), x)]
    pallas_call x0 -> x6, Pallas kernels: none -> 37 us  [the longest x1 14.4 us: project(): pl.pallas_call(project_kernel, grid=(width // depth,), in_specs=[pl.Block...]
    reduce_sum x3 -> x0, other arithmetic: 34.3 us -> none  [the longest x1 14.4 us: shards(): jnp.sum(weights, axis=(0, 1, 2))]
    dot_general x2 -> x0, matrix products: 31.2 us -> none  [the longest x1 15.9 us: shards(): jnp.einsum('tkgd,vkd->kgtv', q_split, k_split, preferred_element_type=jnp...]
    gather x2 -> x0, local copies, waits for them, and re-layouts: 22 us -> none  [the longest x1 20 us: shards(): gathered = jnp.take(hidden, keep_index, axis=0)]
    ppermute x0 -> x14, starting transfers between devices: none -> 18.7 us  [swap(): return lax.ppermute(x, 'seq', [(i, i ^ r) for i in range(size)])]
    ppermute x0 -> x14, waiting for transfers between devices: none -> 14.9 us  [swap(): return lax.ppermute(x, 'seq', [(i, i ^ r) for i in range(size)])]
    unnamed x1 -> x0, blocking collectives: 13.8 us -> none
  transfers between devices with their start and end apart: 4 -> 16, of which waited for: 3 -> 9; matrix products, arithmetic and copies ran while one was open for 33% -> 7% of each run, Pallas kernels for 0% -> 35%
where the time goes in v1:
time: 101 us
  Pallas kernels  37 us (37%)
  starting transfers between devices  28.7 us (28%)
  local copies, waits for them, and re-layouts  15.8 us (16%)
  waiting for transfers between devices  14.9 us (15%)
  other arithmetic  2.85 us (3%)
  between operations  1.45 us (1%)
    ppermute x14, starting transfers between devices, swap(): return lax.ppermute(x, 'seq', [(i, i ^ r) for i in range(size)])  18.7 us
    ppermute x14, waiting for transfers between devices, swap(): return lax.ppermute(x, 'seq', [(i, i ^ r) for i in range(size)])  14.9 us
    pallas_call x1, Pallas kernels, project(): pl.pallas_call(project_kernel, grid=(width // depth,), in_specs=[pl.Block...  14.4 us
    unnamed x16, local copies, waits for them, and re-layouts  13.5 us
    pallas_call x1, Pallas kernels, score(): pl.pallas_call(functools.partial(score_kernel, chunk), grid=(rows // tile...  12.8 us
    all_to_all x1, starting transfers between devices, shards(): lax.all_to_all(to_all, 'seq', split_axis=0, concat_axis=0, tiled=True)  6.33 us
    pallas_call x1, Pallas kernels, weigh(): pl.pallas_call(functools.partial(weigh_kernel, factor), grid=(chunks,), i...  5.4 us
    all_to_all x1, starting transfers between devices, shards(): lax.all_to_all(picked.reshape(size, cap, -1), 'seq', split_axis=0, concat...  3.66 us
  transfers between devices with their start and end apart: 16, of which 9 were waited for; matrix products, arithmetic and copies ran while one was open for 7% of the time, Pallas kernels for 35%

profile of v1, /device:TPU:0, one launch (start us, length us, event | category | flops | bytes accessed | tf_op | source)
XLA Modules:
  0.0 100.7 jit_solution(5905875070794916578)
XLA Ops:
  0.6 0.0 copy-start.1
  0.6 1.0 %copy-done.1 = bf16[512,512]{1,0:T(8,128)(2,1)S(1)} copy-done((bf16[512,512]{1,0:T(8,128)(2,1)S(1)}, bf16[512,512]{1,0:T(8,128)(2,1)}, u32[]{:S(2)}) %copy-start.1) | copy-done | bytes 524312
  1.7 0.1 prepare.1
  1.8 3.0 %collective-permute-start = (bf16[512,128]{1,0:T(8,128)(2,1)S(1)}, bf16[512,128]{1,0:T(8,128)(2,1)}, u32[]{:S(2)}, u32[]{:S(2)}) collective-permute-start(bf16[512,128]{1,0:T(8,128)(2,1)S(1)} %get-tuple-element.10), channel_id=1, source_target_pairs={{0,2},{1,3},{2,0},{3,1},{4,6},{5,7},{6,4},{7,5},{8,10},{9,11},{10,... | collective-permute-start | bytes 393224 | tf_op jit(solution)/shard_map/ppermute | solution.py:276
  4.8 1.6 %collective-permute-start.1 = (bf16[512,128]{1,0:T(8,128)(2,1)S(1)}, bf16[512,128]{1,0:T(8,128)(2,1)}, u32[]{:S(2)}, u32[]{:S(2)}) collective-permute-start(bf16[512,128]{1,0:T(8,128)(2,1)S(1)} %get-tuple-element.11), channel_id=1, source_target_pairs={{0,4},{1,5},{2,6},{3,7},{4,0},{5,1},{6,2},{7,3},{8,12},{9,13},{10,... | collective-permute-start | bytes 393224 | tf_op jit(solution)/shard_map/ppermute | solution.py:276
  6.4 0.0 collective-permute-start.2
  6.4 1.0 copy.28
  7.4 0.0 copy-start.5
  7.4 0.8 pad_maximum_fusion
  8.2 6.3 %all-to-all-start = ((bf16[16,32,512]{2,1,0:T(8,128)(2,1)}), bf16[16,32,512]{2,1,0:T(8,128)(2,1)S(1)}, u32[]{:S(2)}, u32[]{:S(2)}) async-start(bf16[16,32,512]{2,1,0:T(8,128)(2,1)} %pad_maximum_fusion), calls=%async_computation | async-start | bytes 1048576 | tf_op jit(solution)/shard_map/all_to_all | solution.py:281
  14.5 2.8 %collective-permute-start.9 = (s32[1]{0:T(128)}, s32[1]{0:T(128)}, u32[]{:S(2)}, u32[]{:S(2)}) collective-permute-start(s32[1]{0:T(128)} %param.11), channel_id=1, source_target_pairs={{0,8},{1,9},{2,10},{3,11},{4,12},{5,13},{6,14},{7,15},{8,0},{9,1},... | collective-permute-start | bytes 20 | tf_op jit(solution)/shard_map/ppermute | solution.py:276
  17.4 0.0 copy-start.2
  17.4 3.4 %copy-done.2 = bf16[512,8192]{1,0:T(8,128)(2,1)S(1)} copy-done((bf16[512,8192]{1,0:T(8,128)(2,1)S(1)}, bf16[512,8192]{1,0:T(8,128)(2,1)}, u32[]{:S(2)}) %copy-start.2) | copy-done | bytes 8388632
  20.8 0.0 copy-start.3
  20.8 0.8 copy-done.3
  21.5 0.0 copy-start.4
  21.5 0.7 copy-done.4
  22.2 14.4 %project.1.rows_ref = bf16[512,1024]{1,0:T(8,128)(2,1)S(1)} custom-call(bf16[512,8192]{1,0:T(8,128)(2,1)S(1)} %copy-done.2, f32[1,8192]{1,0:T(1,128)S(1)} %bitcast.36, bf16[8192,1024]{1,0:T(8,128)(2,1)} %weight_ref.1, f32[1,1024]{1,0:T(1,128)S(1)} %bitcast.37), custom_call_target="tpu_custom_call" | custom-call | flops 8589934592 | bytes 25165824 | tf_op jit(solution)/shard_map/project/pallas_call | solution.py:59
  37.2 0.0 collective-permute-done.9
  37.2 0.7 pad_add_fusion.1
  38.0 1.5 %collective-permute-start.11 = (s32[2]{0:T(128)S(1)}, s32[2]{0:T(128)S(1)}, u32[]{:S(2)}, u32[]{:S(2)}) collective-permute-start(s32[2]{0:T(128)S(1)} %pad_add_fusion.1), channel_id=1, source_target_pairs={{0,4},{1,5},{2,6},{3,7},{4,0},{5,1},{6,2},{7,3},{8,12},{9,13},{10,... | collective-permute-start | bytes 32 | tf_op jit(solution)/shard_map/ppermute | solution.py:276
  39.4 1.5 %collective-permute-start.12 = (s32[2]{0:T(128)S(1)}, s32[2]{0:T(128)S(1)}, u32[]{:S(2)}, u32[]{:S(2)}) collective-permute-start(s32[2]{0:T(128)S(1)} %pad_add_fusion.1), channel_id=1, source_target_pairs={{0,6},{1,7},{2,4},{3,5},{4,2},{5,3},{6,0},{7,1},{8,14},{9,15},{10,... | collective-permute-start | bytes 32 | tf_op jit(solution)/shard_map/ppermute | solution.py:276
  40.9 0.7 fusion.3
  41.6 0.0 collective-permute-done.11
  41.6 1.4 %collective-permute-start.10 = (s32[2]{0:T(128)S(1)}, s32[2]{0:T(128)S(1)}, u32[]{:S(2)}, u32[]{:S(2)}) collective-permute-start(s32[2]{0:T(128)S(1)} %pad_add_fusion.1), channel_id=1, source_target_pairs={{0,2},{1,3},{2,0},{3,1},{4,6},{5,7},{6,4},{7,5},{8,10},{9,11},{10,... | collective-permute-start | bytes 32 | tf_op jit(solution)/shard_map/ppermute | solution.py:276
  43.0 0.9 collective-permute-done.12
  43.9 1.3 %collective-permute-done.10 = s32[2]{0:T(128)S(1)} collective-permute-done((s32[2]{0:T(128)S(1)}, s32[2]{0:T(128)S(1)}, u32[]{:S(2)}, u32[]{:S(2)}) %collective-permute-start.10) | collective-permute-done | bytes 40 | tf_op jit(solution)/shard_map/ppermute | solution.py:276
  45.2 0.1 collective-permute-start.13
  45.2 0.1 copy.17
  45.3 1.0 %collective-permute-done.13 = s32[4,2]{1,0:T(4,128)S(1)} collective-permute-done((s32[4,2]{1,0:T(4,128)S(1)}, s32[4,2]{1,0:T(4,128)S(1)}, u32[]{:S(2)}, u32[]{:S(2)}) %collective-permute-start.13) | collective-permute-done | bytes 64 | tf_op jit(solution)/shard_map/ppermute | solution.py:276
  46.4 0.1 copy.18
  46.5 0.1 copy.19
  46.6 0.1 reshape.39.counts_ref
  46.7 0.0 copy-done.5
  46.7 2.6 %pick.1 = bf16[512,1024]{1,0:T(8,128)(2,1)} custom-call(s32[1]{0:T(128)} %bitcast.2.me_ref, s32[16]{0:T(128)S(1)} %reshape.39.counts_ref, s32[1,512]{1,0:T(1,128)S(1)} %bitcast.38, bf16[512,1024]{1,0:T(8,128)(2,1)S(1)} %project.1.rows_ref), custom_call_target="tpu_custom_call" | custom-call | flops 805306368 | bytes 2097152 | tf_op jit(solution)/shard_map/pick/pallas_call | solution.py:106
  49.3 0.0 all-to-all-done
  49.3 3.7 %all-to-all-start.1 = ((bf16[16,32,1024]{2,1,0:T(8,128)(2,1)}), bf16[16,32,1024]{2,1,0:T(8,128)(2,1)S(1)}, u32[]{:S(2)}, u32[]{:S(2)}) async-start(bf16[16,32,1024]{2,1,0:T(8,128)(2,1)} %bitcast.18), calls=%async_computation.1 | async-start | bytes 2097152 | tf_op jit(solution)/shard_map/all_to_all | solution.py:299
  52.9 0.0 collective-permute-done
  52.9 0.9 constant_dynamic-update-slice_fusion.2
  53.9 0.0 collective-permute-done.1
  53.9 0.9 constant_dynamic-update-slice_fusion.1
  54.8 0.0 collective-permute-done.2
  54.8 0.9 constant_dynamic-update-slice_fusion.even_ref
  55.7 0.5 collective-permute-start.3
  56.2 1.5 %collective-permute-done.3.odd_ref = bf16[2048,128]{1,0:T(8,128)(2,1)S(1)} collective-permute-done((bf16[2048,128]{1,0:T(8,128)(2,1)S(1)}, bf16[2048,128]{1,0:T(8,128)(2,1)S(1)}, u32[]{:S(2)}, u32[]{:S(2)}) %collective-permute-start.3) | collective-permute-done | bytes 524320 | tf_op jit(solution)/shard_map/ppermute | solution.py:276
  57.7 12.8 %score.1 = (bf16[4096,2048]{1,0:T(8,128)(2,1)}, f32[8,2048]{1,0:T(8,128)S(1)}, f32[1,2048]{1,0:T(1,128)S(1)}) custom-call(bf16[512,512]{1,0:T(8,128)(2,1)S(1)} %bitcast.35, bf16[2048,128]{1,0:T(8,128)(2,1)S(1)} %constant_dynamic-update-slice_fusion.even_ref, bf16[2048,128]{1,0:T(8,128)(2,1)S(1)} %collective-permute-done.3.odd_ref), custom_call_target="tpu_custom_call" | custom-call | flops 2147483648 | bytes 16777216 | tf_op jit(solution)/shard_map/score/pallas_call | solution.py:204
  70.5 2.8 %collective-permute-start.4 = (f32[1,2048]{1,0:T(1,128)S(1)}, f32[1,2048]{1,0:T(1,128)S(1)}, u32[]{:S(2)}, u32[]{:S(2)}) collective-permute-start(f32[1,2048]{1,0:T(1,128)S(1)} %get-tuple-element.15.lse_ref), channel_id=1, source_target_pairs={{0,8},{1,9},{2,10},{3,11},{4,12},{5,13},{6,14},{7,15},{8,0},{9,1},... | collective-permute-start | bytes 24584 | tf_op jit(solution)/shard_map/ppermute | solution.py:276
  73.3 6.5 %collective-permute-done.4.rest_0_ = f32[1,2048]{1,0:T(1,128)S(1)} collective-permute-done((f32[1,2048]{1,0:T(1,128)S(1)}, f32[1,2048]{1,0:T(1,128)S(1)}, u32[]{:S(2)}, u32[]{:S(2)}) %collective-permute-start.4) | collective-permute-done | bytes 8224 | tf_op jit(solution)/shard_map/ppermute | solution.py:276
  79.8 0.0 copy-start
  79.8 5.8 %copy-done = bf16[4096,2048]{1,0:T(8,128)(2,1)S(1)} copy-done((bf16[4096,2048]{1,0:T(8,128)(2,1)S(1)}, bf16[4096,2048]{1,0:T(8,128)(2,1)}, u32[]{:S(2)}) %copy-start) | copy-done | bytes 16777240
  85.6 5.4 %weigh.1 = f32[8,1,512]{2,1,0:T(1,128)S(1)} custom-call(bf16[4096,2048]{1,0:T(8,128)(2,1)S(1)} %copy-done, f32[8,2048]{1,0:T(8,128)S(1)} %get-tuple-element.14.top_ref, f32[1,2048]{1,0:T(1,128)S(1)} %get-tuple-element.15.lse_ref, f32[1,2048]{1,0:T(1,128)S(1)} %collective-permute-done.4.rest_0_), custom_call_target="tpu_custom_call" | custom-call | flops 33554432 | bytes 16777216 | tf_op jit(solution)/shard_map/weigh/pallas_call | solution.py:252
  91.0 0.1 collective-permute-start.5
  91.1 1.2 %collective-permute-done.5 = f32[4,512]{1,0:T(4,128)S(1)} collective-permute-done((f32[4,512]{1,0:T(4,128)S(1)}, f32[4,512]{1,0:T(4,128)S(1)}, u32[]{:S(2)}, u32[]{:S(2)}) %collective-permute-start.5) | collective-permute-done | bytes 8224 | tf_op jit(solution)/shard_map/ppermute | solution.py:276
  92.3 1.5 %collective-permute-start.6 = (f32[512]{0:T(512)S(1)}, f32[512]{0:T(512)S(1)}, u32[]{:S(2)}, u32[]{:S(2)}) collective-permute-start(f32[512]{0:T(512)S(1)} %bitcast.47), channel_id=1, source_target_pairs={{0,2},{1,3},{2,0},{3,1},{4,6},{5,7},{6,4},{7,5},{8,10},{9,11},{10,... | collective-permute-start | bytes 6152 | tf_op jit(solution)/shard_map/ppermute | solution.py:276
  93.8 0.0 collective-permute-start.7
  93.8 2.0 %collective-permute-start.8 = (f32[512]{0:T(512)S(1)}, f32[512]{0:T(512)S(1)}, u32[]{:S(2)}, u32[]{:S(2)}) collective-permute-start(f32[512]{0:T(512)S(1)} %bitcast.45), channel_id=1, source_target_pairs={{0,6},{1,7},{2,4},{3,5},{4,2},{5,3},{6,0},{7,1},{8,14},{9,15},{10,... | collective-permute-start | bytes 6152 | tf_op jit(solution)/shard_map/ppermute | solution.py:276
  95.8 0.1 collective-permute-done.6
  95.9 1.5 %collective-permute-done.7 = f32[512]{0:T(512)S(1)} collective-permute-done((f32[512]{0:T(512)S(1)}, f32[512]{0:T(512)S(1)}, u32[]{:S(2)}, u32[]{:S(2)}) %collective-permute-start.7) | collective-permute-done | bytes 2080 | tf_op jit(solution)/shard_map/ppermute | solution.py:276
  97.4 0.9 collective-permute-done.8
  98.3 0.6 add_add_fusion
  98.9 0.0 all-to-all-done.1
  98.9 1.8 %place.1 = bf16[256,1024]{1,0:T(8,128)(2,1)} custom-call(s32[1]{0:T(128)} %bitcast.2.me_ref, s32[16]{0:T(128)S(1)} %reshape.39.counts_ref, bf16[512,1024]{1,0:T(8,128)(2,1)S(1)} %bitcast.34), custom_call_target="tpu_custom_call" | custom-call | flops 268435456 | bytes 1572864 | tf_op jit(solution)/shard_map/place/pallas_call | solution.py:141
  (7 shorter events, 0.0 us)
Async XLA Ops:
  0.6 1.0 %copy-start.1 = (bf16[512,512]{1,0:T(8,128)(2,1)S(1)}, bf16[512,512]{1,0:T(8,128)(2,1)}, u32[]{:S(2)}) copy-start(bf16[512,512]{1,0:T(8,128)(2,1)} %keys_ref.1) | copy-start | bytes 1572868
  1.8 51.2 %collective-permute-start = (bf16[512,128]{1,0:T(8,128)(2,1)S(1)}, bf16[512,128]{1,0:T(8,128)(2,1)}, u32[]{:S(2)}, u32[]{:S(2)}) collective-permute-start(bf16[512,128]{1,0:T(8,128)(2,1)S(1)} %get-tuple-element.10), channel_id=1, source_target_pairs={{0,2},{1,3},{2,0},{3,1},{4,6},{5,7},{6,4},{7,5},{8,10},{9,11},{10,... | collective-permute-start | bytes 393224 | tf_op jit(solution)/shard_map/ppermute | solution.py:276
  4.8 49.1 %collective-permute-start.1 = (bf16[512,128]{1,0:T(8,128)(2,1)S(1)}, bf16[512,128]{1,0:T(8,128)(2,1)}, u32[]{:S(2)}, u32[]{:S(2)}) collective-permute-start(bf16[512,128]{1,0:T(8,128)(2,1)S(1)} %get-tuple-element.11), channel_id=1, source_target_pairs={{0,4},{1,5},{2,6},{3,7},{4,0},{5,1},{6,2},{7,3},{8,12},{9,13},{10,... | collective-permute-start | bytes 393224 | tf_op jit(solution)/shard_map/ppermute | solution.py:276
  6.4 48.4 %collective-permute-start.2 = (bf16[512,128]{1,0:T(8,128)(2,1)S(1)}, bf16[512,128]{1,0:T(8,128)(2,1)}, u32[]{:S(2)}, u32[]{:S(2)}) collective-permute-start(bf16[512,128]{1,0:T(8,128)(2,1)S(1)} %get-tuple-element.12), channel_id=1, source_target_pairs={{0,6},{1,7},{2,4},{3,5},{4,2},{5,3},{6,0},{7,1},{8,14},{9,15},{10,... | collective-permute-start | bytes 393224 | tf_op jit(solution)/shard_map/ppermute | solution.py:276
  7.4 39.3 %copy-start.5 = (s32[512]{0:T(512)S(1)}, s32[512]{0:T(512)}, u32[]{:S(2)}) copy-start(s32[512]{0:T(512)} %param.12) | copy-start | bytes 6148
  8.2 41.1 %all-to-all-start = ((bf16[16,32,512]{2,1,0:T(8,128)(2,1)}), bf16[16,32,512]{2,1,0:T(8,128)(2,1)S(1)}, u32[]{:S(2)}, u32[]{:S(2)}) async-start(bf16[16,32,512]{2,1,0:T(8,128)(2,1)} %pad_maximum_fusion), calls=%async_computation | async-start | bytes 1048576 | tf_op jit(solution)/shard_map/all_to_all | solution.py:281
  14.5 22.7 %collective-permute-start.9 = (s32[1]{0:T(128)}, s32[1]{0:T(128)}, u32[]{:S(2)}, u32[]{:S(2)}) collective-permute-start(s32[1]{0:T(128)} %param.11), channel_id=1, source_target_pairs={{0,8},{1,9},{2,10},{3,11},{4,12},{5,13},{6,14},{7,15},{8,0},{9,1},... | collective-permute-start | bytes 20 | tf_op jit(solution)/shard_map/ppermute | solution.py:276
  17.4 3.4 %copy-start.2 = (bf16[512,8192]{1,0:T(8,128)(2,1)S(1)}, bf16[512,8192]{1,0:T(8,128)(2,1)}, u32[]{:S(2)}) copy-start(bf16[512,8192]{1,0:T(8,128)(2,1)} %x_ref.1) | copy-start | bytes 25165828
  20.8 0.8 copy-start.3
  21.5 0.7 copy-start.4
  38.0 3.6 %collective-permute-start.11 = (s32[2]{0:T(128)S(1)}, s32[2]{0:T(128)S(1)}, u32[]{:S(2)}, u32[]{:S(2)}) collective-permute-start(s32[2]{0:T(128)S(1)} %pad_add_fusion.1), channel_id=1, source_target_pairs={{0,4},{1,5},{2,6},{3,7},{4,0},{5,1},{6,2},{7,3},{8,12},{9,13},{10,... | collective-permute-start | bytes 32 | tf_op jit(solution)/shard_map/ppermute | solution.py:276
  39.4 4.4 %collective-permute-start.12 = (s32[2]{0:T(128)S(1)}, s32[2]{0:T(128)S(1)}, u32[]{:S(2)}, u32[]{:S(2)}) collective-permute-start(s32[2]{0:T(128)S(1)} %pad_add_fusion.1), channel_id=1, source_target_pairs={{0,6},{1,7},{2,4},{3,5},{4,2},{5,3},{6,0},{7,1},{8,14},{9,15},{10,... | collective-permute-start | bytes 32 | tf_op jit(solution)/shard_map/ppermute | solution.py:276
  41.6 3.6 %collective-permute-start.10 = (s32[2]{0:T(128)S(1)}, s32[2]{0:T(128)S(1)}, u32[]{:S(2)}, u32[]{:S(2)}) collective-permute-start(s32[2]{0:T(128)S(1)} %pad_add_fusion.1), channel_id=1, source_target_pairs={{0,2},{1,3},{2,0},{3,1},{4,6},{5,7},{6,4},{7,5},{8,10},{9,11},{10,... | collective-permute-start | bytes 32 | tf_op jit(solution)/shard_map/ppermute | solution.py:276
  45.2 1.2 %collective-permute-start.13 = (s32[4,2]{1,0:T(4,128)S(1)}, s32[4,2]{1,0:T(4,128)S(1)}, u32[]{:S(2)}, u32[]{:S(2)}) collective-permute-start(s32[4,2]{1,0:T(4,128)S(1)} %pad_add_fusion), channel_id=1, source_target_pairs={{0,1},{1,0},{2,3},{3,2},{4,5},{5,4},{6,7},{7,6},{8,9},{9,8},{10,11... | collective-permute-start | bytes 104 | tf_op jit(solution)/shard_map/ppermute | solution.py:276
  49.3 49.6 %all-to-all-start.1 = ((bf16[16,32,1024]{2,1,0:T(8,128)(2,1)}), bf16[16,32,1024]{2,1,0:T(8,128)(2,1)S(1)}, u32[]{:S(2)}, u32[]{:S(2)}) async-start(bf16[16,32,1024]{2,1,0:T(8,128)(2,1)} %bitcast.18), calls=%async_computation.1 | async-start | bytes 2097152 | tf_op jit(solution)/shard_map/all_to_all | solution.py:299
  55.7 2.0 %collective-permute-start.3 = (bf16[2048,128]{1,0:T(8,128)(2,1)S(1)}, bf16[2048,128]{1,0:T(8,128)(2,1)S(1)}, u32[]{:S(2)}, u32[]{:S(2)}) collective-permute-start(bf16[2048,128]{1,0:T(8,128)(2,1)S(1)} %constant_dynamic-update-slice_fusion.even_ref), channel_id=1, source_target_pairs={{0,1},{1,0},{2,3},{3,2},{4,5},{5,4},{6,7},{7,6},{8,9},{9,8},{10,11... | collective-permute-start | bytes 1572872 | tf_op jit(solution)/shard_map/ppermute | solution.py:276
  70.5 9.3 %collective-permute-start.4 = (f32[1,2048]{1,0:T(1,128)S(1)}, f32[1,2048]{1,0:T(1,128)S(1)}, u32[]{:S(2)}, u32[]{:S(2)}) collective-permute-start(f32[1,2048]{1,0:T(1,128)S(1)} %get-tuple-element.15.lse_ref), channel_id=1, source_target_pairs={{0,8},{1,9},{2,10},{3,11},{4,12},{5,13},{6,14},{7,15},{8,0},{9,1},... | collective-permute-start | bytes 24584 | tf_op jit(solution)/shard_map/ppermute | solution.py:276
  79.8 5.8 %copy-start = (bf16[4096,2048]{1,0:T(8,128)(2,1)S(1)}, bf16[4096,2048]{1,0:T(8,128)(2,1)}, u32[]{:S(2)}) copy-start(bf16[4096,2048]{1,0:T(8,128)(2,1)} %get-tuple-element.13.prob_ref) | copy-start | bytes 50331652
  91.0 1.2 %collective-permute-start.5 = (f32[4,512]{1,0:T(4,128)S(1)}, f32[4,512]{1,0:T(4,128)S(1)}, u32[]{:S(2)}, u32[]{:S(2)}) collective-permute-start(f32[4,512]{1,0:T(4,128)S(1)} %bitcast.41), channel_id=1, source_target_pairs={{0,1},{1,0},{2,3},{3,2},{4,5},{5,4},{6,7},{7,6},{8,9},{9,8},{10,11... | collective-permute-start | bytes 24584 | tf_op jit(solution)/shard_map/ppermute | solution.py:276
  92.3 3.7 %collective-permute-start.6 = (f32[512]{0:T(512)S(1)}, f32[512]{0:T(512)S(1)}, u32[]{:S(2)}, u32[]{:S(2)}) collective-permute-start(f32[512]{0:T(512)S(1)} %bitcast.47), channel_id=1, source_target_pairs={{0,2},{1,3},{2,0},{3,1},{4,6},{5,7},{6,4},{7,5},{8,10},{9,11},{10,... | collective-permute-start | bytes 6152 | tf_op jit(solution)/shard_map/ppermute | solution.py:276
  93.8 3.6 %collective-permute-start.7 = (f32[512]{0:T(512)S(1)}, f32[512]{0:T(512)S(1)}, u32[]{:S(2)}, u32[]{:S(2)}) collective-permute-start(f32[512]{0:T(512)S(1)} %bitcast.46), channel_id=1, source_target_pairs={{0,4},{1,5},{2,6},{3,7},{4,0},{5,1},{6,2},{7,3},{8,12},{9,13},{10,... | collective-permute-start | bytes 6152 | tf_op jit(solution)/shard_map/ppermute | solution.py:276
  93.8 4.5 %collective-permute-start.8 = (f32[512]{0:T(512)S(1)}, f32[512]{0:T(512)S(1)}, u32[]{:S(2)}, u32[]{:S(2)}) collective-permute-start(f32[512]{0:T(512)S(1)} %bitcast.45), channel_id=1, source_target_pairs={{0,6},{1,7},{2,4},{3,5},{4,2},{5,3},{6,0},{7,1},{8,14},{9,15},{10,... | collective-permute-start | bytes 6152 | tf_op jit(solution)/shard_map/ppermute | solution.py:276

commit v2 on v1

v2 whole, which is shorter than its diff:
```python
import functools

import jax
import jax.numpy as jnp
from jax import lax
from jax.experimental import pallas as pl
from jax.experimental.pallas import tpu as pltpu
from jax.sharding import PartitionSpec as P

HD = 128
CELL = 8
EPS = 1e-06
F32 = jnp.float32
BF16 = jnp.bfloat16
LOG2E = 1.4426950408889634
MIB = 1024 * 1024


def params(mib):
    return pltpu.CompilerParams(vmem_limit_bytes=mib * MIB)


def cost(flops, bytes_accessed, transcendentals=0):
    return pl.CostEstimate(
        flops=int(flops), bytes_accessed=int(bytes_accessed), transcendentals=int(transcendentals)
    )


def in_hbm(x):
    return pltpu.with_memory_space_constraint(x, pltpu.HBM)


SMEM = pl.BlockSpec(memory_space=pltpu.SMEM)
VMEM = pl.BlockSpec(memory_space=pltpu.VMEM)
EXTRA = 16


def project_kernel(x_ref, gain_ref, weight_ref, bias_ref, out_ref, total, squares):
    step = pl.program_id(0)
    values = x_ref[...].astype(F32)
    scaled = (values * gain_ref[...]).astype(BF16)
    part = jnp.dot(scaled, weight_ref[...], preferred_element_type=F32)
    square = values * values
    lanes = square[:, :128]
    for col in range(128, square.shape[1], 128):
        lanes = lanes + square[:, col : col + 128]

    @pl.when(step == 0)
    def _():
        total[...] = part
        squares[...] = lanes

    @pl.when(step > 0)
    def _():
        total[...] += part
        squares[...] += lanes

    @pl.when(step == pl.num_programs(0) - 1)
    def _():
        width = x_ref.shape[1] * pl.num_programs(0)
        mean_sq = jnp.sum(squares[...], axis=1, keepdims=True) * (1.0 / width)
        out_ref[...] = (total[...] * lax.rsqrt(mean_sq + EPS) + bias_ref[...]).astype(BF16)


def project(hidden, gain, weight, bias, depth=2048):
    rows, width = hidden.shape
    cols = weight.shape[1]
    return pl.pallas_call(
        project_kernel,
        grid=(width // depth,),
        in_specs=[
            pl.BlockSpec((rows, depth), lambda k: (0, k)),
            pl.BlockSpec((1, depth), lambda k: (0, k)),
            pl.BlockSpec((depth, cols), lambda k: (k, 0)),
            pl.BlockSpec((1, cols), lambda k: (0, 0)),
        ],
        out_specs=pl.BlockSpec((rows, cols), lambda k: (0, 0)),
        out_shape=jax.ShapeDtypeStruct((rows, cols), BF16),
        scratch_shapes=[pltpu.VMEM((rows, cols), F32), pltpu.VMEM((rows, 128), F32)],
        compiler_params=params(32),
        cost_estimate=cost(2 * rows * width * cols, 2 * width * (rows + cols)),
        name="project",
    )(*map(in_hbm, (hidden, gain.reshape(1, -1), weight, bias.reshape(1, -1))))


def spread_kernel(q_ref, out_ref):
    share = out_ref.shape[2]
    for i in range(out_ref.shape[0]):
        at = (i % CELL) * share
        out_ref[i] = q_ref[:, at : at + share]


def spread(queries, size):
    tokens, width = queries.shape
    return pl.pallas_call(
        spread_kernel,
        in_specs=[VMEM],
        out_specs=VMEM,
        out_shape=jax.ShapeDtypeStruct((size, tokens, width // CELL), BF16),
        compiler_params=params(16),
        cost_estimate=cost(0, 6 * queries.size),
        name="spread",
    )(queries)


def prepare_kernel(cells, me_ref, *refs):
    count_refs, keys_ref, out_refs = refs[:cells], refs[cells], refs[cells + 1 :]
    me = me_ref[0] & (CELL - 1)
    rows = keys_ref.shape[0]
    lane = lax.broadcasted_iota(jnp.int32, (EXTRA, 128), 1)
    high = lax.broadcasted_iota(jnp.int32, (EXTRA, 128), 0) < EXTRA // 2
    extra = jnp.zeros((EXTRA, 128), jnp.int32)
    for c in range(cells):
        count = count_refs[c][0]
        extra = jnp.where(lane == c, jnp.where(high, count // 8, count % 8), extra)
    extra = extra.astype(F32).astype(BF16)
    for i, out_ref in enumerate(out_refs):
        head = (me ^ (2 * i)) // 2
        out_ref[:rows, :] = keys_ref[:, pl.ds(pl.multiple_of(head * HD, HD), HD)]
        out_ref[rows:, :] = extra


def prepare(me, counts, keys):
    n = CELL // 2
    block = jax.ShapeDtypeStruct((keys.shape[0] + EXTRA, HD), BF16)
    return pl.pallas_call(
        functools.partial(prepare_kernel, len(counts)),
        in_specs=[SMEM] * (1 + len(counts)) + [VMEM],
        out_specs=[VMEM] * n,
        out_shape=[block] * n,
        compiler_params=params(16),
        cost_estimate=cost(0, 4 * keys.size),
        name="prepare",
    )(me, *counts, keys)


def counts_of(me, refs, cells):
    pairs = []
    for r, ref in enumerate(refs):
        extra = ref[...].astype(F32)
        count = (extra[:1] * 8.0 + extra[EXTRA // 2 : EXTRA // 2 + 1]).astype(jnp.int32)
        for c in range(cells):
            pairs.append((me ^ (r + CELL * c), count[:, c : c + 1]))
    return pairs


def pick_kernel(size, me_ref, *refs):
    count_refs, (keep_ref, rows_ref, out_ref) = refs[:CELL], refs[CELL:]
    me = me_ref[0]
    start = jnp.zeros((1, 1), jnp.int32)
    for device, count in counts_of(me, count_refs, size // CELL):
        start += jnp.where(device < me, count, 0)
    n = rows_ref.shape[0]
    cap = n // size
    slot = lax.broadcasted_iota(jnp.int32, (n, n), 0)
    entry = lax.broadcasted_iota(jnp.int32, (n, n), 1)
    wanted = ((slot // cap - start) & (size - 1)) + (slot & (cap - 1)) * size
    chooses = (wanted == entry).astype(F32).astype(BF16)
    listed = (keep_ref[...] == slot).astype(F32).astype(BF16)
    select = lax.dot_general(
        chooses, listed, (((1,), (1,)), ((), ())), preferred_element_type=F32
    ).astype(BF16)
    out_ref[...] = jnp.dot(select, rows_ref[...], preferred_element_type=F32).astype(BF16)


def extra_spec(block):
    at = block.shape[0] // EXTRA - 1
    return pl.BlockSpec((EXTRA, HD), lambda i: (at, 0))


def pick(me, blocks, keep_index, rows, size):
    n = rows.shape[0]
    return pl.pallas_call(
        functools.partial(pick_kernel, size),
        grid=(1,),
        in_specs=[SMEM, *map(extra_spec, blocks), VMEM, VMEM],
        out_specs=VMEM,
        out_shape=jax.ShapeDtypeStruct(rows.shape, BF16),
        compiler_params=params(32),
        cost_estimate=cost(2 * n * n * (n + rows.shape[1]), 4 * rows.size),
        name="pick",
    )(me, *blocks, keep_index.reshape(1, -1), rows)


def place_kernel(size, me_ref, *refs):
    count_refs, (rows_ref, out_ref) = refs[:CELL], refs[CELL:]
    me = me_ref[0]
    keep, n = out_ref.shape[0], rows_ref.shape[0]
    cap = n // size
    slot = lax.broadcasted_iota(jnp.int32, (1, n), 1)
    source = slot // cap
    starts = jnp.zeros((1, n), jnp.int32)
    counts = jnp.zeros((1, n), jnp.int32)
    for device, count in counts_of(me, count_refs, size // CELL):
        starts += jnp.where(source > device, count, 0)
        counts = jnp.where(source == device, count, counts)
    pos = ((me - starts) & (size - 1)) + (slot & (cap - 1)) * size
    target = jnp.where(pos < counts, (starts + pos) // size, keep)
    row = lax.broadcasted_iota(jnp.int32, (keep, n), 0)
    select = (row == target).astype(F32).astype(BF16)
    out_ref[...] = jnp.dot(select, rows_ref[...], preferred_element_type=F32).astype(BF16)


def place(me, blocks, rows, keep, size):
    return pl.pallas_call(
        functools.partial(place_kernel, size),
        grid=(1,),
        in_specs=[SMEM, *map(extra_spec, blocks), VMEM],
        out_specs=VMEM,
        out_shape=jax.ShapeDtypeStruct((keep, rows.shape[1]), BF16),
        compiler_params=params(32),
        cost_estimate=cost(2 * keep * rows.size, 3 * rows.size),
        name="place",
    )(me, *blocks, rows)


def score_kernel(first, chunk, tile, q_ref, *refs):
    key_refs, (prob_ref, top_ref, lse_ref) = refs[:CELL], refs[CELL:]
    scale = HD**-0.5 * LOG2E
    per = q_ref.shape[0] // tile
    keys = key_refs[0].shape[0] - EXTRA

    def step(i, _):
        rows = pl.ds(pl.multiple_of((i % per) * tile, tile), tile)
        head = pl.ds(pl.multiple_of((first + i // per) * HD, HD), HD)
        cols = pl.ds(pl.multiple_of(i * tile, tile), tile)
        query = q_ref[rows, head]
        tops, sums = [], []
        for c in range(CELL * keys // chunk):
            block, at = divmod(c * chunk, keys)
            s = lax.dot_general(
                key_refs[block][at : at + chunk, :],
                query,
                (((1,), (1,)), ((), ())),
                preferred_element_type=F32,
            )
            top = jnp.max(s, axis=0, keepdims=True)
            p = jnp.exp2((s - top) * scale)
            sums.append(jnp.sum(p, axis=0, keepdims=True))
            tops.append(top * scale)
            prob_ref[c * chunk : (c + 1) * chunk, cols] = p.astype(BF16)
        top_all = functools.reduce(jnp.maximum, tops)
        total = sum(part * jnp.exp2(top - top_all) for part, top in zip(sums, tops))
        for c, top in enumerate(tops):
            top_ref[c : c + 1, cols] = top
        lse_ref[:, cols] = top_all + jnp.log2(total)
        return 0

    lax.fori_loop(0, prob_ref.shape[1] // tile, step, 0)


def score(q, blocks, first, heads, chunk=256, tile=512):
    keys = CELL * (blocks[0].shape[0] - EXTRA)
    rows = q.shape[0] * heads
    tile = min(tile, q.shape[0])
    return pl.pallas_call(
        functools.partial(score_kernel, first, chunk, tile),
        in_specs=[VMEM] * (1 + CELL),
        out_specs=[VMEM] * 3,
        out_shape=[
            pltpu.VMEM((keys, rows), BF16),
            pltpu.VMEM((keys // chunk, rows), F32),
            pltpu.VMEM((1, rows), F32),
        ],
        compiler_params=params(16),
        cost_estimate=cost(2 * rows * keys * HD, 2 * rows * keys, rows * keys),
        name="score",
    )(q, *blocks)


def weigh_kernel(factor, prob_ref, top_ref, lse_ref, *rest):
    others, out_ref = rest[:-1], rest[-1]
    mine = lse_ref[...]
    top = functools.reduce(jnp.maximum, [ref[...] for ref in others], mine)
    total = jnp.exp2(mine - top)
    for ref in others:
        total = total + jnp.exp2(ref[...] - top)
    lse = top + jnp.log2(total)
    weight = jnp.exp2(top_ref[...] - lse) * factor
    high = weight.astype(BF16).astype(F32)
    low = weight - high
    chunk = out_ref.shape[1]
    for c in range(out_ref.shape[0]):
        both = jnp.concatenate([high[c : c + 1], low[c : c + 1]], axis=0).astype(BF16)
        got = lax.dot_general(
            both,
            prob_ref[c * chunk : (c + 1) * chunk, :],
            (((1,), (1,)), ((), ())),
            preferred_element_type=F32,
        )
        out_ref[c : c + 1, :] = jnp.sum(got, axis=0, keepdims=True)


def weigh(prob, tops, lse, others, factor):
    keys, rows = prob.shape
    chunks = tops.shape[0]
    return pl.pallas_call(
        functools.partial(weigh_kernel, factor),
        in_specs=[VMEM] * (3 + len(others)),
        out_specs=VMEM,
        out_shape=jax.ShapeDtypeStruct((chunks, keys // chunks), F32),
        compiler_params=params(16),
        cost_estimate=cost(4 * rows * keys, 2 * rows * keys),
        name="weigh",
    )(prob, tops, lse, *others)


def shards(queries, visual_keys, hidden, keep_count, keep_index, norm_gain, kv_weight, kv_bias):
    size = lax.axis_size("seq")
    me = lax.axis_index("seq").astype(jnp.int32).reshape(1)
    own_keys = visual_keys.shape[0]
    tokens = queries.shape[0]

    def swap(x, r):
        return lax.ppermute(x, "seq", [(i, i ^ r) for i in range(size)])

    counts = [keep_count] + [swap(keep_count, CELL * d) for d in range(1, size // CELL)]

    my_q = lax.all_to_all(spread(queries, size), "seq", split_axis=0, concat_axis=0, tiled=True)
    my_q = my_q.reshape(size * tokens, -1)

    evens = prepare(me, counts, visual_keys)
    evens = [evens[0]] + [swap(evens[i], 2 * i) for i in range(1, CELL // 2)]
    odds = [swap(block, 1) for block in evens]
    blocks = [block for pair in zip(evens, odds) for block in pair]

    projected = project(hidden, norm_gain, kv_weight, kv_bias)
    picked = pick(me, blocks, keep_index, projected, size)
    arrived = lax.all_to_all(
        picked.reshape(size, own_keys // size, -1), "seq", split_axis=0, concat_axis=0, tiled=True
    ).reshape(own_keys, -1)
    layer_kv = place(me, blocks, arrived, own_keys // 2, size)

    heads = queries.shape[1] // HD // CELL
    parts = [score(my_q, blocks, at, heads // 2) for at in (0, heads // 2)]
    total_rows = size * tokens * (queries.shape[1] // HD)
    factor = own_keys * size / total_rows
    partial = 0.0
    for prob, tops, lse in parts:
        others = [swap(lse, CELL * d) for d in range(1, size // CELL)]
        partial = partial + weigh(prob, tops, lse, others, factor)
    partial = partial.reshape(CELL // 2, 2, own_keys)
    chip = partial[:, 0] + swap(partial[:, 1], 1)
    importance = chip[0]
    for i in range(1, CELL // 2):
        importance = importance + swap(chip[i], 2 * i)
    return (importance, layer_kv)


def solution(mesh):
    rows = P(("groups", "seq"), None)
    flat = P(("groups", "seq"))
    return jax.shard_map(
        shards,
        mesh=mesh,
        in_specs=(rows, rows, rows, flat, flat, P(), P(), P()),
        out_specs=(flat, rows),
        check_vma=False,
    )
```

time: 101 us -> 83.9 us (0.83)
  local copies, waits for them, and re-layouts: 15.8 us -> 2.04 us
  Pallas kernels: 37 us -> 34 us
  waiting for transfers between devices: 14.9 us -> 17.8 us
  other arithmetic: 2.85 us -> 0.59 us
  starting transfers between devices: 28.7 us -> 27.6 us
    unnamed x16 -> x7, local copies, waits for them, and re-layouts: 13.5 us -> 2 us
    ppermute x14, starting transfers between devices: 18.7 us -> 15.4 us  [swap(): return lax.ppermute(x, 'seq', [(i, i ^ r) for i in range(size)])]
    ppermute x14, waiting for transfers between devices: 14.9 us -> 17.8 us  [swap(): return lax.ppermute(x, 'seq', [(i, i ^ r) for i in range(size)])]
    pallas_call x5 -> x8, Pallas kernels: 22.6 us -> 20.4 us  [the longest x2 10.6 us: score(): pl.pallas_call(functools.partial(score_kernel, first, chunk, tile), in_sp...]
    all_to_all x2, starting transfers between devices: 9.98 us -> 12.2 us  [the longest x1 6.27 us: shards(): lax.all_to_all(spread(queries, size), 'seq', split_axis=0, concat_axis=0,...]
    concatenate x2 -> x0, other arithmetic: 1.54 us -> none  [the longest x1 0.83 us: shards(): to_all = jnp.concatenate([by_share] * (size // CELL), axis=0)]
    reshape x2 -> x1, local copies, waits for them, and re-layouts: 1.05 us -> 0.01 us  [shards(): partial = partial.reshape(CELL // 2, 2, own_keys)]
  transfers between devices with their start and end apart: 16 -> 16, of which waited for: 9 -> 6; matrix products, arithmetic and copies ran while one was open for 7% -> 1% of each run, Pallas kernels for 35% -> 38%
where the time goes in v2:
time: 83.9 us; the launch traced here: 83.5 us
  Pallas kernels  34 us (41%)
  starting transfers between devices  27.6 us (33%)
  waiting for transfers between devices  17.8 us (21%)
  local copies, waits for them, and re-layouts  2.04 us (2%)
  between operations  1.48 us (2%)
    ppermute x14, waiting for transfers between devices, swap(): return lax.ppermute(x, 'seq', [(i, i ^ r) for i in range(size)])  17.8 us
    ppermute x14, starting transfers between devices, swap(): return lax.ppermute(x, 'seq', [(i, i ^ r) for i in range(size)])  15.4 us
    pallas_call x1, Pallas kernels, project(): pl.pallas_call(project_kernel, grid=(width // depth,), in_specs=[pl.Block...  13.6 us
    pallas_call x2, Pallas kernels, score(): pl.pallas_call(functools.partial(score_kernel, first, chunk, tile), in_sp...  10.6 us
    all_to_all x1, starting transfers between devices, shards(): lax.all_to_all(spread(queries, size), 'seq', split_axis=0, concat_axis=0,...  6.27 us
    all_to_all x1, starting transfers between devices, shards(): lax.all_to_all(picked.reshape(size, own_keys // size, -1), 'seq', split_a...  5.96 us
    pallas_call x2, Pallas kernels, weigh(): pl.pallas_call(functools.partial(weigh_kernel, factor), in_specs=[VMEM] *...  4.58 us
    pallas_call x1, Pallas kernels, pick(): pl.pallas_call(functools.partial(pick_kernel, size), grid=(1,), in_specs=...  2.2 us
  transfers between devices with their start and end apart: 16, of which 6 were waited for; matrix products, arithmetic and copies ran while one was open for 1% of the time, Pallas kernels for 38%

profile of v2, /device:TPU:0, one launch (start us, length us, event | category | flops | bytes accessed | tf_op | source)
XLA Modules:
  0.0 83.5 jit_solution(16012966701878650895)
XLA Ops:
  0.6 4.1 %collective-permute-start = (s32[1]{0:T(128)}, s32[1]{0:T(128)}, u32[]{:S(2)}, u32[]{:S(2)}) collective-permute-start(s32[1]{0:T(128)} %param.11), channel_id=1, source_target_pairs={{0,8},{1,9},{2,10},{3,11},{4,12},{5,13},{6,14},{7,15},{8,0},{9,1},... | collective-permute-start | bytes 20 | tf_op jit(solution)/shard_map/ppermute | solution.py:315
  5.4 0.9 %collective-permute-done.refs_1_ = s32[1]{0:T(128)} collective-permute-done((s32[1]{0:T(128)}, s32[1]{0:T(128)}, u32[]{:S(2)}, u32[]{:S(2)}) %collective-permute-start) | collective-permute-done | bytes 36 | tf_op jit(solution)/shard_map/ppermute | solution.py:315
  6.3 0.0 copy-start
  6.3 1.0 %copy-done = bf16[512,512]{1,0:T(8,128)(2,1)S(1)} copy-done((bf16[512,512]{1,0:T(8,128)(2,1)S(1)}, bf16[512,512]{1,0:T(8,128)(2,1)}, u32[]{:S(2)}) %copy-start) | copy-done | bytes 524312
  7.4 0.8 prepare.1
  8.2 1.9 %collective-permute-start.2 = (bf16[528,128]{1,0:T(8,128)(2,1)S(1)}, bf16[528,128]{1,0:T(8,128)(2,1)S(1)}, u32[]{:S(2)}, u32[]{:S(2)}) collective-permute-start(bf16[528,128]{1,0:T(8,128)(2,1)S(1)} %get-tuple-element.13), channel_id=1, source_target_pairs={{0,2},{1,3},{2,0},{3,1},{4,6},{5,7},{6,4},{7,5},{8,10},{9,11},{10,... | collective-permute-start | bytes 405512 | tf_op jit(solution)/shard_map/ppermute | solution.py:315
  10.1 1.6 %collective-permute-start.4 = (bf16[528,128]{1,0:T(8,128)(2,1)S(1)}, bf16[528,128]{1,0:T(8,128)(2,1)S(1)}, u32[]{:S(2)}, u32[]{:S(2)}) collective-permute-start(bf16[528,128]{1,0:T(8,128)(2,1)S(1)} %get-tuple-element.14), channel_id=1, source_target_pairs={{0,4},{1,5},{2,6},{3,7},{4,0},{5,1},{6,2},{7,3},{8,12},{9,13},{10,... | collective-permute-start | bytes 405512 | tf_op jit(solution)/shard_map/ppermute | solution.py:315
  11.7 0.1 collective-permute-start.6
  11.8 0.0 copy-start.1
  11.8 0.9 %copy-done.1 = bf16[32,4096]{1,0:T(8,128)(2,1)S(1)} copy-done((bf16[32,4096]{1,0:T(8,128)(2,1)S(1)}, bf16[32,4096]{1,0:T(8,128)(2,1)}, u32[]{:S(2)}) %copy-start.1) | copy-done | bytes 262168
  12.7 0.8 spread.1
  13.5 6.3 %all-to-all-start = ((bf16[16,32,512]{2,1,0:T(8,128)(2,1)}), bf16[16,32,512]{2,1,0:T(8,128)(2,1)S(1)}, u32[]{:S(2)}, u32[]{:S(2)}) async-start(bf16[16,32,512]{2,1,0:T(8,128)(2,1)} %spread.1), calls=%async_computation | async-start | bytes 1048576 | tf_op jit(solution)/shard_map/all_to_all | solution.py:319
  19.8 0.4 collective-permute-start.1
  20.2 0.0 collective-permute-done.2.refs_2_
  20.2 0.2 collective-permute-start.3
  20.4 0.0 collective-permute-done.4.refs_4_
  20.4 0.3 collective-permute-start.5
  20.7 0.0 collective-permute-done.6.refs_6_
  20.7 0.2 collective-permute-start.7
  20.9 0.0 copy-start.2
  20.9 13.6 %project.1.refs_9_ = bf16[512,1024]{1,0:T(8,128)(2,1)S(1)} custom-call(bf16[512,8192]{1,0:T(8,128)(2,1)} %x_ref.1, f32[1,8192]{1,0:T(1,128)} %bitcast.27, bf16[8192,1024]{1,0:T(8,128)(2,1)} %weight_ref.1, f32[1,1024]{1,0:T(1,128)} %bitcast.28), custom_call_target="tpu_custom_call" | custom-call | flops 8589934592 | bytes 25165824 | tf_op jit(solution)/shard_map/project/pallas_call | solution.py:68
  34.5 0.0 collective-permute-done.1.refs_1_
  34.5 0.0 collective-permute-done.3.refs_3_
  34.6 0.0 collective-permute-done.5.refs_5_
  34.6 0.0 collective-permute-done.7.refs_7_
  34.6 0.0 copy-done.2
  34.6 2.2 %pick.1 = bf16[512,1024]{1,0:T(8,128)(2,1)} custom-call(s32[1]{0:T(128)} %bitcast.1.me_ref, bf16[528,128]{1,0:T(8,128)(2,1)S(1)} %get-tuple-element.12.refs_0_, bf16[528,128]{1,0:T(8,128)(2,1)S(1)} %collective-permute-done.1.refs_1_, bf16[528,128]{1,0:T(8,128)(2,1)S(1)} %collective-permute-done.2.refs_2_, ...), custom_call_target="tpu_custom_call" | custom-call | flops 805306368 | bytes 2097152 | tf_op jit(solution)/shard_map/pick/pallas_call | solution.py:173
  36.8 0.0 all-to-all-done
  36.8 6.0 %all-to-all-start.1 = ((bf16[16,32,1024]{2,1,0:T(8,128)(2,1)}), bf16[16,32,1024]{2,1,0:T(8,128)(2,1)S(1)}, u32[]{:S(2)}, u32[]{:S(2)}) async-start(bf16[16,32,1024]{2,1,0:T(8,128)(2,1)} %bitcast.10), calls=%async_computation.1 | async-start | bytes 2097152 | tf_op jit(solution)/shard_map/all_to_all | solution.py:329
  42.8 5.4 %score.3 = (bf16[4096,1024]{1,0:T(8,128)(2,1)S(1)}, f32[16,1024]{1,0:T(8,128)S(1)}, f32[1,1024]{1,0:T(1,128)S(1)}) custom-call(bf16[512,512]{1,0:T(8,128)(2,1)S(1)} %bitcast.19, bf16[528,128]{1,0:T(8,128)(2,1)S(1)} %get-tuple-element.12.refs_0_, bf16[528,128]{1,0:T(8,128)(2,1)S(1)} %collective-permute-done.1.refs_1_, ...), custom_call_target="tpu_custom_call" | custom-call | flops 1073741824 | bytes 8388608 | tf_op jit(solution)/shard_map/score/pallas_call | solution.py:256
  48.2 2.9 %collective-permute-start.9 = (f32[1,1024]{1,0:T(1,128)S(1)}, f32[1,1024]{1,0:T(1,128)S(1)}, u32[]{:S(2)}, u32[]{:S(2)}) collective-permute-start(f32[1,1024]{1,0:T(1,128)S(1)} %get-tuple-element.21.lse_ref), channel_id=1, source_target_pairs={{0,8},{1,9},{2,10},{3,11},{4,12},{5,13},{6,14},{7,15},{8,0},{9,1},... | collective-permute-start | bytes 12296 | tf_op jit(solution)/shard_map/ppermute | solution.py:315
  51.0 5.2 %score.2 = (bf16[4096,1024]{1,0:T(8,128)(2,1)S(1)}, f32[16,1024]{1,0:T(8,128)S(1)}, f32[1,1024]{1,0:T(1,128)S(1)}) custom-call(bf16[512,512]{1,0:T(8,128)(2,1)S(1)} %bitcast.20, bf16[528,128]{1,0:T(8,128)(2,1)S(1)} %get-tuple-element.12.refs_0_, bf16[528,128]{1,0:T(8,128)(2,1)S(1)} %collective-permute-done.1.refs_1_, ...), custom_call_target="tpu_custom_call" | custom-call | flops 1073741824 | bytes 8388608 | tf_op jit(solution)/shard_map/score/pallas_call | solution.py:256
  56.2 0.2 collective-permute-start.8
  56.4 13.2 %collective-permute-done.9.rest_0_ = f32[1,1024]{1,0:T(1,128)S(1)} collective-permute-done((f32[1,1024]{1,0:T(1,128)S(1)}, f32[1,1024]{1,0:T(1,128)S(1)}, u32[]{:S(2)}, u32[]{:S(2)}) %collective-permute-start.9) | collective-permute-done | bytes 4128 | tf_op jit(solution)/shard_map/ppermute | solution.py:315
  69.6 2.3 %weigh.3 = f32[16,256]{1,0:T(8,128)S(1)} custom-call(bf16[4096,1024]{1,0:T(8,128)(2,1)S(1)} %get-tuple-element.19.prob_ref, f32[16,1024]{1,0:T(8,128)S(1)} %get-tuple-element.20.top_ref, f32[1,1024]{1,0:T(1,128)S(1)} %get-tuple-element.21.lse_ref, f32[1,1024]{1,0:T(1,128)S(1)} %collective-permute-done.9.rest_0_), custom_call_target="tpu_custom_call" | custom-call | flops 16777216 | bytes 8388608 | tf_op jit(solution)/shard_map/weigh/pallas_call | solution.py:297
  71.9 0.0 collective-permute-done.8.rest_0_
  71.9 2.3 %weigh.2 = f32[16,256]{1,0:T(8,128)S(1)} custom-call(bf16[4096,1024]{1,0:T(8,128)(2,1)S(1)} %get-tuple-element.16.prob_ref, f32[16,1024]{1,0:T(8,128)S(1)} %get-tuple-element.17.top_ref, f32[1,1024]{1,0:T(1,128)S(1)} %get-tuple-element.18.lse_ref, f32[1,1024]{1,0:T(1,128)S(1)} %collective-permute-done.8.rest_0_), custom_call_target="tpu_custom_call" | custom-call | flops 16777216 | bytes 8388608 | tf_op jit(solution)/shard_map/weigh/pallas_call | solution.py:297
  74.3 0.1 collective-permute-start.10
  74.4 1.2 %collective-permute-done.10 = f32[4,512]{1,0:T(4,128)S(1)} collective-permute-done((f32[4,512]{1,0:T(4,128)S(1)}, f32[4,512]{1,0:T(4,128)S(1)}, u32[]{:S(2)}, u32[]{:S(2)}) %collective-permute-start.10) | collective-permute-done | bytes 8224 | tf_op jit(solution)/shard_map/ppermute | solution.py:315
  75.5 1.5 %collective-permute-start.11 = (f32[512]{0:T(512)S(1)}, f32[512]{0:T(512)S(1)}, u32[]{:S(2)}, u32[]{:S(2)}) collective-permute-start(f32[512]{0:T(512)S(1)} %bitcast.26), channel_id=1, source_target_pairs={{0,2},{1,3},{2,0},{3,1},{4,6},{5,7},{6,4},{7,5},{8,10},{9,11},{10,... | collective-permute-start | bytes 6152 | tf_op jit(solution)/shard_map/ppermute | solution.py:315
  77.1 0.0 collective-permute-start.12
  77.1 2.0 %collective-permute-start.13 = (f32[512]{0:T(512)S(1)}, f32[512]{0:T(512)S(1)}, u32[]{:S(2)}, u32[]{:S(2)}) collective-permute-start(f32[512]{0:T(512)S(1)} %bitcast.24), channel_id=1, source_target_pairs={{0,6},{1,7},{2,4},{3,5},{4,2},{5,3},{6,0},{7,1},{8,14},{9,15},{10,... | collective-permute-start | bytes 6152 | tf_op jit(solution)/shard_map/ppermute | solution.py:315
  79.1 0.1 collective-permute-done.11
  79.2 1.5 %collective-permute-done.12 = f32[512]{0:T(512)S(1)} collective-permute-done((f32[512]{0:T(512)S(1)}, f32[512]{0:T(512)S(1)}, u32[]{:S(2)}, u32[]{:S(2)}) %collective-permute-start.12) | collective-permute-done | bytes 2080 | tf_op jit(solution)/shard_map/ppermute | solution.py:315
  80.7 0.9 %collective-permute-done.13 = f32[512]{0:T(512)S(1)} collective-permute-done((f32[512]{0:T(512)S(1)}, f32[512]{0:T(512)S(1)}, u32[]{:S(2)}, u32[]{:S(2)}) %collective-permute-start.13) | collective-permute-done | bytes 2080 | tf_op jit(solution)/shard_map/ppermute | solution.py:315
  81.6 0.6 add_add_fusion
  82.2 0.0 all-to-all-done.1
  82.2 1.3 %place.1 = bf16[256,1024]{1,0:T(8,128)(2,1)} custom-call(s32[1]{0:T(128)} %bitcast.1.me_ref, bf16[528,128]{1,0:T(8,128)(2,1)S(1)} %get-tuple-element.12.refs_0_, bf16[528,128]{1,0:T(8,128)(2,1)S(1)} %collective-permute-done.1.refs_1_, bf16[528,128]{1,0:T(8,128)(2,1)S(1)} %collective-permute-done.2.refs_2_, ...), custom_call_target="tpu_custom_call" | custom-call | flops 268435456 | bytes 1572864 | tf_op jit(solution)/shard_map/place/pallas_call | solution.py:205
  (6 shorter events, 0.1 us)
Async XLA Ops:
  0.6 5.7 %collective-permute-start = (s32[1]{0:T(128)}, s32[1]{0:T(128)}, u32[]{:S(2)}, u32[]{:S(2)}) collective-permute-start(s32[1]{0:T(128)} %param.11), channel_id=1, source_target_pairs={{0,8},{1,9},{2,10},{3,11},{4,12},{5,13},{6,14},{7,15},{8,0},{9,1},... | collective-permute-start | bytes 20 | tf_op jit(solution)/shard_map/ppermute | solution.py:315
  6.3 1.0 %copy-start = (bf16[512,512]{1,0:T(8,128)(2,1)S(1)}, bf16[512,512]{1,0:T(8,128)(2,1)}, u32[]{:S(2)}) copy-start(bf16[512,512]{1,0:T(8,128)(2,1)} %refs_2_.1) | copy-start | bytes 1572868
  8.2 12.0 %collective-permute-start.2 = (bf16[528,128]{1,0:T(8,128)(2,1)S(1)}, bf16[528,128]{1,0:T(8,128)(2,1)S(1)}, u32[]{:S(2)}, u32[]{:S(2)}) collective-permute-start(bf16[528,128]{1,0:T(8,128)(2,1)S(1)} %get-tuple-element.13), channel_id=1, source_target_pairs={{0,2},{1,3},{2,0},{3,1},{4,6},{5,7},{6,4},{7,5},{8,10},{9,11},{10,... | collective-permute-start | bytes 405512 | tf_op jit(solution)/shard_map/ppermute | solution.py:315
  10.1 10.3 %collective-permute-start.4 = (bf16[528,128]{1,0:T(8,128)(2,1)S(1)}, bf16[528,128]{1,0:T(8,128)(2,1)S(1)}, u32[]{:S(2)}, u32[]{:S(2)}) collective-permute-start(bf16[528,128]{1,0:T(8,128)(2,1)S(1)} %get-tuple-element.14), channel_id=1, source_target_pairs={{0,4},{1,5},{2,6},{3,7},{4,0},{5,1},{6,2},{7,3},{8,12},{9,13},{10,... | collective-permute-start | bytes 405512 | tf_op jit(solution)/shard_map/ppermute | solution.py:315
  11.7 9.0 %collective-permute-start.6 = (bf16[528,128]{1,0:T(8,128)(2,1)S(1)}, bf16[528,128]{1,0:T(8,128)(2,1)S(1)}, u32[]{:S(2)}, u32[]{:S(2)}) collective-permute-start(bf16[528,128]{1,0:T(8,128)(2,1)S(1)} %get-tuple-element.15), channel_id=1, source_target_pairs={{0,6},{1,7},{2,4},{3,5},{4,2},{5,3},{6,0},{7,1},{8,14},{9,15},{10,... | collective-permute-start | bytes 405512 | tf_op jit(solution)/shard_map/ppermute | solution.py:315
  11.8 0.9 %copy-start.1 = (bf16[32,4096]{1,0:T(8,128)(2,1)S(1)}, bf16[32,4096]{1,0:T(8,128)(2,1)}, u32[]{:S(2)}) copy-start(bf16[32,4096]{1,0:T(8,128)(2,1)} %q_ref.1) | copy-start | bytes 786436
  13.5 23.3 %all-to-all-start = ((bf16[16,32,512]{2,1,0:T(8,128)(2,1)}), bf16[16,32,512]{2,1,0:T(8,128)(2,1)S(1)}, u32[]{:S(2)}, u32[]{:S(2)}) async-start(bf16[16,32,512]{2,1,0:T(8,128)(2,1)} %spread.1), calls=%async_computation | async-start | bytes 1048576 | tf_op jit(solution)/shard_map/all_to_all | solution.py:319
  19.8 14.7 %collective-permute-start.1 = (bf16[528,128]{1,0:T(8,128)(2,1)S(1)}, bf16[528,128]{1,0:T(8,128)(2,1)S(1)}, u32[]{:S(2)}, u32[]{:S(2)}) collective-permute-start(bf16[528,128]{1,0:T(8,128)(2,1)S(1)} %get-tuple-element.12.refs_0_), channel_id=1, source_target_pairs={{0,1},{1,0},{2,3},{3,2},{4,5},{5,4},{6,7},{7,6},{8,9},{9,8},{10,11... | collective-permute-start | bytes 405512 | tf_op jit(solution)/shard_map/ppermute | solution.py:315
  20.2 14.3 %collective-permute-start.3 = (bf16[528,128]{1,0:T(8,128)(2,1)S(1)}, bf16[528,128]{1,0:T(8,128)(2,1)S(1)}, u32[]{:S(2)}, u32[]{:S(2)}) collective-permute-start(bf16[528,128]{1,0:T(8,128)(2,1)S(1)} %collective-permute-done.2.refs_2_), channel_id=1, source_target_pairs={{0,1},{1,0},{2,3},{3,2},{4,5},{5,4},{6,7},{7,6},{8,9},{9,8},{10,11... | collective-permute-start | bytes 405512 | tf_op jit(solution)/shard_map/ppermute | solution.py:315
  20.4 14.2 %collective-permute-start.5 = (bf16[528,128]{1,0:T(8,128)(2,1)S(1)}, bf16[528,128]{1,0:T(8,128)(2,1)S(1)}, u32[]{:S(2)}, u32[]{:S(2)}) collective-permute-start(bf16[528,128]{1,0:T(8,128)(2,1)S(1)} %collective-permute-done.4.refs_4_), channel_id=1, source_target_pairs={{0,1},{1,0},{2,3},{3,2},{4,5},{5,4},{6,7},{7,6},{8,9},{9,8},{10,11... | collective-permute-start | bytes 405512 | tf_op jit(solution)/shard_map/ppermute | solution.py:315
  20.7 13.8 %collective-permute-start.7 = (bf16[528,128]{1,0:T(8,128)(2,1)S(1)}, bf16[528,128]{1,0:T(8,128)(2,1)S(1)}, u32[]{:S(2)}, u32[]{:S(2)}) collective-permute-start(bf16[528,128]{1,0:T(8,128)(2,1)S(1)} %collective-permute-done.6.refs_6_), channel_id=1, source_target_pairs={{0,1},{1,0},{2,3},{3,2},{4,5},{5,4},{6,7},{7,6},{8,9},{9,8},{10,11... | collective-permute-start | bytes 405512 | tf_op jit(solution)/shard_map/ppermute | solution.py:315
  20.9 13.7 %copy-start.2 = (s32[512]{0:T(512)S(1)}, s32[512]{0:T(512)}, u32[]{:S(2)}) copy-start(s32[512]{0:T(512)} %param.12) | copy-start | bytes 6148
  36.8 45.4 %all-to-all-start.1 = ((bf16[16,32,1024]{2,1,0:T(8,128)(2,1)}), bf16[16,32,1024]{2,1,0:T(8,128)(2,1)S(1)}, u32[]{:S(2)}, u32[]{:S(2)}) async-start(bf16[16,32,1024]{2,1,0:T(8,128)(2,1)} %bitcast.10), calls=%async_computation.1 | async-start | bytes 2097152 | tf_op jit(solution)/shard_map/all_to_all | solution.py:329
  48.2 21.4 %collective-permute-start.9 = (f32[1,1024]{1,0:T(1,128)S(1)}, f32[1,1024]{1,0:T(1,128)S(1)}, u32[]{:S(2)}, u32[]{:S(2)}) collective-permute-start(f32[1,1024]{1,0:T(1,128)S(1)} %get-tuple-element.21.lse_ref), channel_id=1, source_target_pairs={{0,8},{1,9},{2,10},{3,11},{4,12},{5,13},{6,14},{7,15},{8,0},{9,1},... | collective-permute-start | bytes 12296 | tf_op jit(solution)/shard_map/ppermute | solution.py:315
  56.2 15.7 %collective-permute-start.8 = (f32[1,1024]{1,0:T(1,128)S(1)}, f32[1,1024]{1,0:T(1,128)S(1)}, u32[]{:S(2)}, u32[]{:S(2)}) collective-permute-start(f32[1,1024]{1,0:T(1,128)S(1)} %get-tuple-element.18.lse_ref), channel_id=1, source_target_pairs={{0,8},{1,9},{2,10},{3,11},{4,12},{5,13},{6,14},{7,15},{8,0},{9,1},... | collective-permute-start | bytes 12296 | tf_op jit(solution)/shard_map/ppermute | solution.py:315
  74.3 1.2 %collective-permute-start.10 = (f32[4,512]{1,0:T(4,128)S(1)}, f32[4,512]{1,0:T(4,128)S(1)}, u32[]{:S(2)}, u32[]{:S(2)}) collective-permute-start(f32[4,512]{1,0:T(4,128)S(1)} %bitcast.22), channel_id=1, source_target_pairs={{0,1},{1,0},{2,3},{3,2},{4,5},{5,4},{6,7},{7,6},{8,9},{9,8},{10,11... | collective-permute-start | bytes 24584 | tf_op jit(solution)/shard_map/ppermute | solution.py:315
  75.5 3.7 %collective-permute-start.11 = (f32[512]{0:T(512)S(1)}, f32[512]{0:T(512)S(1)}, u32[]{:S(2)}, u32[]{:S(2)}) collective-permute-start(f32[512]{0:T(512)S(1)} %bitcast.26), channel_id=1, source_target_pairs={{0,2},{1,3},{2,0},{3,1},{4,6},{5,7},{6,4},{7,5},{8,10},{9,11},{10,... | collective-permute-start | bytes 6152 | tf_op jit(solution)/shard_map/ppermute | solution.py:315
  77.1 3.6 %collective-permute-start.12 = (f32[512]{0:T(512)S(1)}, f32[512]{0:T(512)S(1)}, u32[]{:S(2)}, u32[]{:S(2)}) collective-permute-start(f32[512]{0:T(512)S(1)} %bitcast.25), channel_id=1, source_target_pairs={{0,4},{1,5},{2,6},{3,7},{4,0},{5,1},{6,2},{7,3},{8,12},{9,13},{10,... | collective-permute-start | bytes 6152 | tf_op jit(solution)/shard_map/ppermute | solution.py:315
  77.1 4.5 %collective-permute-start.13 = (f32[512]{0:T(512)S(1)}, f32[512]{0:T(512)S(1)}, u32[]{:S(2)}, u32[]{:S(2)}) collective-permute-start(f32[512]{0:T(512)S(1)} %bitcast.24), channel_id=1, source_target_pairs={{0,6},{1,7},{2,4},{3,5},{4,2},{5,3},{6,0},{7,1},{8,14},{9,15},{10,... | collective-permute-start | bytes 6152 | tf_op jit(solution)/shard_map/ppermute | solution.py:315

commit v3 on v2

--- a/solution.py
+++ b/solution.py
@@ -8,7 +8,8 @@
 from jax.sharding import PartitionSpec as P
 
 HD = 128
-CELL = 8
+CHIPS = 4
+CELL = 2 * CHIPS
 EPS = 1e-06
 F32 = jnp.float32
 BF16 = jnp.bfloat16
@@ -83,10 +84,22 @@
     )(*map(in_hbm, (hidden, gain.reshape(1, -1), weight, bias.reshape(1, -1))))
 
 
+def place_in_cell(device, size):
+    return device // (size // CHIPS) * 2 + device % 2
+
+
+def cell_steps(size):
+    return [chip * (size // CHIPS) + core for chip in range(CHIPS) for core in range(2)]
+
+
+def cross_steps(size):
+    return list(range(0, size // CHIPS, 2))
+
+
 def spread_kernel(q_ref, out_ref):
     share = out_ref.shape[2]
     for i in range(out_ref.shape[0]):
-        at = (i % CELL) * share
+        at = place_in_cell(i, out_ref.shape[0]) * share
         out_ref[i] = q_ref[:, at : at + share]
 
 
@@ -103,9 +116,9 @@
     )(queries)
 
 
-def prepare_kernel(cells, me_ref, *refs):
+def prepare_kernel(cells, stride, me_ref, *refs):
     count_refs, keys_ref, out_refs = refs[:cells], refs[cells], refs[cells + 1 :]
-    me = me_ref[0] & (CELL - 1)
+    me = me_ref[0]
     rows = keys_ref.shape[0]
     lane = lax.broadcasted_iota(jnp.int32, (EXTRA, 128), 1)
     high = lax.broadcasted_iota(jnp.int32, (EXTRA, 128), 0) < EXTRA // 2
@@ -115,16 +128,16 @@
         extra = jnp.where(lane == c, jnp.where(high, count // 8, count % 8), extra)
     extra = extra.astype(F32).astype(BF16)
     for i, out_ref in enumerate(out_refs):
-        head = (me ^ (2 * i)) // 2
+        head = (me ^ (stride * i)) // stride
         out_ref[:rows, :] = keys_ref[:, pl.ds(pl.multiple_of(head * HD, HD), HD)]
         out_ref[rows:, :] = extra
 
 
-def prepare(me, counts, keys):
-    n = CELL // 2
+def prepare(me, counts, keys, size):
+    n = CHIPS
     block = jax.ShapeDtypeStruct((keys.shape[0] + EXTRA, HD), BF16)
     return pl.pallas_call(
-        functools.partial(prepare_kernel, len(counts)),
+        functools.partial(prepare_kernel, len(counts), size // CHIPS),
         in_specs=[SMEM] * (1 + len(counts)) + [VMEM],
         out_specs=[VMEM] * n,
         out_shape=[block] * n,
@@ -134,13 +147,13 @@
     )(me, *counts, keys)
 
 
-def counts_of(me, refs, cells):
+def counts_of(me, refs, size):
     pairs = []
-    for r, ref in enumerate(refs):
+    for r, ref in zip(cell_steps(size), refs):
         extra = ref[...].astype(F32)
         count = (extra[:1] * 8.0 + extra[EXTRA // 2 : EXTRA // 2 + 1]).astype(jnp.int32)
-        for c in range(cells):
-            pairs.append((me ^ (r + CELL * c), count[:, c : c + 1]))
+        for c, cross in enumerate(cross_steps(size)):
+            pairs.append((me ^ r ^ cross, count[:, c : c + 1]))
     return pairs
 
 
@@ -148,7 +161,7 @@
     count_refs, (keep_ref, rows_ref, out_ref) = refs[:CELL], refs[CELL:]
     me = me_ref[0]
     start = jnp.zeros((1, 1), jnp.int32)
-    for device, count in counts_of(me, count_refs, size // CELL):
+    for device, count in counts_of(me, count_refs, size):
         start += jnp.where(device < me, count, 0)
     n = rows_ref.shape[0]
     cap = n // size
@@ -191,7 +204,7 @@
     source = slot // cap
     starts = jnp.zeros((1, n), jnp.int32)
     counts = jnp.zeros((1, n), jnp.int32)
-    for device, count in counts_of(me, count_refs, size // CELL):
+    for device, count in counts_of(me, count_refs, size):
         starts += jnp.where(source > device, count, 0)
         counts = jnp.where(source == device, count, counts)
     pos = ((me - starts) & (size - 1)) + (slot & (cap - 1)) * size
@@ -314,13 +327,15 @@
     def swap(x, r):
         return lax.ppermute(x, "seq", [(i, i ^ r) for i in range(size)])
 
-    counts = [keep_count] + [swap(keep_count, CELL * d) for d in range(1, size // CELL)]
+    cross = cross_steps(size)[1:]
+    counts = [keep_count] + [swap(keep_count, r) for r in cross]
 
     my_q = lax.all_to_all(spread(queries, size), "seq", split_axis=0, concat_axis=0, tiled=True)
     my_q = my_q.reshape(size * tokens, -1)
 
-    evens = prepare(me, counts, visual_keys)
-    evens = [evens[0]] + [swap(evens[i], 2 * i) for i in range(1, CELL // 2)]
+    far = [chip * (size // CHIPS) for chip in range(1, CHIPS)]
+    evens = prepare(me, counts, visual_keys, size)
+    evens = [evens[0]] + [swap(block, r) for block, r in zip(evens[1:], far)]
     odds = [swap(block, 1) for block in evens]
     blocks = [block for pair in zip(evens, odds) for block in pair]
 
@@ -337,13 +352,13 @@
     factor = own_keys * size / total_rows
     partial = 0.0
     for prob, tops, lse in parts:
-        others = [swap(lse, CELL * d) for d in range(1, size // CELL)]
+        others = [swap(lse, r) for r in cross]
         partial = partial + weigh(prob, tops, lse, others, factor)
-    partial = partial.reshape(CELL // 2, 2, own_keys)
-    chip = partial[:, 0] + swap(partial[:, 1], 1)
-    importance = chip[0]
-    for i in range(1, CELL // 2):
-        importance = importance + swap(chip[i], 2 * i)
+    partial = partial.reshape(CHIPS, 2, own_keys)
+    chips = partial[:, 0] + swap(partial[:, 1], 1)
+    importance = chips[0]
+    for chip, r in zip(chips[1:], far):
+        importance = importance + swap(chip, r)
     return (importance, layer_kv)
 
 

time: 83.9 us -> 74.5 us (0.89)
  waiting for transfers between devices: 17.8 us -> 9.28 us
    ppermute x14, waiting for transfers between devices: 17.8 us -> 9.28 us  [swap(): return lax.ppermute(x, 'seq', [(i, i ^ r) for i in range(size)])]
    all_to_all x1, starting transfers between devices: 5.96 us -> 5.08 us  [shards(): lax.all_to_all(picked.reshape(size, own_keys // size, -1), 'seq', split_a...]
  transfers between devices with their start and end apart: 16 -> 16, of which waited for: 6 -> 6; matrix products, arithmetic and copies ran while one was open for 1% -> 1% of each run, Pallas kernels for 38% -> 43%
where the time goes in v3:
time: 74.5 us; the launch traced here: 74.1 us
  Pallas kernels  34 us (46%)
  starting transfers between devices  26.8 us (36%)
  waiting for transfers between devices  9.28 us (12%)
  local copies, waits for them, and re-layouts  2.04 us (3%)
  between operations  1.47 us (2%)
    ppermute x14, starting transfers between devices, swap(): return lax.ppermute(x, 'seq', [(i, i ^ r) for i in range(size)])  15.5 us
    pallas_call x1, Pallas kernels, project(): pl.pallas_call(project_kernel, grid=(width // depth,), in_specs=[pl.Block...  13.6 us
    pallas_call x2, Pallas kernels, score(): pl.pallas_call(functools.partial(score_kernel, first, chunk, tile), in_sp...  10.6 us
    ppermute x14, waiting for transfers between devices, swap(): return lax.ppermute(x, 'seq', [(i, i ^ r) for i in range(size)])  9.28 us
    all_to_all x1, starting transfers between devices, shards(): lax.all_to_all(spread(queries, size), 'seq', split_axis=0, concat_axis=0,...  6.16 us
    all_to_all x1, starting transfers between devices, shards(): lax.all_to_all(picked.reshape(size, own_keys // size, -1), 'seq', split_a...  5.08 us
    pallas_call x2, Pallas kernels, weigh(): pl.pallas_call(functools.partial(weigh_kernel, factor), in_specs=[VMEM] *...  4.58 us
    pallas_call x1, Pallas kernels, pick(): pl.pallas_call(functools.partial(pick_kernel, size), grid=(1,), in_specs=...  2.21 us
  transfers between devices with their start and end apart: 16, of which 6 were waited for; matrix products, arithmetic and copies ran while one was open for 1% of the time, Pallas kernels for 43%

profile of v3, /device:TPU:0, one launch (start us, length us, event | category | flops | bytes accessed | tf_op | source)
XLA Modules:
  0.0 74.1 jit_solution(17312322493612166682)
XLA Ops:
  0.6 3.0 %collective-permute-start = (s32[1]{0:T(128)}, s32[1]{0:T(128)}, u32[]{:S(2)}, u32[]{:S(2)}) collective-permute-start(s32[1]{0:T(128)} %param.11), channel_id=1, source_target_pairs={{0,2},{1,3},{2,0},{3,1},{4,6},{5,7},{6,4},{7,5},{8,10},{9,11},{10,... | collective-permute-start | bytes 20 | tf_op jit(solution)/shard_map/ppermute | solution.py:328
  4.3 0.9 %collective-permute-done.refs_1_ = s32[1]{0:T(128)} collective-permute-done((s32[1]{0:T(128)}, s32[1]{0:T(128)}, u32[]{:S(2)}, u32[]{:S(2)}) %collective-permute-start) | collective-permute-done | bytes 36 | tf_op jit(solution)/shard_map/ppermute | solution.py:328
  5.3 0.0 copy-start
  5.3 1.0 %copy-done = bf16[512,512]{1,0:T(8,128)(2,1)S(1)} copy-done((bf16[512,512]{1,0:T(8,128)(2,1)S(1)}, bf16[512,512]{1,0:T(8,128)(2,1)}, u32[]{:S(2)}) %copy-start) | copy-done | bytes 524312
  6.3 0.8 %prepare.1 = (bf16[528,128]{1,0:T(8,128)(2,1)S(1)}, bf16[528,128]{1,0:T(8,128)(2,1)S(1)}, bf16[528,128]{1,0:T(8,128)(2,1)S(1)}, bf16[528,128]{1,0:T(8,128)(2,1)S(1)}) custom-call(s32[1]{0:T(128)} %bitcast.1.me_ref, s32[1]{0:T(128)S(6)} %copy.18.refs_0_, s32[1]{0:T(128)} %collective-permute-done.refs_1_, bf16[512,512]{1,0:T(8,128)(2,1)S(1)} %copy-done), custom_call_target="tpu_custom_call" | custom-call | bytes 1048576 | tf_op jit(solution)/shard_map/prepare/pallas_call | solution.py:139
  7.1 2.1 %collective-permute-start.2 = (bf16[528,128]{1,0:T(8,128)(2,1)S(1)}, bf16[528,128]{1,0:T(8,128)(2,1)S(1)}, u32[]{:S(2)}, u32[]{:S(2)}) collective-permute-start(bf16[528,128]{1,0:T(8,128)(2,1)S(1)} %get-tuple-element.13), channel_id=1, source_target_pairs={{0,4},{1,5},{2,6},{3,7},{4,0},{5,1},{6,2},{7,3},{8,12},{9,13},{10,... | collective-permute-start | bytes 405512 | tf_op jit(solution)/shard_map/ppermute | solution.py:328
  9.3 2.6 %collective-permute-start.4 = (bf16[528,128]{1,0:T(8,128)(2,1)S(1)}, bf16[528,128]{1,0:T(8,128)(2,1)S(1)}, u32[]{:S(2)}, u32[]{:S(2)}) collective-permute-start(bf16[528,128]{1,0:T(8,128)(2,1)S(1)} %get-tuple-element.14), channel_id=1, source_target_pairs={{0,8},{1,9},{2,10},{3,11},{4,12},{5,13},{6,14},{7,15},{8,0},{9,1},... | collective-permute-start | bytes 405512 | tf_op jit(solution)/shard_map/ppermute | solution.py:328
  11.9 0.0 collective-permute-start.6
  11.9 0.0 copy-start.1
  11.9 0.9 %copy-done.1 = bf16[32,4096]{1,0:T(8,128)(2,1)S(1)} copy-done((bf16[32,4096]{1,0:T(8,128)(2,1)S(1)}, bf16[32,4096]{1,0:T(8,128)(2,1)}, u32[]{:S(2)}) %copy-start.1) | copy-done | bytes 262168
  12.8 0.8 %spread.1 = bf16[16,32,512]{2,1,0:T(8,128)(2,1)} custom-call(bf16[32,4096]{1,0:T(8,128)(2,1)S(1)} %copy-done.1), custom_call_target="tpu_custom_call" | custom-call | bytes 786432 | tf_op jit(solution)/shard_map/spread/pallas_call | solution.py:108
  13.6 6.2 %all-to-all-start = ((bf16[16,32,512]{2,1,0:T(8,128)(2,1)}), bf16[16,32,512]{2,1,0:T(8,128)(2,1)S(1)}, u32[]{:S(2)}, u32[]{:S(2)}) async-start(bf16[16,32,512]{2,1,0:T(8,128)(2,1)} %spread.1), calls=%async_computation | async-start | bytes 1048576 | tf_op jit(solution)/shard_map/all_to_all | solution.py:333
  19.8 0.4 collective-permute-start.1
  20.2 0.0 collective-permute-done.2.refs_2_
  20.2 0.2 collective-permute-start.3
  20.4 1.1 %collective-permute-done.4.refs_4_ = bf16[528,128]{1,0:T(8,128)(2,1)S(1)} collective-permute-done((bf16[528,128]{1,0:T(8,128)(2,1)S(1)}, bf16[528,128]{1,0:T(8,128)(2,1)S(1)}, u32[]{:S(2)}, u32[]{:S(2)}) %collective-permute-start.4) | collective-permute-done | bytes 135200 | tf_op jit(solution)/shard_map/ppermute | solution.py:328
  21.5 0.0 collective-permute-start.5
  21.5 0.0 collective-permute-done.6.refs_6_
  21.5 0.5 collective-permute-start.7
  22.0 0.0 copy-start.2
  22.0 13.6 %project.1.refs_9_ = bf16[512,1024]{1,0:T(8,128)(2,1)S(1)} custom-call(bf16[512,8192]{1,0:T(8,128)(2,1)} %x_ref.1, f32[1,8192]{1,0:T(1,128)} %bitcast.27, bf16[8192,1024]{1,0:T(8,128)(2,1)} %weight_ref.1, f32[1,1024]{1,0:T(1,128)} %bitcast.28), custom_call_target="tpu_custom_call" | custom-call | flops 8589934592 | bytes 25165824 | tf_op jit(solution)/shard_map/project/pallas_call | solution.py:69
  35.7 0.0 collective-permute-done.1.refs_1_
  35.7 0.0 collective-permute-done.3.refs_3_
  35.7 0.0 collective-permute-done.5.refs_5_
  35.7 0.0 collective-permute-done.7.refs_7_
  35.7 0.0 copy-done.2
  35.7 2.2 %pick.1 = bf16[512,1024]{1,0:T(8,128)(2,1)} custom-call(s32[1]{0:T(128)} %bitcast.1.me_ref, bf16[528,128]{1,0:T(8,128)(2,1)S(1)} %get-tuple-element.12.refs_0_, bf16[528,128]{1,0:T(8,128)(2,1)S(1)} %collective-permute-done.1.refs_1_, bf16[528,128]{1,0:T(8,128)(2,1)S(1)} %collective-permute-done.2.refs_2_, ...), custom_call_target="tpu_custom_call" | custom-call | flops 805306368 | bytes 2097152 | tf_op jit(solution)/shard_map/pick/pallas_call | solution.py:186
  37.9 0.0 all-to-all-done
  37.9 5.1 %all-to-all-start.1 = ((bf16[16,32,1024]{2,1,0:T(8,128)(2,1)}), bf16[16,32,1024]{2,1,0:T(8,128)(2,1)S(1)}, u32[]{:S(2)}, u32[]{:S(2)}) async-start(bf16[16,32,1024]{2,1,0:T(8,128)(2,1)} %bitcast.10), calls=%async_computation.1 | async-start | bytes 2097152 | tf_op jit(solution)/shard_map/all_to_all | solution.py:344
  43.0 5.4 %score.3 = (bf16[4096,1024]{1,0:T(8,128)(2,1)S(1)}, f32[16,1024]{1,0:T(8,128)S(1)}, f32[1,1024]{1,0:T(1,128)S(1)}) custom-call(bf16[512,512]{1,0:T(8,128)(2,1)S(1)} %bitcast.19, bf16[528,128]{1,0:T(8,128)(2,1)S(1)} %get-tuple-element.12.refs_0_, bf16[528,128]{1,0:T(8,128)(2,1)S(1)} %collective-permute-done.1.refs_1_, ...), custom_call_target="tpu_custom_call" | custom-call | flops 1073741824 | bytes 8388608 | tf_op jit(solution)/shard_map/score/pallas_call | solution.py:269
  48.4 2.0 %collective-permute-start.9 = (f32[1,1024]{1,0:T(1,128)S(1)}, f32[1,1024]{1,0:T(1,128)S(1)}, u32[]{:S(2)}, u32[]{:S(2)}) collective-permute-start(f32[1,1024]{1,0:T(1,128)S(1)} %get-tuple-element.21.lse_ref), channel_id=1, source_target_pairs={{0,2},{1,3},{2,0},{3,1},{4,6},{5,7},{6,4},{7,5},{8,10},{9,11},{10,... | collective-permute-start | bytes 12296 | tf_op jit(solution)/shard_map/ppermute | solution.py:328
  50.4 5.2 %score.2 = (bf16[4096,1024]{1,0:T(8,128)(2,1)S(1)}, f32[16,1024]{1,0:T(8,128)S(1)}, f32[1,1024]{1,0:T(1,128)S(1)}) custom-call(bf16[512,512]{1,0:T(8,128)(2,1)S(1)} %bitcast.20, bf16[528,128]{1,0:T(8,128)(2,1)S(1)} %get-tuple-element.12.refs_0_, bf16[528,128]{1,0:T(8,128)(2,1)S(1)} %collective-permute-done.1.refs_1_, ...), custom_call_target="tpu_custom_call" | custom-call | flops 1073741824 | bytes 8388608 | tf_op jit(solution)/shard_map/score/pallas_call | solution.py:269
  55.6 0.2 collective-permute-start.8
  55.8 0.0 collective-permute-done.9.rest_0_
  55.8 2.3 %weigh.3 = f32[16,256]{1,0:T(8,128)S(1)} custom-call(bf16[4096,1024]{1,0:T(8,128)(2,1)S(1)} %get-tuple-element.19.prob_ref, f32[16,1024]{1,0:T(8,128)S(1)} %get-tuple-element.20.top_ref, f32[1,1024]{1,0:T(1,128)S(1)} %get-tuple-element.21.lse_ref, f32[1,1024]{1,0:T(1,128)S(1)} %collective-permute-done.9.rest_0_), custom_call_target="tpu_custom_call" | custom-call | flops 16777216 | bytes 8388608 | tf_op jit(solution)/shard_map/weigh/pallas_call | solution.py:310
  58.1 1.2 %collective-permute-done.8.rest_0_ = f32[1,1024]{1,0:T(1,128)S(1)} collective-permute-done((f32[1,1024]{1,0:T(1,128)S(1)}, f32[1,1024]{1,0:T(1,128)S(1)}, u32[]{:S(2)}, u32[]{:S(2)}) %collective-permute-start.8) | collective-permute-done | bytes 4128 | tf_op jit(solution)/shard_map/ppermute | solution.py:328
  59.3 2.3 %weigh.2 = f32[16,256]{1,0:T(8,128)S(1)} custom-call(bf16[4096,1024]{1,0:T(8,128)(2,1)S(1)} %get-tuple-element.16.prob_ref, f32[16,1024]{1,0:T(8,128)S(1)} %get-tuple-element.17.top_ref, f32[1,1024]{1,0:T(1,128)S(1)} %get-tuple-element.18.lse_ref, f32[1,1024]{1,0:T(1,128)S(1)} %collective-permute-done.8.rest_0_), custom_call_target="tpu_custom_call" | custom-call | flops 16777216 | bytes 8388608 | tf_op jit(solution)/shard_map/weigh/pallas_call | solution.py:310
  61.6 0.1 collective-permute-start.10
  61.7 1.2 %collective-permute-done.10 = f32[4,512]{1,0:T(4,128)S(1)} collective-permute-done((f32[4,512]{1,0:T(4,128)S(1)}, f32[4,512]{1,0:T(4,128)S(1)}, u32[]{:S(2)}, u32[]{:S(2)}) %collective-permute-start.10) | collective-permute-done | bytes 8224 | tf_op jit(solution)/shard_map/ppermute | solution.py:328
  62.9 1.6 %collective-permute-start.11 = (f32[512]{0:T(512)S(1)}, f32[512]{0:T(512)S(1)}, u32[]{:S(2)}, u32[]{:S(2)}) collective-permute-start(f32[512]{0:T(512)S(1)} %bitcast.26), channel_id=1, source_target_pairs={{0,4},{1,5},{2,6},{3,7},{4,0},{5,1},{6,2},{7,3},{8,12},{9,13},{10,... | collective-permute-start | bytes 6152 | tf_op jit(solution)/shard_map/ppermute | solution.py:328
  64.5 2.4 %collective-permute-start.12 = (f32[512]{0:T(512)S(1)}, f32[512]{0:T(512)S(1)}, u32[]{:S(2)}, u32[]{:S(2)}) collective-permute-start(f32[512]{0:T(512)S(1)} %bitcast.25), channel_id=1, source_target_pairs={{0,8},{1,9},{2,10},{3,11},{4,12},{5,13},{6,14},{7,15},{8,0},{9,1},... | collective-permute-start | bytes 6152 | tf_op jit(solution)/shard_map/ppermute | solution.py:328
  66.8 0.5 collective-permute-start.13
  67.3 0.0 collective-permute-done.11
  67.3 2.3 %collective-permute-done.12 = f32[512]{0:T(512)S(1)} collective-permute-done((f32[512]{0:T(512)S(1)}, f32[512]{0:T(512)S(1)}, u32[]{:S(2)}, u32[]{:S(2)}) %collective-permute-start.12) | collective-permute-done | bytes 2080 | tf_op jit(solution)/shard_map/ppermute | solution.py:328
  69.7 2.5 %collective-permute-done.13 = f32[512]{0:T(512)S(1)} collective-permute-done((f32[512]{0:T(512)S(1)}, f32[512]{0:T(512)S(1)}, u32[]{:S(2)}, u32[]{:S(2)}) %collective-permute-start.13) | collective-permute-done | bytes 2080 | tf_op jit(solution)/shard_map/ppermute | solution.py:328
  72.2 0.6 add_add_fusion
  72.8 0.0 all-to-all-done.1
  72.8 1.3 %place.1 = bf16[256,1024]{1,0:T(8,128)(2,1)} custom-call(s32[1]{0:T(128)} %bitcast.1.me_ref, bf16[528,128]{1,0:T(8,128)(2,1)S(1)} %get-tuple-element.12.refs_0_, bf16[528,128]{1,0:T(8,128)(2,1)S(1)} %collective-permute-done.1.refs_1_, bf16[528,128]{1,0:T(8,128)(2,1)S(1)} %collective-permute-done.2.refs_2_, ...), custom_call_target="tpu_custom_call" | custom-call | flops 268435456 | bytes 1572864 | tf_op jit(solution)/shard_map/place/pallas_call | solution.py:218
  (6 shorter events, 0.1 us)
Async XLA Ops:
  0.6 4.6 %collective-permute-start = (s32[1]{0:T(128)}, s32[1]{0:T(128)}, u32[]{:S(2)}, u32[]{:S(2)}) collective-permute-start(s32[1]{0:T(128)} %param.11), channel_id=1, source_target_pairs={{0,2},{1,3},{2,0},{3,1},{4,6},{5,7},{6,4},{7,5},{8,10},{9,11},{10,... | collective-permute-start | bytes 20 | tf_op jit(solution)/shard_map/ppermute | solution.py:328
  5.3 1.0 %copy-start = (bf16[512,512]{1,0:T(8,128)(2,1)S(1)}, bf16[512,512]{1,0:T(8,128)(2,1)}, u32[]{:S(2)}) copy-start(bf16[512,512]{1,0:T(8,128)(2,1)} %refs_2_.1) | copy-start | bytes 1572868
  7.1 13.1 %collective-permute-start.2 = (bf16[528,128]{1,0:T(8,128)(2,1)S(1)}, bf16[528,128]{1,0:T(8,128)(2,1)S(1)}, u32[]{:S(2)}, u32[]{:S(2)}) collective-permute-start(bf16[528,128]{1,0:T(8,128)(2,1)S(1)} %get-tuple-element.13), channel_id=1, source_target_pairs={{0,4},{1,5},{2,6},{3,7},{4,0},{5,1},{6,2},{7,3},{8,12},{9,13},{10,... | collective-permute-start | bytes 405512 | tf_op jit(solution)/shard_map/ppermute | solution.py:328
  9.3 12.2 %collective-permute-start.4 = (bf16[528,128]{1,0:T(8,128)(2,1)S(1)}, bf16[528,128]{1,0:T(8,128)(2,1)S(1)}, u32[]{:S(2)}, u32[]{:S(2)}) collective-permute-start(bf16[528,128]{1,0:T(8,128)(2,1)S(1)} %get-tuple-element.14), channel_id=1, source_target_pairs={{0,8},{1,9},{2,10},{3,11},{4,12},{5,13},{6,14},{7,15},{8,0},{9,1},... | collective-permute-start | bytes 405512 | tf_op jit(solution)/shard_map/ppermute | solution.py:328
  11.9 9.7 %collective-permute-start.6 = (bf16[528,128]{1,0:T(8,128)(2,1)S(1)}, bf16[528,128]{1,0:T(8,128)(2,1)S(1)}, u32[]{:S(2)}, u32[]{:S(2)}) collective-permute-start(bf16[528,128]{1,0:T(8,128)(2,1)S(1)} %get-tuple-element.15), channel_id=1, source_target_pairs={{0,12},{1,13},{2,14},{3,15},{4,8},{5,9},{6,10},{7,11},{8,4},{9,5},... | collective-permute-start | bytes 405512 | tf_op jit(solution)/shard_map/ppermute | solution.py:328
  11.9 1.0 %copy-start.1 = (bf16[32,4096]{1,0:T(8,128)(2,1)S(1)}, bf16[32,4096]{1,0:T(8,128)(2,1)}, u32[]{:S(2)}) copy-start(bf16[32,4096]{1,0:T(8,128)(2,1)} %q_ref.1) | copy-start | bytes 786436
  13.6 24.3 %all-to-all-start = ((bf16[16,32,512]{2,1,0:T(8,128)(2,1)}), bf16[16,32,512]{2,1,0:T(8,128)(2,1)S(1)}, u32[]{:S(2)}, u32[]{:S(2)}) async-start(bf16[16,32,512]{2,1,0:T(8,128)(2,1)} %spread.1), calls=%async_computation | async-start | bytes 1048576 | tf_op jit(solution)/shard_map/all_to_all | solution.py:333
  19.8 15.8 %collective-permute-start.1 = (bf16[528,128]{1,0:T(8,128)(2,1)S(1)}, bf16[528,128]{1,0:T(8,128)(2,1)S(1)}, u32[]{:S(2)}, u32[]{:S(2)}) collective-permute-start(bf16[528,128]{1,0:T(8,128)(2,1)S(1)} %get-tuple-element.12.refs_0_), channel_id=1, source_target_pairs={{0,1},{1,0},{2,3},{3,2},{4,5},{5,4},{6,7},{7,6},{8,9},{9,8},{10,11... | collective-permute-start | bytes 405512 | tf_op jit(solution)/shard_map/ppermute | solution.py:328
  20.2 15.4 %collective-permute-start.3 = (bf16[528,128]{1,0:T(8,128)(2,1)S(1)}, bf16[528,128]{1,0:T(8,128)(2,1)S(1)}, u32[]{:S(2)}, u32[]{:S(2)}) collective-permute-start(bf16[528,128]{1,0:T(8,128)(2,1)S(1)} %collective-permute-done.2.refs_2_), channel_id=1, source_target_pairs={{0,1},{1,0},{2,3},{3,2},{4,5},{5,4},{6,7},{7,6},{8,9},{9,8},{10,11... | collective-permute-start | bytes 405512 | tf_op jit(solution)/shard_map/ppermute | solution.py:328
  21.5 14.2 %collective-permute-start.5 = (bf16[528,128]{1,0:T(8,128)(2,1)S(1)}, bf16[528,128]{1,0:T(8,128)(2,1)S(1)}, u32[]{:S(2)}, u32[]{:S(2)}) collective-permute-start(bf16[528,128]{1,0:T(8,128)(2,1)S(1)} %collective-permute-done.4.refs_4_), channel_id=1, source_target_pairs={{0,1},{1,0},{2,3},{3,2},{4,5},{5,4},{6,7},{7,6},{8,9},{9,8},{10,11... | collective-permute-start | bytes 405512 | tf_op jit(solution)/shard_map/ppermute | solution.py:328
  21.5 14.2 %collective-permute-start.7 = (bf16[528,128]{1,0:T(8,128)(2,1)S(1)}, bf16[528,128]{1,0:T(8,128)(2,1)S(1)}, u32[]{:S(2)}, u32[]{:S(2)}) collective-permute-start(bf16[528,128]{1,0:T(8,128)(2,1)S(1)} %collective-permute-done.6.refs_6_), channel_id=1, source_target_pairs={{0,1},{1,0},{2,3},{3,2},{4,5},{5,4},{6,7},{7,6},{8,9},{9,8},{10,11... | collective-permute-start | bytes 405512 | tf_op jit(solution)/shard_map/ppermute | solution.py:328
  22.0 13.7 %copy-start.2 = (s32[512]{0:T(512)S(1)}, s32[512]{0:T(512)}, u32[]{:S(2)}) copy-start(s32[512]{0:T(512)} %param.12) | copy-start | bytes 6148
  37.9 34.9 %all-to-all-start.1 = ((bf16[16,32,1024]{2,1,0:T(8,128)(2,1)}), bf16[16,32,1024]{2,1,0:T(8,128)(2,1)S(1)}, u32[]{:S(2)}, u32[]{:S(2)}) async-start(bf16[16,32,1024]{2,1,0:T(8,128)(2,1)} %bitcast.10), calls=%async_computation.1 | async-start | bytes 2097152 | tf_op jit(solution)/shard_map/all_to_all | solution.py:344
  48.4 7.4 %collective-permute-start.9 = (f32[1,1024]{1,0:T(1,128)S(1)}, f32[1,1024]{1,0:T(1,128)S(1)}, u32[]{:S(2)}, u32[]{:S(2)}) collective-permute-start(f32[1,1024]{1,0:T(1,128)S(1)} %get-tuple-element.21.lse_ref), channel_id=1, source_target_pairs={{0,2},{1,3},{2,0},{3,1},{4,6},{5,7},{6,4},{7,5},{8,10},{9,11},{10,... | collective-permute-start | bytes 12296 | tf_op jit(solution)/shard_map/ppermute | solution.py:328
  55.6 3.7 %collective-permute-start.8 = (f32[1,1024]{1,0:T(1,128)S(1)}, f32[1,1024]{1,0:T(1,128)S(1)}, u32[]{:S(2)}, u32[]{:S(2)}) collective-permute-start(f32[1,1024]{1,0:T(1,128)S(1)} %get-tuple-element.18.lse_ref), channel_id=1, source_target_pairs={{0,2},{1,3},{2,0},{3,1},{4,6},{5,7},{6,4},{7,5},{8,10},{9,11},{10,... | collective-permute-start | bytes 12296 | tf_op jit(solution)/shard_map/ppermute | solution.py:328
  61.6 1.2 %collective-permute-start.10 = (f32[4,512]{1,0:T(4,128)S(1)}, f32[4,512]{1,0:T(4,128)S(1)}, u32[]{:S(2)}, u32[]{:S(2)}) collective-permute-start(f32[4,512]{1,0:T(4,128)S(1)} %bitcast.22), channel_id=1, source_target_pairs={{0,1},{1,0},{2,3},{3,2},{4,5},{5,4},{6,7},{7,6},{8,9},{9,8},{10,11... | collective-permute-start | bytes 24584 | tf_op jit(solution)/shard_map/ppermute | solution.py:328
  62.9 4.5 %collective-permute-start.11 = (f32[512]{0:T(512)S(1)}, f32[512]{0:T(512)S(1)}, u32[]{:S(2)}, u32[]{:S(2)}) collective-permute-start(f32[512]{0:T(512)S(1)} %bitcast.26), channel_id=1, source_target_pairs={{0,4},{1,5},{2,6},{3,7},{4,0},{5,1},{6,2},{7,3},{8,12},{9,13},{10,... | collective-permute-start | bytes 6152 | tf_op jit(solution)/shard_map/ppermute | solution.py:328
  64.5 5.2 %collective-permute-start.12 = (f32[512]{0:T(512)S(1)}, f32[512]{0:T(512)S(1)}, u32[]{:S(2)}, u32[]{:S(2)}) collective-permute-start(f32[512]{0:T(512)S(1)} %bitcast.25), channel_id=1, source_target_pairs={{0,8},{1,9},{2,10},{3,11},{4,12},{5,13},{6,14},{7,15},{8,0},{9,1},... | collective-permute-start | bytes 6152 | tf_op jit(solution)/shard_map/ppermute | solution.py:328
  66.8 5.4 %collective-permute-start.13 = (f32[512]{0:T(512)S(1)}, f32[512]{0:T(512)S(1)}, u32[]{:S(2)}, u32[]{:S(2)}) collective-permute-start(f32[512]{0:T(512)S(1)} %bitcast.24), channel_id=1, source_target_pairs={{0,12},{1,13},{2,14},{3,15},{4,8},{5,9},{6,10},{7,11},{8,4},{9,5},... | collective-permute-start | bytes 6152 | tf_op jit(solution)/shard_map/ppermute | solution.py:328

commit v4 on v2

v4 whole, which is shorter than its diff:
```python
import functools

import jax
import jax.numpy as jnp
from jax import lax
from jax.experimental import pallas as pl
from jax.experimental.pallas import tpu as pltpu
from jax.sharding import PartitionSpec as P

HD = 128
EPS = 1e-06
F32 = jnp.float32
BF16 = jnp.bfloat16
LOG2E = 1.4426950408889634
MIB = 1024 * 1024
SMEM = pl.BlockSpec(memory_space=pltpu.SMEM)
VMEM = pl.BlockSpec(memory_space=pltpu.VMEM)
ANY = pl.BlockSpec(memory_space=pl.ANY)
EXTRA = 16


def params(mib):
    return pltpu.CompilerParams(vmem_limit_bytes=mib * MIB)


def cost(flops, bytes_accessed, transcendentals=0):
    return pl.CostEstimate(
        flops=int(flops), bytes_accessed=int(bytes_accessed), transcendentals=int(transcendentals)
    )


def in_hbm(x):
    return pltpu.with_memory_space_constraint(x, pltpu.HBM)


def project_kernel(cuts, x_hbm, gain_hbm, weight_hbm, bias_hbm, out_ref, x, gain, weight, bias, total, sems):
    copies = []
    start = 0
    for i, depth in enumerate(cuts):
        at = pl.ds(start, depth)
        copies.append(
            [
                pltpu.make_async_copy(x_hbm.at[:, at], x.at[:, at], sems.at[0, i]),
                pltpu.make_async_copy(weight_hbm.at[at, :], weight.at[at, :], sems.at[1, i]),
            ]
        )
        start += depth
    copies[0].append(pltpu.make_async_copy(gain_hbm, gain, sems.at[2, 0]))
    copies[-1].append(pltpu.make_async_copy(bias_hbm, bias, sems.at[2, 1]))
    for group in copies:
        for copy in group:
            copy.start()
    width = x.shape[1]
    start = 0
    squares = None
    for i, depth in enumerate(cuts):
        for copy in copies[i]:
            copy.wait()
        values = x[:, start : start + depth].astype(F32)
        scaled = (values * gain[:, start : start + depth]).astype(BF16)
        part = jnp.dot(scaled, weight[start : start + depth, :], preferred_element_type=F32)
        square = values * values
        for col in range(0, depth, 128):
            lanes = square[:, col : col + 128]
            squares = lanes if squares is None else squares + lanes
        if i == 0:
            total[...] = part
        elif i < len(cuts) - 1:
            total[...] += part
        else:
            mean_sq = jnp.sum(squares, axis=1, keepdims=True) * (1.0 / width)
            scale = lax.rsqrt(mean_sq + EPS)
            out_ref[...] = ((total[...] + part) * scale + bias[...]).astype(BF16)
        start += depth


def project(hidden, gain, weight, bias):
    rows, width = hidden.shape
    cols = weight.shape[1]
    cuts = []
    for depth in (256, 256, 512, 1024, *[2048] * (width // 2048)):
        if sum(cuts) < width:
            cuts.append(min(depth, width - sum(cuts)))
    return pl.pallas_call(
        functools.partial(project_kernel, cuts),
        in_specs=[ANY] * 4,
        out_specs=VMEM,
        out_shape=jax.ShapeDtypeStruct((rows, cols), BF16),
        scratch_shapes=[
            pltpu.VMEM((rows, width), BF16),
            pltpu.VMEM((1, width), F32),
            pltpu.VMEM((width, cols), BF16),
            pltpu.VMEM((1, cols), F32),
            pltpu.VMEM((rows, cols), F32),
            pltpu.SemaphoreType.DMA((3, len(cuts))),
        ],
        compiler_params=params(40),
        cost_estimate=cost(2 * rows * width * cols, 2 * width * (rows + cols)),
        name="project",
    )(*map(in_hbm, (hidden, gain.reshape(1, -1), weight, bias.reshape(1, -1))))


def front_kernel(heads, count_ref, keys_ref, q_ref, to_keys_ref, to_q_ref):
    size = to_keys_ref.shape[0]
    places = size // heads
    part = keys_ref.shape[0] // places
    share = to_q_ref.shape[2]
    count = count_ref[0]
    high = lax.broadcasted_iota(jnp.int32, (EXTRA, HD), 0) < EXTRA // 2
    extra = jnp.where(high, count // 8, count % 8).astype(F32).astype(BF16)
    for device in range(size):
        head, place = divmod(device, places)
        to_keys_ref[device, :part] = keys_ref[
            place * part : (place + 1) * part, head * HD : (head + 1) * HD
        ]
        to_keys_ref[device, part:] = extra
        at = (2 * head + place % 2) * share
        to_q_ref[device] = q_ref[:, at : at + share]


def front(count, keys, queries, size):
    heads = keys.shape[1] // HD
    part = keys.shape[0] * heads // size
    return pl.pallas_call(
        functools.partial(front_kernel, heads),
        in_specs=[SMEM, VMEM, VMEM],
        out_specs=[VMEM, VMEM],
        out_shape=[
            jax.ShapeDtypeStruct((size, part + EXTRA, HD), BF16),
            jax.ShapeDtypeStruct((size, queries.shape[0], queries.shape[1] // heads // 2), BF16),
        ],
        compiler_params=params(16),
        cost_estimate=cost(0, 4 * keys.size + 6 * queries.size),
        name="front",
    )(count, in_hbm(keys), in_hbm(queries))


def counts_of(ref):
    extra = ref[...].astype(F32)
    return (extra[:, 0, :1] * 8.0 + extra[:, EXTRA // 2, :1]).astype(jnp.int32)


def pick_kernel(me_ref, counts_ref, keep_ref, rows_ref, out_ref):
    me = me_ref[0]
    counts = counts_of(counts_ref)
    size = counts.shape[0]
    before = lax.broadcasted_iota(jnp.int32, (size, 1), 0) < me
    start = jnp.sum(jnp.where(before, counts, 0), axis=0, keepdims=True)
    n = rows_ref.shape[0]
    cap = n // size
    slot = lax.broadcasted_iota(jnp.int32, (n, n), 0)
    entry = lax.broadcasted_iota(jnp.int32, (n, n), 1)
    wanted = ((slot // cap - start) & (size - 1)) + (slot & (cap - 1)) * size
    chooses = (wanted == entry).astype(F32).astype(BF16)
    listed = (keep_ref[...] == slot).astype(F32).astype(BF16)
    select = lax.dot_general(
        chooses, listed, (((1,), (1,)), ((), ())), preferred_element_type=F32
    ).astype(BF16)
    out_ref[...] = jnp.dot(select, rows_ref[...], preferred_element_type=F32).astype(BF16)


def counts_spec(blocks):
    size, rows, _ = blocks.shape
    return pl.BlockSpec((size, EXTRA, HD), lambda i: (0, rows // EXTRA - 1, 0))


def pick(me, blocks, keep_index, rows):
    n = rows.shape[0]
    return pl.pallas_call(
        pick_kernel,
        grid=(1,),
        in_specs=[SMEM, counts_spec(blocks), VMEM, VMEM],
        out_specs=VMEM,
        out_shape=jax.ShapeDtypeStruct(rows.shape, BF16),
        compiler_params=params(32),
        cost_estimate=cost(2 * n * n * (n + rows.shape[1]), 4 * rows.size),
        name="pick",
    )(me, blocks, keep_index.reshape(1, -1), rows)


def place_kernel(me_ref, counts_ref, rows_ref, out_ref):
    me = me_ref[0]
    counts = counts_of(counts_ref)
    size = counts.shape[0]
    keep, n = out_ref.shape[0], rows_ref.shape[0]
    cap = n // size
    slot = lax.broadcasted_iota(jnp.int32, (1, n), 1)
    source = slot // cap
    device = lax.broadcasted_iota(jnp.int32, (size, n), 0)
    starts = jnp.sum(jnp.where(device < source, counts, 0), axis=0, keepdims=True)
    here = jnp.sum(jnp.where(device == source, counts, 0), axis=0, keepdims=True)
    pos = ((me - starts) & (size - 1)) + (slot & (cap - 1)) * size
    target = jnp.where(pos < here, (starts + pos) // size, keep)
    row = lax.broadcasted_iota(jnp.int32, (keep, n), 0)
    select = (row == target).astype(F32).astype(BF16)
    out_ref[...] = jnp.dot(select, rows_ref[...], preferred_element_type=F32).astype(BF16)


def place(me, blocks, rows, keep):
    return pl.pallas_call(
        place_kernel,
        grid=(1,),
        in_specs=[SMEM, counts_spec(blocks), VMEM],
        out_specs=VMEM,
        out_shape=jax.ShapeDtypeStruct((keep, rows.shape[1]), BF16),
        compiler_params=params(32),
        cost_estimate=cost(2 * keep * rows.size, 3 * rows.size),
        name="place",
    )(me, blocks, rows)


def score_kernel(core, chunk, tile, me_ref, mine_ref, other_ref, blocks_ref, prob_ref, top_ref, lse_ref, q, keys):
    scale = HD**-0.5 * LOG2E
    size, part = blocks_ref.shape[0], blocks_ref.shape[1] - EXTRA
    for device in range(size):
        keys[device * part : (device + 1) * part, :] = blocks_ref[device, :part]

    @pl.when(me_ref[0] % 2 == core)
    def _():
        q[...] = mine_ref[...]

    @pl.when(me_ref[0] % 2 != core)
    def _():
        q[...] = other_ref[...]

    per = q.shape[0] // tile

    def step(i, _):
        rows = pl.ds(pl.multiple_of((i % per) * tile, tile), tile)
        head = pl.ds(pl.multiple_of((i // per) * HD, HD), HD)
        cols = pl.ds(pl.multiple_of(i * tile, tile), tile)
        query = q[rows, head]
        tops, sums = [], []
        for at in range(0, keys.shape[0], chunk):
            s = lax.dot_general(
                keys[at : at + chunk, :],
                query,
                (((1,), (1,)), ((), ())),
                preferred_element_type=F32,
            )
            top = jnp.max(s, axis=0, keepdims=True)
            p = jnp.exp2((s - top) * scale)
            sums.append(jnp.sum(p, axis=0, keepdims=True))
            tops.append(top * scale)
            prob_ref[at : at + chunk, cols] = p.astype(BF16)
        top_all = functools.reduce(jnp.maximum, tops)
        total = sum(part * jnp.exp2(top - top_all) for part, top in zip(sums, tops))
        for c, top in enumerate(tops):
            top_ref[c : c + 1, cols] = top
        lse_ref[:, cols] = top_all + jnp.log2(total)
        return 0

    lax.fori_loop(0, prob_ref.shape[1] // tile, step, 0)


def score(me, core, mine, other, blocks, chunk=256, tile=512):
    size, height, _ = blocks.shape
    keys = size * (height - EXTRA)
    tokens, width = mine.shape
    rows = tokens * width // HD
    tile = min(tile, tokens)
    return pl.pallas_call(
        functools.partial(score_kernel, core, chunk, tile),
        in_specs=[SMEM] + [VMEM] * 3,
        out_specs=[VMEM] * 3,
        out_shape=[
            pltpu.VMEM((keys, rows), BF16),
            pltpu.VMEM((keys // chunk, rows), F32),
            pltpu.VMEM((1, rows), F32),
        ],
        scratch_shapes=[pltpu.VMEM(mine.shape, BF16), pltpu.VMEM((keys, HD), BF16)],
        compiler_params=params(16),
        cost_estimate=cost(2 * rows * keys * HD, 2 * rows * keys, rows * keys),
        name="score",
    )(me, mine, other, blocks)


def weigh_kernel(factor, prob_ref, top_ref, lse_ref, *rest):
    others, out_ref = rest[:-1], rest[-1]
    mine = lse_ref[...]
    top = functools.reduce(jnp.maximum, [ref[...] for ref in others], mine)
    total = jnp.exp2(mine - top)
    for ref in others:
        total = total + jnp.exp2(ref[...] - top)
    lse = top + jnp.log2(total)
    weight = jnp.exp2(top_ref[...] - lse) * factor
    high = weight.astype(BF16).astype(F32)
    low = weight - high
    chunks, part = top_ref.shape[0], out_ref.shape[2]
    chunk = prob_ref.shape[0] // chunks
    for c in range(chunks):
        both = jnp.concatenate([high[c : c + 1], low[c : c + 1]], axis=0).astype(BF16)
        got = lax.dot_general(
            both,
            prob_ref[c * chunk : (c + 1) * chunk, :],
            (((1,), (1,)), ((), ())),
            preferred_element_type=F32,
        )
        got = jnp.sum(got, axis=0, keepdims=True)
        for at in range(0, chunk, part):
            out_ref[(c * chunk + at) // part] = got[:, at : at + part]


def weigh(prob, tops, lse, others, factor, part):
    keys, rows = prob.shape
    return pl.pallas_call(
        functools.partial(weigh_kernel, factor),
        in_specs=[VMEM] * (3 + len(others)),
        out_specs=VMEM,
        out_shape=jax.ShapeDtypeStruct((keys // part, 1, part), F32),
        compiler_params=params(16),
        cost_estimate=cost(4 * rows * keys, 2 * rows * keys),
        name="weigh",
    )(prob, tops, lse, *others)


def shards(queries, visual_keys, hidden, keep_count, keep_index, norm_gain, kv_weight, kv_bias):
    size = lax.axis_size("seq")
    me = lax.axis_index("seq").astype(jnp.int32).reshape(1)
    own_keys = visual_keys.shape[0]
    heads = visual_keys.shape[1] // HD
    places = size // heads
    part = own_keys // places

    def swap(x, r):
        return lax.ppermute(x, "seq", [(i, i ^ r) for i in range(size)])

    def exchange(x):
        return lax.all_to_all(x, "seq", split_axis=0, concat_axis=0, tiled=True)

    to_keys, to_q = front(keep_count, visual_keys, queries, size)
    blocks = exchange(to_keys)
    mine = exchange(to_q)
    mine = mine.reshape(-1, mine.shape[2])
    other = swap(mine, 1)

    projected = project(hidden, norm_gain, kv_weight, kv_bias)
    picked = pick(me, blocks, keep_index, projected)
    arrived = exchange(picked.reshape(size, own_keys // size, -1)).reshape(own_keys, -1)
    layer_kv = place(me, blocks, arrived, own_keys // 2)

    total_rows = mine.shape[0] * (queries.shape[1] // HD)
    factor = own_keys * size / total_rows
    partial = 0.0
    for core in range(2):
        prob, tops, lse = score(me, core, mine, other, blocks)
        others = [swap(lse, r) for r in range(1, places)]
        partial = partial + weigh(prob, tops, lse, others, factor, part)
    sums = exchange(partial)
    importance = jnp.sum(sums.reshape(heads, own_keys), axis=0)
    return (importance, layer_kv)


def solution(mesh):
    rows = P(("groups", "seq"), None)
    flat = P(("groups", "seq"))
    return jax.shard_map(
        shards,
        mesh=mesh,
        in_specs=(rows, rows, rows, flat, flat, P(), P(), P()),
        out_specs=(flat, rows),
        check_vma=False,
    )
```

time: 83.9 us -> 118 us (1.41); the launches traced: 83.5 us -> 116 us
  waiting for transfers between devices: 17.8 us -> 40.5 us
  blocking collectives: 0 us -> 21.6 us
  starting transfers between devices: 27.6 us -> 16.9 us
  local copies, waits for them, and re-layouts: 2.04 us -> 0.53 us
  other arithmetic: 0.59 us -> 1.88 us
    all_to_all x2 -> x3, waiting for transfers between devices: 0.01 us -> 40.5 us  [exchange(): return lax.all_to_all(x, 'seq', split_axis=0, concat_axis=0, tiled=True)]
    all_to_all x0 -> x1, blocking collectives: none -> 21.6 us  [exchange(): return lax.all_to_all(x, 'seq', split_axis=0, concat_axis=0, tiled=True)]
    ppermute x14 -> x7, waiting for transfers between devices: 17.8 us -> 0.02 us  [swap(): return lax.ppermute(x, 'seq', [(i, i ^ r) for i in range(size)])]
    ppermute x14 -> x7, starting transfers between devices: 15.4 us -> 4.28 us  [swap(): return lax.ppermute(x, 'seq', [(i, i ^ r) for i in range(size)])]
    unnamed x7 -> x2, local copies, waits for them, and re-layouts: 2 us -> 0.01 us
    pallas_call x7 -> x6, Pallas kernels: 29.4 us -> 28.7 us  [the longest x1 11.8 us: project(): pl.pallas_call(functools.partial(project_kernel, cuts), in_specs=[ANY] *...]
    all_to_all x2 -> x3, starting transfers between devices: 12.2 us -> 12.6 us  [exchange(): return lax.all_to_all(x, 'seq', split_axis=0, concat_axis=0, tiled=True)]
  transfers between devices with their start and end apart: 16 -> 10, of which waited for: 6 -> 3; matrix products, arithmetic and copies ran while one was open for 1% -> 2% of each run, Pallas kernels for 38% -> 19%
where the time goes in v4:
time: 118 us; the launch traced here: 116 us
  waiting for transfers between devices  40.5 us (34%)
  Pallas kernels  33.2 us (28%)
  blocking collectives  21.6 us (18%)
  starting transfers between devices  16.9 us (14%)
  other arithmetic  1.88 us (2%)
  between operations  1.41 us (1%)
    all_to_all x3, waiting for transfers between devices, exchange(): return lax.all_to_all(x, 'seq', split_axis=0, concat_axis=0, tiled=True)  40.5 us
    all_to_all x1, blocking collectives, exchange(): return lax.all_to_all(x, 'seq', split_axis=0, concat_axis=0, tiled=True)  21.6 us
    all_to_all x3, starting transfers between devices, exchange(): return lax.all_to_all(x, 'seq', split_axis=0, concat_axis=0, tiled=True)  12.6 us
    pallas_call x1, Pallas kernels, project(): pl.pallas_call(functools.partial(project_kernel, cuts), in_specs=[ANY] *...  11.8 us
    pallas_call x2, Pallas kernels, score(): pl.pallas_call(functools.partial(score_kernel, core, chunk, tile), in_spe...  11.5 us
    pallas_call x2, Pallas kernels, weigh(): pl.pallas_call(functools.partial(weigh_kernel, factor), in_specs=[VMEM] *...  4.54 us
    ppermute x7, starting transfers between devices, swap(): return lax.ppermute(x, 'seq', [(i, i ^ r) for i in range(size)])  4.28 us
  transfers between devices with their start and end apart: 10, of which 3 were waited for; matrix products, arithmetic and copies ran while one was open for 2% of the time, Pallas kernels for 19%

profile of v4, /device:TPU:0, one launch (start us, length us, event | category | flops | bytes accessed | tf_op | source)
XLA Modules:
  0.0 116.1 jit_solution(17651352478548610952)
XLA Ops:
  1.3 2.0 %front.1 = (bf16[16,144,128]{2,1,0:T(8,128)(2,1)}, bf16[16,32,512]{2,1,0:T(8,128)(2,1)S(1)}) custom-call(s32[1]{0:T(128)S(6)} %copy.10.count_ref, bf16[512,512]{1,0:T(8,128)(2,1)} %keys_ref.1, bf16[32,4096]{1,0:T(8,128)(2,1)} %q_ref.1), custom_call_target="tpu_custom_call" | custom-call | bytes 1835008 | tf_op jit(solution)/shard_map/front/pallas_call | solution.py:124
  3.3 21.6 %all_to_all.20 = bf16[16,32,512]{2,1,0:T(8,128)(2,1)S(1)} all-to-all(bf16[16,32,512]{2,1,0:T(8,128)(2,1)S(1)} %get-tuple-element.10), channel_id=1, replica_groups=mesh['groups'=2,'seq'=16] {'seq'}, dimensions={0} | all-to-all | bytes 1048576 | tf_op jit(solution)/shard_map/all_to_all | solution.py:329
  24.9 4.1 %all-to-all-start.1 = ((bf16[16,144,128]{2,1,0:T(8,128)(2,1)}), bf16[16,144,128]{2,1,0:T(8,128)(2,1)S(1)}, u32[]{:S(2)}, u32[]{:S(2)}) async-start(bf16[16,144,128]{2,1,0:T(8,128)(2,1)} %get-tuple-element.11), calls=%async_computation.1 | async-start | bytes 1179648 | tf_op jit(solution)/shard_map/all_to_all | solution.py:329
  29.0 0.4 collective-permute-start
  29.5 15.1 %all-to-all-done.1.blocks_ref.counts_ref = bf16[16,144,128]{2,1,0:T(8,128)(2,1)S(1)} async-done(((bf16[16,144,128]{2,1,0:T(8,128)(2,1)}), bf16[16,144,128]{2,1,0:T(8,128)(2,1)S(1)}, u32[]{:S(2)}, u32[]{:S(2)}) %all-to-all-start.1) | async-done | bytes 589856 | tf_op jit(solution)/shard_map/all_to_all | solution.py:329
  44.6 0.0 collective-permute-done.other_ref
  44.6 5.7 %score.2 = (bf16[2048,2048]{1,0:T(8,128)(2,1)S(1)}, f32[8,2048]{1,0:T(8,128)S(1)}, f32[1,2048]{1,0:T(1,128)S(1)}) custom-call(s32[1]{0:T(128)} %bitcast.me_ref, bf16[512,512]{1,0:T(8,128)(2,1)S(1)} %bitcast.9, bf16[512,512]{1,0:T(8,128)(2,1)S(1)} %collective-permute-done.other_ref, bf16[16,144,128]{2,1,0:T(8,128)(2,1)S(1)} %all-to-all-done.1.blocks_ref.counts_ref), custom_call_target="tpu_custom_call" | custom-call | flops 1073741824 | bytes 8388608 | tf_op jit(solution)/shard_map/score/pallas_call | solution.py:262
  50.2 0.1 collective-permute-start.1
  50.3 1.3 %collective-permute-start.2 = (f32[1,2048]{1,0:T(1,128)S(1)}, f32[1,2048]{1,0:T(1,128)S(1)}, u32[]{:S(2)}, u32[]{:S(2)}) collective-permute-start(f32[1,2048]{1,0:T(1,128)S(1)} %get-tuple-element.14.lse_ref), channel_id=1, source_target_pairs={{0,2},{1,3},{2,0},{3,1},{4,6},{5,7},{6,4},{7,5},{8,10},{9,11},{10,... | collective-permute-start | bytes 24584 | tf_op jit(solution)/shard_map/ppermute | solution.py:326
  51.7 0.5 collective-permute-start.3
  52.2 5.8 %score.3 = (bf16[2048,2048]{1,0:T(8,128)(2,1)S(1)}, f32[8,2048]{1,0:T(8,128)S(1)}, f32[1,2048]{1,0:T(1,128)S(1)}) custom-call(s32[1]{0:T(128)} %bitcast.me_ref, bf16[512,512]{1,0:T(8,128)(2,1)S(1)} %bitcast.10, bf16[512,512]{1,0:T(8,128)(2,1)S(1)} %collective-permute-done.other_ref, bf16[16,144,128]{2,1,0:T(8,128)(2,1)S(1)} %all-to-all-done.1.blocks_ref.counts_ref), custom_call_target="tpu_custom_call" | custom-call | flops 1073741824 | bytes 8388608 | tf_op jit(solution)/shard_map/score/pallas_call | solution.py:262
  58.0 0.4 collective-permute-start.4
  58.4 1.3 %collective-permute-start.5 = (f32[1,2048]{1,0:T(1,128)S(1)}, f32[1,2048]{1,0:T(1,128)S(1)}, u32[]{:S(2)}, u32[]{:S(2)}) collective-permute-start(f32[1,2048]{1,0:T(1,128)S(1)} %get-tuple-element.17.lse_ref), channel_id=1, source_target_pairs={{0,2},{1,3},{2,0},{3,1},{4,6},{5,7},{6,4},{7,5},{8,10},{9,11},{10,... | collective-permute-start | bytes 24584 | tf_op jit(solution)/shard_map/ppermute | solution.py:326
  59.7 0.0 collective-permute-done.1.rest_0_
  59.7 0.2 collective-permute-start.6
  59.9 11.8 %project.1.rows_ref = bf16[512,1024]{1,0:T(8,128)(2,1)S(1)} custom-call(bf16[512,8192]{1,0:T(8,128)(2,1)} %x_hbm.1, f32[1,8192]{1,0:T(1,128)} %bitcast.12, bf16[8192,1024]{1,0:T(8,128)(2,1)} %weight_hbm.1, f32[1,1024]{1,0:T(1,128)} %bitcast.13), custom_call_target="tpu_custom_call" | custom-call | flops 8589934592 | bytes 25165824 | tf_op jit(solution)/shard_map/project/pallas_call | solution.py:84
  71.7 0.0 collective-permute-done.2.rest_1_
  71.7 0.0 collective-permute-done.3.rest_2_
  71.7 0.0 copy-start
  71.8 2.3 %weigh.2 = f32[16,1,128]{2,1,0:T(1,128)S(1)} custom-call(bf16[2048,2048]{1,0:T(8,128)(2,1)S(1)} %get-tuple-element.12.prob_ref, f32[8,2048]{1,0:T(8,128)S(1)} %get-tuple-element.13.top_ref, f32[1,2048]{1,0:T(1,128)S(1)} %get-tuple-element.14.lse_ref, f32[1,2048]{1,0:T(1,128)S(1)} %collective-permute-done.1.rest_0_, ...), custom_call_target="tpu_custom_call" | custom-call | flops 16777216 | bytes 8388608 | tf_op jit(solution)/shard_map/weigh/pallas_call | solution.py:306
  74.0 0.0 collective-permute-done.4.rest_0_
  74.1 0.0 collective-permute-done.5.rest_1_
  74.1 0.0 collective-permute-done.6.rest_2_
  74.1 2.3 %weigh.3 = f32[16,1,128]{2,1,0:T(1,128)S(1)} custom-call(bf16[2048,2048]{1,0:T(8,128)(2,1)S(1)} %get-tuple-element.15.prob_ref, f32[8,2048]{1,0:T(8,128)S(1)} %get-tuple-element.16.top_ref, f32[1,2048]{1,0:T(1,128)S(1)} %get-tuple-element.17.lse_ref, f32[1,2048]{1,0:T(1,128)S(1)} %collective-permute-done.4.rest_0_, ...), custom_call_target="tpu_custom_call" | custom-call | flops 16777216 | bytes 8388608 | tf_op jit(solution)/shard_map/weigh/pallas_call | solution.py:306
  76.4 0.6 add.3
  77.0 4.8 %all-to-all-start.2 = ((f32[16,1,128]{2,1,0:T(1,128)}), f32[16,1,128]{2,1,0:T(1,128)S(1)}, u32[]{:S(2)}, u32[]{:S(2)}) async-start(f32[16,1,128]{2,1,0:T(1,128)} %add.3), calls=%async_computation.2 | async-start | bytes 16384 | tf_op jit(solution)/shard_map/all_to_all | solution.py:329
  81.8 0.0 copy-done
  81.8 2.1 %pick.1 = bf16[512,1024]{1,0:T(8,128)(2,1)} custom-call(s32[1]{0:T(128)} %bitcast.me_ref, bf16[16,144,128]{2,1,0:T(8,128)(2,1)S(1)} %all-to-all-done.1.blocks_ref.counts_ref, s32[1,512]{1,0:T(1,128)S(1)} %bitcast.11, bf16[512,1024]{1,0:T(8,128)(2,1)S(1)} %project.1.rows_ref), custom_call_target="tpu_custom_call" | custom-call | flops 805306368 | bytes 2097152 | tf_op jit(solution)/shard_map/pick/pallas_call | solution.py:169
  83.9 4.2 %all-to-all-done.2 = f32[16,1,128]{2,1,0:T(1,128)S(1)} async-done(((f32[16,1,128]{2,1,0:T(1,128)}), f32[16,1,128]{2,1,0:T(1,128)S(1)}, u32[]{:S(2)}, u32[]{:S(2)}) %all-to-all-start.2) | async-done | bytes 8224 | tf_op jit(solution)/shard_map/all_to_all | solution.py:329
  88.2 3.7 %all-to-all-start.3 = ((bf16[16,32,1024]{2,1,0:T(8,128)(2,1)}), bf16[16,32,1024]{2,1,0:T(8,128)(2,1)S(1)}, u32[]{:S(2)}, u32[]{:S(2)}) async-start(bf16[16,32,1024]{2,1,0:T(8,128)(2,1)} %bitcast.5), calls=%async_computation.3 | async-start | bytes 2097152 | tf_op jit(solution)/shard_map/all_to_all | solution.py:329
  91.8 0.5 broadcast.3
  92.3 0.7 reduce.3
  93.0 0.6 reduce_sum.9
  93.6 21.1 %all-to-all-done.3 = bf16[16,32,1024]{2,1,0:T(8,128)(2,1)S(1)} async-done(((bf16[16,32,1024]{2,1,0:T(8,128)(2,1)}), bf16[16,32,1024]{2,1,0:T(8,128)(2,1)S(1)}, u32[]{:S(2)}, u32[]{:S(2)}) %all-to-all-start.3) | async-done | bytes 1048608 | tf_op jit(solution)/shard_map/all_to_all | solution.py:329
  114.7 1.3 %place.1 = bf16[256,1024]{1,0:T(8,128)(2,1)} custom-call(s32[1]{0:T(128)} %bitcast.me_ref, bf16[16,144,128]{2,1,0:T(8,128)(2,1)S(1)} %all-to-all-done.1.blocks_ref.counts_ref, bf16[512,1024]{1,0:T(8,128)(2,1)S(1)} %bitcast.7), custom_call_target="tpu_custom_call" | custom-call | flops 268435456 | bytes 1572864 | tf_op jit(solution)/shard_map/place/pallas_call | solution.py:200
  (1 shorter events, 0.0 us)
Async XLA Ops:
  24.9 19.7 %all-to-all-start.1 = ((bf16[16,144,128]{2,1,0:T(8,128)(2,1)}), bf16[16,144,128]{2,1,0:T(8,128)(2,1)S(1)}, u32[]{:S(2)}, u32[]{:S(2)}) async-start(bf16[16,144,128]{2,1,0:T(8,128)(2,1)} %get-tuple-element.11), calls=%async_computation.1 | async-start | bytes 1179648 | tf_op jit(solution)/shard_map/all_to_all | solution.py:329
  29.0 15.6 %collective-permute-start = (bf16[512,512]{1,0:T(8,128)(2,1)S(1)}, bf16[512,512]{1,0:T(8,128)(2,1)S(1)}, u32[]{:S(2)}, u32[]{:S(2)}) collective-permute-start(bf16[512,512]{1,0:T(8,128)(2,1)S(1)} %bitcast.8), channel_id=1, source_target_pairs={{0,1},{1,0},{2,3},{3,2},{4,5},{5,4},{6,7},{7,6},{8,9},{9,8},{10,11... | collective-permute-start | bytes 1572872 | tf_op jit(solution)/shard_map/ppermute | solution.py:326
  50.2 9.5 %collective-permute-start.1 = (f32[1,2048]{1,0:T(1,128)S(1)}, f32[1,2048]{1,0:T(1,128)S(1)}, u32[]{:S(2)}, u32[]{:S(2)}) collective-permute-start(f32[1,2048]{1,0:T(1,128)S(1)} %get-tuple-element.14.lse_ref), channel_id=1, source_target_pairs={{0,1},{1,0},{2,3},{3,2},{4,5},{5,4},{6,7},{7,6},{8,9},{9,8},{10,11... | collective-permute-start | bytes 24584 | tf_op jit(solution)/shard_map/ppermute | solution.py:326
  50.3 21.4 %collective-permute-start.2 = (f32[1,2048]{1,0:T(1,128)S(1)}, f32[1,2048]{1,0:T(1,128)S(1)}, u32[]{:S(2)}, u32[]{:S(2)}) collective-permute-start(f32[1,2048]{1,0:T(1,128)S(1)} %get-tuple-element.14.lse_ref), channel_id=1, source_target_pairs={{0,2},{1,3},{2,0},{3,1},{4,6},{5,7},{6,4},{7,5},{8,10},{9,11},{10,... | collective-permute-start | bytes 24584 | tf_op jit(solution)/shard_map/ppermute | solution.py:326
  51.7 20.1 %collective-permute-start.3 = (f32[1,2048]{1,0:T(1,128)S(1)}, f32[1,2048]{1,0:T(1,128)S(1)}, u32[]{:S(2)}, u32[]{:S(2)}) collective-permute-start(f32[1,2048]{1,0:T(1,128)S(1)} %get-tuple-element.14.lse_ref), channel_id=1, source_target_pairs={{0,3},{1,2},{2,1},{3,0},{4,7},{5,6},{6,5},{7,4},{8,11},{9,10},{10,... | collective-permute-start | bytes 24584 | tf_op jit(solution)/shard_map/ppermute | solution.py:326
  58.0 16.0 %collective-permute-start.4 = (f32[1,2048]{1,0:T(1,128)S(1)}, f32[1,2048]{1,0:T(1,128)S(1)}, u32[]{:S(2)}, u32[]{:S(2)}) collective-permute-start(f32[1,2048]{1,0:T(1,128)S(1)} %get-tuple-element.17.lse_ref), channel_id=1, source_target_pairs={{0,1},{1,0},{2,3},{3,2},{4,5},{5,4},{6,7},{7,6},{8,9},{9,8},{10,11... | collective-permute-start | bytes 24584 | tf_op jit(solution)/shard_map/ppermute | solution.py:326
  58.4 15.6 %collective-permute-start.5 = (f32[1,2048]{1,0:T(1,128)S(1)}, f32[1,2048]{1,0:T(1,128)S(1)}, u32[]{:S(2)}, u32[]{:S(2)}) collective-permute-start(f32[1,2048]{1,0:T(1,128)S(1)} %get-tuple-element.17.lse_ref), channel_id=1, source_target_pairs={{0,2},{1,3},{2,0},{3,1},{4,6},{5,7},{6,4},{7,5},{8,10},{9,11},{10,... | collective-permute-start | bytes 24584 | tf_op jit(solution)/shard_map/ppermute | solution.py:326
  59.7 14.4 %collective-permute-start.6 = (f32[1,2048]{1,0:T(1,128)S(1)}, f32[1,2048]{1,0:T(1,128)S(1)}, u32[]{:S(2)}, u32[]{:S(2)}) collective-permute-start(f32[1,2048]{1,0:T(1,128)S(1)} %get-tuple-element.17.lse_ref), channel_id=1, source_target_pairs={{0,3},{1,2},{2,1},{3,0},{4,7},{5,6},{6,5},{7,4},{8,11},{9,10},{10,... | collective-permute-start | bytes 24584 | tf_op jit(solution)/shard_map/ppermute | solution.py:326
  71.7 10.1 %copy-start = (s32[512]{0:T(512)S(1)}, s32[512]{0:T(512)}, u32[]{:S(2)}) copy-start(s32[512]{0:T(512)} %param.12) | copy-start | bytes 6148
  77.0 11.2 %all-to-all-start.2 = ((f32[16,1,128]{2,1,0:T(1,128)}), f32[16,1,128]{2,1,0:T(1,128)S(1)}, u32[]{:S(2)}, u32[]{:S(2)}) async-start(f32[16,1,128]{2,1,0:T(1,128)} %add.3), calls=%async_computation.2 | async-start | bytes 16384 | tf_op jit(solution)/shard_map/all_to_all | solution.py:329
  88.2 26.6 %all-to-all-start.3 = ((bf16[16,32,1024]{2,1,0:T(8,128)(2,1)}), bf16[16,32,1024]{2,1,0:T(8,128)(2,1)S(1)}, u32[]{:S(2)}, u32[]{:S(2)}) async-start(bf16[16,32,1024]{2,1,0:T(8,128)(2,1)} %bitcast.5), calls=%async_computation.3 | async-start | bytes 2097152 | tf_op jit(solution)/shard_map/all_to_all | solution.py:329

commit v5 on v3

v5 whole, which is shorter than its diff:
```python
import functools

import jax
import jax.numpy as jnp
from jax import lax
from jax.experimental import pallas as pl
from jax.experimental.pallas import tpu as pltpu
from jax.sharding import PartitionSpec as P

HD = 128
CHIPS = 4
CELL = 2 * CHIPS
EPS = 1e-06
F32 = jnp.float32
BF16 = jnp.bfloat16
LOG2E = 1.4426950408889634
MIB = 1024 * 1024


def params(mib):
    return pltpu.CompilerParams(vmem_limit_bytes=mib * MIB)


def cost(flops, bytes_accessed, transcendentals=0):
    return pl.CostEstimate(
        flops=int(flops), bytes_accessed=int(bytes_accessed), transcendentals=int(transcendentals)
    )


def in_hbm(x):
    return pltpu.with_memory_space_constraint(x, pltpu.HBM)


SMEM = pl.BlockSpec(memory_space=pltpu.SMEM)
VMEM = pl.BlockSpec(memory_space=pltpu.VMEM)
ANY = pl.BlockSpec(memory_space=pl.ANY)
EXTRA = 16


def project_kernel(cuts, x_hbm, gain_hbm, weight_hbm, bias_hbm, out_ref, x, gain, weight, bias, total, sems):
    copies = []
    start = 0
    for i, depth in enumerate(cuts):
        at = pl.ds(start, depth)
        copies.append(
            [
                pltpu.make_async_copy(x_hbm.at[:, at], x.at[:, at], sems.at[0, i]),
                pltpu.make_async_copy(weight_hbm.at[at, :], weight.at[at, :], sems.at[1, i]),
            ]
        )
        start += depth
    copies[0].append(pltpu.make_async_copy(gain_hbm, gain, sems.at[2, 0]))
    copies[-1].append(pltpu.make_async_copy(bias_hbm, bias, sems.at[2, 1]))
    for group in copies:
        for copy in group:
            copy.start()
    width = x.shape[1]
    start = 0
    squares = None
    for i, depth in enumerate(cuts):
        for copy in copies[i]:
            copy.wait()
        values = x[:, start : start + depth].astype(F32)
        scaled = (values * gain[:, start : start + depth]).astype(BF16)
        part = jnp.dot(scaled, weight[start : start + depth, :], preferred_element_type=F32)
        square = values * values
        for col in range(0, depth, 128):
            lanes = square[:, col : col + 128]
            squares = lanes if squares is None else squares + lanes
        if i == 0:
            total[...] = part
        elif i < len(cuts) - 1:
            total[...] += part
        else:
            mean_sq = jnp.sum(squares, axis=1, keepdims=True) * (1.0 / width)
            scale = lax.rsqrt(mean_sq + EPS)
            out_ref[...] = ((total[...] + part) * scale + bias[...]).astype(BF16)
        start += depth


def project(hidden, gain, weight, bias):
    rows, width = hidden.shape
    cols = weight.shape[1]
    cuts = []
    for depth in (256, 256, 512, 1024, *[2048] * (width // 2048)):
        if sum(cuts) < width:
            cuts.append(min(depth, width - sum(cuts)))
    return pl.pallas_call(
        functools.partial(project_kernel, cuts),
        in_specs=[ANY] * 4,
        out_specs=VMEM,
        out_shape=jax.ShapeDtypeStruct((rows, cols), BF16),
        scratch_shapes=[
            pltpu.VMEM((rows, width), BF16),
            pltpu.VMEM((1, width), F32),
            pltpu.VMEM((width, cols), BF16),
            pltpu.VMEM((1, cols), F32),
            pltpu.VMEM((rows, cols), F32),
            pltpu.SemaphoreType.DMA((3, len(cuts))),
        ],
        compiler_params=params(40),
        cost_estimate=cost(2 * rows * width * cols, 2 * width * (rows + cols)),
        name="project",
    )(*map(in_hbm, (hidden, gain.reshape(1, -1), weight, bias.reshape(1, -1))))


def cell_steps(size):
    return [chip * (size // CHIPS) + core for chip in range(CHIPS) for core in range(2)]


def cross_steps(size):
    return list(range(0, size // CHIPS, 2))


def front_kernel(cells, stride, keys, me_ref, *refs):
    count_refs, (keys_ref, q_ref), out_refs = refs[:cells], refs[cells : cells + 2], refs[cells + 2 :]
    me = me_ref[0]
    tokens = q_ref.shape[0]
    heads = q_ref.shape[1] // HD // CHIPS
    lane = lax.broadcasted_iota(jnp.int32, (EXTRA, 128), 1)
    high = lax.broadcasted_iota(jnp.int32, (EXTRA, 128), 0) < EXTRA // 2
    extra = jnp.zeros((EXTRA, 128), jnp.int32)
    for c in range(cells):
        count = count_refs[c][0]
        extra = jnp.where(lane == c, jnp.where(high, count // 8, count % 8), extra)
    extra = extra.astype(F32).astype(BF16)
    first = (1 - me % 2) * (heads // 2)
    for i, out_ref in enumerate(out_refs):
        head = (me ^ (stride * i)) // stride
        out_ref[:keys, :] = keys_ref[:, pl.ds(pl.multiple_of(head * HD, HD), HD)]
        out_ref[keys : keys + EXTRA, :] = extra
        for h in range(heads):
            q_head = head * heads + (first + h) % heads
            at = keys + EXTRA + h * tokens
            out_ref[at : at + tokens, :] = q_ref[:, pl.ds(pl.multiple_of(q_head * HD, HD), HD)]


def front(me, counts, keys, queries, size):
    rows = keys.shape[0] + EXTRA + queries.size // HD // CHIPS
    return pl.pallas_call(
        functools.partial(front_kernel, len(counts), size // CHIPS, keys.shape[0]),
        in_specs=[SMEM] * (1 + len(counts)) + [VMEM] * 2,
        out_specs=[VMEM] * CHIPS,
        out_shape=[jax.ShapeDtypeStruct((rows, HD), BF16)] * CHIPS,
        compiler_params=params(16),
        cost_estimate=cost(0, 4 * keys.size + 4 * queries.size),
        name="front",
    )(me, *counts, in_hbm(keys), in_hbm(queries))


def collect_kernel(*refs):
    block_refs, out_ref = refs[:CELL], refs[CELL]
    rows = out_ref.shape[0] // CELL
    for i, ref in enumerate(block_refs):
        at = ref.shape[0] - rows * (2 if i % 2 else 1)
        out_ref[i * rows : (i + 1) * rows, :] = ref[at : at + rows, :]


def collect(blocks, keys):
    rows = (blocks[0].shape[0] - keys - EXTRA) // 2
    return pl.pallas_call(
        collect_kernel,
        in_specs=[VMEM] * CELL,
        out_specs=VMEM,
        out_shape=jax.ShapeDtypeStruct((CELL * rows, HD), BF16),
        compiler_params=params(16),
        cost_estimate=cost(0, 4 * CELL * rows * HD),
        name="collect",
    )(*blocks)


def counts_of(me, refs, size, keys):
    pairs = []
    for r, ref in zip(cell_steps(size), refs):
        extra = ref[keys : keys + EXTRA, :].astype(F32)
        count = (extra[:1] * 8.0 + extra[EXTRA // 2 : EXTRA // 2 + 1]).astype(jnp.int32)
        for c, cross in enumerate(cross_steps(size)):
            pairs.append((me ^ r ^ cross, count[:, c : c + 1]))
    return pairs


def pick_kernel(size, me_ref, *refs):
    count_refs, (keep_ref, rows_ref, out_ref) = refs[:CELL], refs[CELL:]
    me = me_ref[0]
    n = rows_ref.shape[0]
    start = jnp.zeros((1, 1), jnp.int32)
    for device, count in counts_of(me, count_refs, size, n):
        start += jnp.where(device < me, count, 0)
    cap = n // size
    slot = lax.broadcasted_iota(jnp.int32, (n, n), 0)
    entry = lax.broadcasted_iota(jnp.int32, (n, n), 1)
    wanted = ((slot // cap - start) & (size - 1)) + (slot & (cap - 1)) * size
    chooses = (wanted == entry).astype(F32).astype(BF16)
    listed = (keep_ref[...] == slot).astype(F32).astype(BF16)
    select = lax.dot_general(
        chooses, listed, (((1,), (1,)), ((), ())), preferred_element_type=F32
    ).astype(BF16)
    out_ref[...] = jnp.dot(select, rows_ref[...], preferred_element_type=F32).astype(BF16)


def pick(me, blocks, keep_index, rows, size):
    n = rows.shape[0]
    return pl.pallas_call(
        functools.partial(pick_kernel, size),
        in_specs=[SMEM] + [VMEM] * (CELL + 2),
        out_specs=VMEM,
        out_shape=jax.ShapeDtypeStruct(rows.shape, BF16),
        compiler_params=params(32),
        cost_estimate=cost(2 * n * n * (n + rows.shape[1]), 4 * rows.size),
        name="pick",
    )(me, *blocks, keep_index.reshape(1, -1), rows)


def place_kernel(size, me_ref, *refs):
    count_refs, (rows_ref, out_ref) = refs[:CELL], refs[CELL:]
    me = me_ref[0]
    keep, n = out_ref.shape[0], rows_ref.shape[0]
    cap = n // size
    slot = lax.broadcasted_iota(jnp.int32, (1, n), 1)
    source = slot // cap
    starts = jnp.zeros((1, n), jnp.int32)
    counts = jnp.zeros((1, n), jnp.int32)
    for device, count in counts_of(me, count_refs, size, n):
        starts += jnp.where(source > device, count, 0)
        counts = jnp.where(source == device, count, counts)
    pos = ((me - starts) & (size - 1)) + (slot & (cap - 1)) * size
    target = jnp.where(pos < counts, (starts + pos) // size, keep)
    row = lax.broadcasted_iota(jnp.int32, (keep, n), 0)
    select = (row == target).astype(F32).astype(BF16)
    out_ref[...] = jnp.dot(select, rows_ref[...], preferred_element_type=F32).astype(BF16)


def place(me, blocks, rows, keep, size):
    return pl.pallas_call(
        functools.partial(place_kernel, size),
        in_specs=[SMEM] + [VMEM] * (CELL + 1),
        out_specs=VMEM,
        out_shape=jax.ShapeDtypeStruct((keep, rows.shape[1]), BF16),
        compiler_params=params(32),
        cost_estimate=cost(2 * keep * rows.size, 3 * rows.size),
        name="place",
    )(me, *blocks, rows)


def score_kernel(keys, chunk, tile, q_ref, *refs):
    key_refs, (_, prob_ref, top_ref, lse_ref) = refs[:CELL], refs[CELL:]
    scale = HD**-0.5 * LOG2E

    def step(i, _):
        cols = pl.ds(pl.multiple_of(i * tile, tile), tile)
        query = q_ref[cols, :]
        tops, sums = [], []
        for c in range(CELL * keys // chunk):
            block, at = divmod(c * chunk, keys)
            s = lax.dot_general(
                key_refs[block][at : at + chunk, :],
                query,
                (((1,), (1,)), ((), ())),
                preferred_element_type=F32,
            )
            top = jnp.max(s, axis=0, keepdims=True)
            p = jnp.exp2((s - top) * scale)
            sums.append(jnp.sum(p, axis=0, keepdims=True))
            tops.append(top * scale)
            prob_ref[c * chunk : (c + 1) * chunk, cols] = p.astype(BF16)
        top_all = functools.reduce(jnp.maximum, tops)
        total = sum(part * jnp.exp2(top - top_all) for part, top in zip(sums, tops))
        for c, top in enumerate(tops):
            top_ref[c : c + 1, cols] = top
        lse_ref[:, cols] = top_all + jnp.log2(total)
        return 0

    lax.fori_loop(0, prob_ref.shape[1] // tile, step, 0)


def score(q, blocks, keys, after, chunk=256, tile=512):
    rows = q.shape[0]
    tile = min(tile, rows)
    return pl.pallas_call(
        functools.partial(score_kernel, keys, chunk, tile),
        in_specs=[VMEM] * (1 + CELL) + [ANY],
        out_specs=[VMEM] * 3,
        out_shape=[
            pltpu.VMEM((CELL * keys, rows), BF16),
            pltpu.VMEM((CELL * keys // chunk, rows), F32),
            pltpu.VMEM((1, rows), F32),
        ],
        compiler_params=params(16),
        cost_estimate=cost(8 * 2 * rows * CELL * keys * HD, 2 * rows * CELL * keys, rows * CELL * keys),
        name="score",
    )(q, *blocks, after)


def weigh_kernel(factor, cells, prob_ref, top_ref, lse_ref, *rest):
    others, earlier, out_ref = rest[: cells - 1], rest[cells - 1 : -1], rest[-1]
    mine = lse_ref[...]
    top = functools.reduce(jnp.maximum, [ref[...] for ref in others], mine)
    total = jnp.exp2(mine - top)
    for ref in others:
        total = total + jnp.exp2(ref[...] - top)
    lse = top + jnp.log2(total)
    weight = jnp.exp2(top_ref[...] - lse) * factor
    high = weight.astype(BF16).astype(F32)
    low = weight - high
    chunk = out_ref.shape[1]
    for c in range(out_ref.shape[0]):
        both = jnp.concatenate([high[c : c + 1], low[c : c + 1]], axis=0).astype(BF16)
        got = lax.dot_general(
            both,
            prob_ref[c * chunk : (c + 1) * chunk, :],
            (((1,), (1,)), ((), ())),
            preferred_element_type=F32,
        )
        got = jnp.sum(got, axis=0, keepdims=True)
        out_ref[c : c + 1, :] = sum([ref[c : c + 1, :] for ref in earlier], got)


def weigh(prob, tops, lse, others, factor, earlier):
    keys, rows = prob.shape
    earlier = [] if earlier is None else [earlier]
    chunks = tops.shape[0]
    return pl.pallas_call(
        functools.partial(weigh_kernel, factor, 1 + len(others)),
        in_specs=[VMEM] * (3 + len(others) + len(earlier)),
        out_specs=VMEM,
        out_shape=jax.ShapeDtypeStruct((chunks, keys // chunks), F32),
        compiler_params=params(16),
        cost_estimate=cost(4 * rows * keys, 2 * rows * keys),
        name="weigh",
    )(prob, tops, lse, *others, *earlier)


def finish_kernel(*refs):
    parts, (_, out_ref) = refs[:CHIPS], refs[CHIPS:]
    out_ref[...] = sum([ref[...] for ref in parts[1:]], parts[0][...])


def finish(parts, after):
    keys = parts[0].shape[0]
    row = (1, keys)
    return pl.pallas_call(
        finish_kernel,
        in_specs=[VMEM] * CHIPS + [ANY],
        out_specs=VMEM,
        out_shape=jax.ShapeDtypeStruct(row, F32),
        compiler_params=params(16),
        cost_estimate=cost(CHIPS * keys, 4 * CHIPS * keys),
        name="finish",
    )(*[part.reshape(row) for part in parts], after).reshape(keys)


def shards(queries, visual_keys, hidden, keep_count, keep_index, norm_gain, kv_weight, kv_bias):
    size = lax.axis_size("seq")
    me = lax.axis_index("seq").astype(jnp.int32).reshape(1)
    own_keys = visual_keys.shape[0]

    def swap(x, r):
        return lax.ppermute(x, "seq", [(i, i ^ r) for i in range(size)])

    steps = cross_steps(size)
    counts = [keep_count] + [swap(keep_count, r) for r in steps[1:]]

    far = [chip * (size // CHIPS) for chip in range(1, CHIPS)]
    evens = front(me, counts, visual_keys, queries, size)
    evens = [evens[0]] + [swap(block, r) for block, r in zip(evens[1:], far)]

    projected = project(hidden, norm_gain, kv_weight, kv_bias)
    *evens, projected = lax.optimization_barrier((*evens, projected))
    odds = [swap(block, 1) for block in evens]
    blocks = [block for pair in zip(evens, odds) for block in pair]

    my_q = collect(blocks, own_keys)
    all_q = [my_q] + [swap(my_q, r) for r in steps[1:]]

    picked = pick(me, blocks, keep_index, projected, size)
    arrived = lax.all_to_all(
        picked.reshape(size, own_keys // size, -1), "seq", split_axis=0, concat_axis=0, tiled=True
    ).reshape(own_keys, -1)
    layer_kv = place(me, blocks, arrived, own_keys // 2, size)

    total_rows = size * queries.shape[0] * (queries.shape[1] // HD)
    factor = own_keys * size / total_rows
    parts = {}
    after = picked
    for r, q in reversed([*zip(steps, all_q)]):
        parts[r] = score(q, blocks, own_keys, after)
        after = parts[r][2]
    partial = None
    for r in steps:
        prob, tops, lse = parts[r]
        others = [swap(parts[r ^ step][2], step) for step in steps[1:]]
        partial = weigh(prob, tops, lse, others, factor, partial)
    partial = partial.reshape(CHIPS, 2, own_keys)
    chips = partial[:, 0] + swap(partial[:, 1], 1)
    parts = [chips[0]] + [swap(chip, r) for chip, r in zip(chips[1:], far)]
    return (finish(parts, layer_kv), layer_kv)


def solution(mesh):
    rows = P(("groups", "seq"), None)
    flat = P(("groups", "seq"))
    return jax.shard_map(
        shards,
        mesh=mesh,
        in_specs=(rows, rows, rows, flat, flat, P(), P(), P()),
        out_specs=(flat, rows),
        check_vma=False,
    )
```

time: 74.5 us -> 67.3 us (0.903)
  starting transfers between devices: 26.8 us -> 22.2 us
  Pallas kernels: 34 us -> 32.7 us
  local copies, waits for them, and re-layouts: 2.04 us -> 1.09 us
    all_to_all x1 -> x0, starting transfers between devices: 6.16 us -> none  [shards(): lax.all_to_all(spread(queries, size), 'seq', split_axis=0, concat_axis=0,...]
    ppermute x14 -> x15, starting transfers between devices: 15.5 us -> 17 us  [swap(): return lax.ppermute(x, 'seq', [(i, i ^ r) for i in range(size)])]
    pallas_call x9 -> x10, Pallas kernels: 34 us -> 32.7 us  [the longest x1 11.8 us: project(): pl.pallas_call(functools.partial(project_kernel, cuts), in_specs=[ANY] *...]
    unnamed x7 -> x5, local copies, waits for them, and re-layouts: 2 us -> 1.05 us
    ppermute x14 -> x15, waiting for transfers between devices: 9.28 us -> 9.59 us  [swap(): return lax.ppermute(x, 'seq', [(i, i ^ r) for i in range(size)])]
  transfers between devices with their start and end apart: 16 -> 16, of which waited for: 6 -> 10; matrix products, arithmetic and copies ran while one was open for 1% -> 0% of each run, Pallas kernels for 43% -> 45%
where the time goes in v5:
time: 67.3 us; the launch traced here: 67 us
  Pallas kernels  32.7 us (49%)
  starting transfers between devices  22.2 us (33%)
  waiting for transfers between devices  9.59 us (14%)
  between operations  1.43 us (2%)
  local copies, waits for them, and re-layouts  1.09 us (2%)
    ppermute x15, starting transfers between devices, swap(): return lax.ppermute(x, 'seq', [(i, i ^ r) for i in range(size)])  17 us
    pallas_call x1, Pallas kernels, project(): pl.pallas_call(functools.partial(project_kernel, cuts), in_specs=[ANY] *...  11.8 us
    pallas_call x2, Pallas kernels, score(): pl.pallas_call(functools.partial(score_kernel, keys, chunk, tile), in_spe...  10.3 us
    ppermute x15, waiting for transfers between devices, swap(): return lax.ppermute(x, 'seq', [(i, i ^ r) for i in range(size)])  9.59 us
    all_to_all x1, starting transfers between devices, shards(): lax.all_to_all(picked.reshape(size, own_keys // size, -1), 'seq', split_a...  5.11 us
    pallas_call x2, Pallas kernels, weigh(): pl.pallas_call(functools.partial(weigh_kernel, factor, 1 + len(others)),...  4.58 us
    pallas_call x1, Pallas kernels, pick(): pl.pallas_call(functools.partial(pick_kernel, size), in_specs=[SMEM] + [V...  2.19 us
    pallas_call x1, Pallas kernels, front(): pl.pallas_call(functools.partial(front_kernel, len(counts), size // CHIPS...  1.92 us
  transfers between devices with their start and end apart: 16, of which 10 were waited for; matrix products, arithmetic and copies ran while one was open for 0% of the time, Pallas kernels for 45%

profile of v5, /device:TPU:0, one launch (start us, length us, event | category | flops | bytes accessed | tf_op | source)
XLA Modules:
  0.0 67.0 jit_solution(3935856692217092141)
XLA Ops:
  0.6 3.0 %collective-permute-start = (s32[1]{0:T(128)}, s32[1]{0:T(128)}, u32[]{:S(2)}, u32[]{:S(2)}) collective-permute-start(s32[1]{0:T(128)} %param.11), channel_id=1, source_target_pairs={{0,2},{1,3},{2,0},{3,1},{4,6},{5,7},{6,4},{7,5},{8,10},{9,11},{10,... | collective-permute-start | bytes 20 | tf_op jit(solution)/shard_map/ppermute | solution.py:358
  4.3 0.9 %collective-permute-done.refs_1_ = s32[1]{0:T(128)} collective-permute-done((s32[1]{0:T(128)}, s32[1]{0:T(128)}, u32[]{:S(2)}, u32[]{:S(2)}) %collective-permute-start) | collective-permute-done | bytes 36 | tf_op jit(solution)/shard_map/ppermute | solution.py:358
  5.3 1.9 %front.1 = (bf16[784,128]{1,0:T(8,128)(2,1)S(1)}, bf16[784,128]{1,0:T(8,128)(2,1)S(1)}, bf16[784,128]{1,0:T(8,128)(2,1)S(1)}, bf16[784,128]{1,0:T(8,128)(2,1)S(1)}) custom-call(s32[1]{0:T(128)} %bitcast.me_ref, s32[1]{0:T(128)S(6)} %copy.19.refs_0_, s32[1]{0:T(128)} %collective-permute-done.refs_1_, bf16[512,512]{1,0:T(8,128)(2,1)} %refs_2_.1, ...), custom_call_target="tpu_custom_call" | custom-call | bytes 1572864 | tf_op jit(solution)/shard_map/front/pallas_call | solution.py:140
  7.2 2.1 %collective-permute-start.1 = (bf16[784,128]{1,0:T(8,128)(2,1)S(1)}, bf16[784,128]{1,0:T(8,128)(2,1)S(1)}, u32[]{:S(2)}, u32[]{:S(2)}) collective-permute-start(bf16[784,128]{1,0:T(8,128)(2,1)S(1)} %get-tuple-element.18), channel_id=1, source_target_pairs={{0,4},{1,5},{2,6},{3,7},{4,0},{5,1},{6,2},{7,3},{8,12},{9,13},{10,... | collective-permute-start | bytes 602120 | tf_op jit(solution)/shard_map/ppermute | solution.py:358
  9.3 2.6 %collective-permute-start.2 = (bf16[784,128]{1,0:T(8,128)(2,1)S(1)}, bf16[784,128]{1,0:T(8,128)(2,1)S(1)}, u32[]{:S(2)}, u32[]{:S(2)}) collective-permute-start(bf16[784,128]{1,0:T(8,128)(2,1)S(1)} %get-tuple-element.19), channel_id=1, source_target_pairs={{0,8},{1,9},{2,10},{3,11},{4,12},{5,13},{6,14},{7,15},{8,0},{9,1},... | collective-permute-start | bytes 602120 | tf_op jit(solution)/shard_map/ppermute | solution.py:358
  11.9 0.0 collective-permute-start.3
  11.9 0.0 copy-start.1
  11.9 11.8 %project.1.refs_9_ = bf16[512,1024]{1,0:T(8,128)(2,1)S(1)} custom-call(bf16[512,8192]{1,0:T(8,128)(2,1)} %x_hbm.1, f32[1,8192]{1,0:T(1,128)} %bitcast.30, bf16[8192,1024]{1,0:T(8,128)(2,1)} %weight_hbm.1, f32[1,1024]{1,0:T(1,128)} %bitcast.31), custom_call_target="tpu_custom_call" | custom-call | flops 8589934592 | bytes 25165824 | tf_op jit(solution)/shard_map/project/pallas_call | solution.py:88
  23.7 0.0 collective-permute-done.1.refs_2_
  23.7 2.7 %collective-permute-done.2.refs_4_ = bf16[784,128]{1,0:T(8,128)(2,1)S(1)} collective-permute-done((bf16[784,128]{1,0:T(8,128)(2,1)S(1)}, bf16[784,128]{1,0:T(8,128)(2,1)S(1)}, u32[]{:S(2)}, u32[]{:S(2)}) %collective-permute-start.2) | collective-permute-done | bytes 200736 | tf_op jit(solution)/shard_map/ppermute | solution.py:358
  26.5 0.0 collective-permute-done.3.refs_6_
  26.5 0.0 collective-permute-start.4
  26.5 0.5 collective-permute-start.5
  27.0 0.0 collective-permute-start.6
  27.0 0.5 collective-permute-start.7
  27.5 0.4 collective-permute-done.4.refs_1_
  27.9 0.3 collective-permute-done.5.refs_3_
  28.2 0.3 collective-permute-done.6.refs_5_
  28.5 0.3 collective-permute-done.7.refs_7_
  28.8 1.6 %collective-permute-start.8 = (bf16[1024,128]{1,0:T(8,128)(2,1)S(1)}, bf16[1024,128]{1,0:T(8,128)(2,1)S(1)}, u32[]{:S(2)}, u32[]{:S(2)}) collective-permute-start(bf16[1024,128]{1,0:T(8,128)(2,1)S(1)} %collect.1.q_ref), channel_id=1, source_target_pairs={{0,2},{1,3},{2,0},{3,1},{4,6},{5,7},{6,4},{7,5},{8,10},{9,11},{10,... | collective-permute-start | bytes 786440 | tf_op jit(solution)/shard_map/ppermute | solution.py:358
  30.4 0.0 copy-done.1
  30.4 2.2 %pick.1.refs_8_ = bf16[512,1024]{1,0:T(8,128)(2,1)} custom-call(s32[1]{0:T(128)} %bitcast.me_ref, bf16[784,128]{1,0:T(8,128)(2,1)S(1)} %get-tuple-element.21.refs_0_, bf16[784,128]{1,0:T(8,128)(2,1)S(1)} %collective-permute-done.4.refs_1_, bf16[784,128]{1,0:T(8,128)(2,1)S(1)} %collective-permute-done.1.refs_2_, ...), custom_call_target="tpu_custom_call" | custom-call | flops 805306368 | bytes 2097152 | tf_op jit(solution)/shard_map/pick/pallas_call | solution.py:203
  32.6 5.1 %all-to-all-start = ((bf16[16,32,1024]{2,1,0:T(8,128)(2,1)}), bf16[16,32,1024]{2,1,0:T(8,128)(2,1)S(1)}, u32[]{:S(2)}, u32[]{:S(2)}) async-start(bf16[16,32,1024]{2,1,0:T(8,128)(2,1)} %bitcast.12), calls=%async_computation | async-start | bytes 2097152 | tf_op jit(solution)/shard_map/all_to_all | solution.py:376
  37.7 0.0 collective-permute-done.8.q_ref
  37.7 5.2 %score.2 = (bf16[4096,1024]{1,0:T(8,128)(2,1)S(1)}, f32[16,1024]{1,0:T(8,128)S(1)}, f32[1,1024]{1,0:T(1,128)S(1)}) custom-call(bf16[1024,128]{1,0:T(8,128)(2,1)S(1)} %collective-permute-done.8.q_ref, bf16[784,128]{1,0:T(8,128)(2,1)S(1)} %get-tuple-element.21.refs_0_, bf16[784,128]{1,0:T(8,128)(2,1)S(1)} %collective-permute-done.4.refs_1_, ...), custom_call_target="tpu_custom_call" | custom-call | flops 8589934592 | bytes 8388608 | tf_op jit(solution)/shard_map/score/pallas_call | solution.py:279
  42.9 2.0 %collective-permute-start.10 = (f32[1,1024]{1,0:T(1,128)S(1)}, f32[1,1024]{1,0:T(1,128)S(1)}, u32[]{:S(2)}, u32[]{:S(2)}) collective-permute-start(f32[1,1024]{1,0:T(1,128)S(1)} %get-tuple-element.28.refs_8_.lse_ref), channel_id=1, source_target_pairs={{0,2},{1,3},{2,0},{3,1},{4,6},{5,7},{6,4},{7,5},{8,10},{9,11},{10,... | collective-permute-start | bytes 12296 | tf_op jit(solution)/shard_map/ppermute | solution.py:358
  44.9 5.1 %score.3 = (bf16[4096,1024]{1,0:T(8,128)(2,1)S(1)}, f32[16,1024]{1,0:T(8,128)S(1)}, f32[1,1024]{1,0:T(1,128)S(1)}) custom-call(bf16[1024,128]{1,0:T(8,128)(2,1)S(1)} %collect.1.q_ref, bf16[784,128]{1,0:T(8,128)(2,1)S(1)} %get-tuple-element.21.refs_0_, bf16[784,128]{1,0:T(8,128)(2,1)S(1)} %collective-permute-done.4.refs_1_, ...), custom_call_target="tpu_custom_call" | custom-call | flops 8589934592 | bytes 8388608 | tf_op jit(solution)/shard_map/score/pallas_call | solution.py:279
  50.0 0.2 collective-permute-start.9
  50.2 0.0 collective-permute-done.10.rest_0_
  50.2 2.3 %weigh.2.rest_1_ = f32[16,256]{1,0:T(8,128)S(1)} custom-call(bf16[4096,1024]{1,0:T(8,128)(2,1)S(1)} %get-tuple-element.30.prob_ref, f32[16,1024]{1,0:T(8,128)S(1)} %get-tuple-element.31.top_ref, f32[1,1024]{1,0:T(1,128)S(1)} %get-tuple-element.29.lse_ref, f32[1,1024]{1,0:T(1,128)S(1)} %collective-permute-done.10.rest_0_), custom_call_target="tpu_custom_call" | custom-call | flops 16777216 | bytes 8388608 | tf_op jit(solution)/shard_map/weigh/pallas_call | solution.py:322
  52.5 1.2 %collective-permute-done.9.rest_0_ = f32[1,1024]{1,0:T(1,128)S(1)} collective-permute-done((f32[1,1024]{1,0:T(1,128)S(1)}, f32[1,1024]{1,0:T(1,128)S(1)}, u32[]{:S(2)}, u32[]{:S(2)}) %collective-permute-start.9) | collective-permute-done | bytes 4128 | tf_op jit(solution)/shard_map/ppermute | solution.py:358
  53.7 2.3 %weigh.3 = f32[16,256]{1,0:T(8,128)S(1)} custom-call(bf16[4096,1024]{1,0:T(8,128)(2,1)S(1)} %get-tuple-element.26.prob_ref, f32[16,1024]{1,0:T(8,128)S(1)} %get-tuple-element.27.top_ref, f32[1,1024]{1,0:T(1,128)S(1)} %get-tuple-element.28.refs_8_.lse_ref, f32[1,1024]{1,0:T(1,128)S(1)} %collective-permute-done.9.rest_0_, f32[16,256]{1,0:T(8,128)S(1)} %weigh.2.rest_1_), custom_call_target="tpu_custom_call" | custom-call | flops 16777216 | bytes 8388608 | tf_op jit(solution)/shard_map/weigh/pallas_call | solution.py:322
  56.0 0.1 collective-permute-start.11
  56.1 1.2 %collective-permute-done.11 = f32[4,512]{1,0:T(4,128)S(1)} collective-permute-done((f32[4,512]{1,0:T(4,128)S(1)}, f32[4,512]{1,0:T(4,128)S(1)}, u32[]{:S(2)}, u32[]{:S(2)}) %collective-permute-start.11) | collective-permute-done | bytes 8224 | tf_op jit(solution)/shard_map/ppermute | solution.py:358
  57.3 3.4 %collective-permute-start.14 = (f32[512]{0:T(512)S(1)}, f32[512]{0:T(512)S(1)}, u32[]{:S(2)}, u32[]{:S(2)}) collective-permute-start(f32[512]{0:T(512)S(1)} %bitcast.29), channel_id=1, source_target_pairs={{0,12},{1,13},{2,14},{3,15},{4,8},{5,9},{6,10},{7,11},{8,4},{9,5},... | collective-permute-start | bytes 6152 | tf_op jit(solution)/shard_map/ppermute | solution.py:358
  60.7 0.2 collective-permute-start.12
  60.9 0.9 %collective-permute-start.13 = (f32[512]{0:T(512)S(1)}, f32[512]{0:T(512)S(1)}, u32[]{:S(2)}, u32[]{:S(2)}) collective-permute-start(f32[512]{0:T(512)S(1)} %bitcast.27), channel_id=1, source_target_pairs={{0,8},{1,9},{2,10},{3,11},{4,12},{5,13},{6,14},{7,15},{8,0},{9,1},... | collective-permute-start | bytes 6152 | tf_op jit(solution)/shard_map/ppermute | solution.py:358
  61.7 0.0 all-to-all-done
  61.8 1.3 %place.1.refs_4_ = bf16[256,1024]{1,0:T(8,128)(2,1)} custom-call(s32[1]{0:T(128)} %bitcast.me_ref, bf16[784,128]{1,0:T(8,128)(2,1)S(1)} %get-tuple-element.21.refs_0_, bf16[784,128]{1,0:T(8,128)(2,1)S(1)} %collective-permute-done.4.refs_1_, bf16[784,128]{1,0:T(8,128)(2,1)S(1)} %collective-permute-done.1.refs_2_, ...), custom_call_target="tpu_custom_call" | custom-call | flops 268435456 | bytes 1572864 | tf_op jit(solution)/shard_map/place/pallas_call | solution.py:234
  63.1 0.0 collective-permute-done.14
  63.1 1.1 %collective-permute-done.12 = f32[512]{0:T(512)S(1)} collective-permute-done((f32[512]{0:T(512)S(1)}, f32[512]{0:T(512)S(1)}, u32[]{:S(2)}, u32[]{:S(2)}) %collective-permute-start.12) | collective-permute-done | bytes 2080 | tf_op jit(solution)/shard_map/ppermute | solution.py:358
  64.3 1.1 %collective-permute-done.13 = f32[512]{0:T(512)S(1)} collective-permute-done((f32[512]{0:T(512)S(1)}, f32[512]{0:T(512)S(1)}, u32[]{:S(2)}, u32[]{:S(2)}) %collective-permute-start.13) | collective-permute-done | bytes 2080 | tf_op jit(solution)/shard_map/ppermute | solution.py:358
  65.4 0.0 copy-start
  65.4 1.0 %copy-done = bf16[256,1024]{1,0:T(8,128)(2,1)S(1)} copy-done((bf16[256,1024]{1,0:T(8,128)(2,1)S(1)}, bf16[256,1024]{1,0:T(8,128)(2,1)}, u32[]{:S(2)}) %copy-start) | copy-done | bytes 524312
  66.4 0.6 finish.1
  (6 shorter events, 0.1 us)
Async XLA Ops:
  0.6 4.6 %collective-permute-start = (s32[1]{0:T(128)}, s32[1]{0:T(128)}, u32[]{:S(2)}, u32[]{:S(2)}) collective-permute-start(s32[1]{0:T(128)} %param.11), channel_id=1, source_target_pairs={{0,2},{1,3},{2,0},{3,1},{4,6},{5,7},{6,4},{7,5},{8,10},{9,11},{10,... | collective-permute-start | bytes 20 | tf_op jit(solution)/shard_map/ppermute | solution.py:358
  7.2 16.5 %collective-permute-start.1 = (bf16[784,128]{1,0:T(8,128)(2,1)S(1)}, bf16[784,128]{1,0:T(8,128)(2,1)S(1)}, u32[]{:S(2)}, u32[]{:S(2)}) collective-permute-start(bf16[784,128]{1,0:T(8,128)(2,1)S(1)} %get-tuple-element.18), channel_id=1, source_target_pairs={{0,4},{1,5},{2,6},{3,7},{4,0},{5,1},{6,2},{7,3},{8,12},{9,13},{10,... | collective-permute-start | bytes 602120 | tf_op jit(solution)/shard_map/ppermute | solution.py:358
  9.3 17.2 %collective-permute-start.2 = (bf16[784,128]{1,0:T(8,128)(2,1)S(1)}, bf16[784,128]{1,0:T(8,128)(2,1)S(1)}, u32[]{:S(2)}, u32[]{:S(2)}) collective-permute-start(bf16[784,128]{1,0:T(8,128)(2,1)S(1)} %get-tuple-element.19), channel_id=1, source_target_pairs={{0,8},{1,9},{2,10},{3,11},{4,12},{5,13},{6,14},{7,15},{8,0},{9,1},... | collective-permute-start | bytes 602120 | tf_op jit(solution)/shard_map/ppermute | solution.py:358
  11.9 14.6 %collective-permute-start.3 = (bf16[784,128]{1,0:T(8,128)(2,1)S(1)}, bf16[784,128]{1,0:T(8,128)(2,1)S(1)}, u32[]{:S(2)}, u32[]{:S(2)}) collective-permute-start(bf16[784,128]{1,0:T(8,128)(2,1)S(1)} %get-tuple-element.20), channel_id=1, source_target_pairs={{0,12},{1,13},{2,14},{3,15},{4,8},{5,9},{6,10},{7,11},{8,4},{9,5},... | collective-permute-start | bytes 602120 | tf_op jit(solution)/shard_map/ppermute | solution.py:358
  11.9 18.5 %copy-start.1 = (s32[512]{0:T(512)S(1)}, s32[512]{0:T(512)}, u32[]{:S(2)}) copy-start(s32[512]{0:T(512)} %param.12) | copy-start | bytes 6148
  26.5 1.4 %collective-permute-start.4 = (bf16[784,128]{1,0:T(8,128)(2,1)S(1)}, bf16[784,128]{1,0:T(8,128)(2,1)S(1)}, u32[]{:S(2)}, u32[]{:S(2)}) collective-permute-start(bf16[784,128]{1,0:T(8,128)(2,1)S(1)} %get-tuple-element.21.refs_0_), channel_id=1, source_target_pairs={{0,1},{1,0},{2,3},{3,2},{4,5},{5,4},{6,7},{7,6},{8,9},{9,8},{10,11... | collective-permute-start | bytes 602120 | tf_op jit(solution)/shard_map/ppermute | solution.py:358
  26.5 1.7 %collective-permute-start.5 = (bf16[784,128]{1,0:T(8,128)(2,1)S(1)}, bf16[784,128]{1,0:T(8,128)(2,1)S(1)}, u32[]{:S(2)}, u32[]{:S(2)}) collective-permute-start(bf16[784,128]{1,0:T(8,128)(2,1)S(1)} %collective-permute-done.1.refs_2_), channel_id=1, source_target_pairs={{0,1},{1,0},{2,3},{3,2},{4,5},{5,4},{6,7},{7,6},{8,9},{9,8},{10,11... | collective-permute-start | bytes 602120 | tf_op jit(solution)/shard_map/ppermute | solution.py:358
  27.0 1.5 %collective-permute-start.6 = (bf16[784,128]{1,0:T(8,128)(2,1)S(1)}, bf16[784,128]{1,0:T(8,128)(2,1)S(1)}, u32[]{:S(2)}, u32[]{:S(2)}) collective-permute-start(bf16[784,128]{1,0:T(8,128)(2,1)S(1)} %collective-permute-done.2.refs_4_), channel_id=1, source_target_pairs={{0,1},{1,0},{2,3},{3,2},{4,5},{5,4},{6,7},{7,6},{8,9},{9,8},{10,11... | collective-permute-start | bytes 602120 | tf_op jit(solution)/shard_map/ppermute | solution.py:358
  27.0 1.8 %collective-permute-start.7 = (bf16[784,128]{1,0:T(8,128)(2,1)S(1)}, bf16[784,128]{1,0:T(8,128)(2,1)S(1)}, u32[]{:S(2)}, u32[]{:S(2)}) collective-permute-start(bf16[784,128]{1,0:T(8,128)(2,1)S(1)} %collective-permute-done.3.refs_6_), channel_id=1, source_target_pairs={{0,1},{1,0},{2,3},{3,2},{4,5},{5,4},{6,7},{7,6},{8,9},{9,8},{10,11... | collective-permute-start | bytes 602120 | tf_op jit(solution)/shard_map/ppermute | solution.py:358
  28.8 8.9 %collective-permute-start.8 = (bf16[1024,128]{1,0:T(8,128)(2,1)S(1)}, bf16[1024,128]{1,0:T(8,128)(2,1)S(1)}, u32[]{:S(2)}, u32[]{:S(2)}) collective-permute-start(bf16[1024,128]{1,0:T(8,128)(2,1)S(1)} %collect.1.q_ref), channel_id=1, source_target_pairs={{0,2},{1,3},{2,0},{3,1},{4,6},{5,7},{6,4},{7,5},{8,10},{9,11},{10,... | collective-permute-start | bytes 786440 | tf_op jit(solution)/shard_map/ppermute | solution.py:358
  32.6 29.2 %all-to-all-start = ((bf16[16,32,1024]{2,1,0:T(8,128)(2,1)}), bf16[16,32,1024]{2,1,0:T(8,128)(2,1)S(1)}, u32[]{:S(2)}, u32[]{:S(2)}) async-start(bf16[16,32,1024]{2,1,0:T(8,128)(2,1)} %bitcast.12), calls=%async_computation | async-start | bytes 2097152 | tf_op jit(solution)/shard_map/all_to_all | solution.py:376
  42.9 7.3 %collective-permute-start.10 = (f32[1,1024]{1,0:T(1,128)S(1)}, f32[1,1024]{1,0:T(1,128)S(1)}, u32[]{:S(2)}, u32[]{:S(2)}) collective-permute-start(f32[1,1024]{1,0:T(1,128)S(1)} %get-tuple-element.28.refs_8_.lse_ref), channel_id=1, source_target_pairs={{0,2},{1,3},{2,0},{3,1},{4,6},{5,7},{6,4},{7,5},{8,10},{9,11},{10,... | collective-permute-start | bytes 12296 | tf_op jit(solution)/shard_map/ppermute | solution.py:358
  50.0 3.7 %collective-permute-start.9 = (f32[1,1024]{1,0:T(1,128)S(1)}, f32[1,1024]{1,0:T(1,128)S(1)}, u32[]{:S(2)}, u32[]{:S(2)}) collective-permute-start(f32[1,1024]{1,0:T(1,128)S(1)} %get-tuple-element.29.lse_ref), channel_id=1, source_target_pairs={{0,2},{1,3},{2,0},{3,1},{4,6},{5,7},{6,4},{7,5},{8,10},{9,11},{10,... | collective-permute-start | bytes 12296 | tf_op jit(solution)/shard_map/ppermute | solution.py:358
  56.0 1.2 %collective-permute-start.11 = (f32[4,512]{1,0:T(4,128)S(1)}, f32[4,512]{1,0:T(4,128)S(1)}, u32[]{:S(2)}, u32[]{:S(2)}) collective-permute-start(f32[4,512]{1,0:T(4,128)S(1)} %bitcast.25), channel_id=1, source_target_pairs={{0,1},{1,0},{2,3},{3,2},{4,5},{5,4},{6,7},{7,6},{8,9},{9,8},{10,11... | collective-permute-start | bytes 24584 | tf_op jit(solution)/shard_map/ppermute | solution.py:358
  57.3 5.8 %collective-permute-start.14 = (f32[512]{0:T(512)S(1)}, f32[512]{0:T(512)S(1)}, u32[]{:S(2)}, u32[]{:S(2)}) collective-permute-start(f32[512]{0:T(512)S(1)} %bitcast.29), channel_id=1, source_target_pairs={{0,12},{1,13},{2,14},{3,15},{4,8},{5,9},{6,10},{7,11},{8,4},{9,5},... | collective-permute-start | bytes 6152 | tf_op jit(solution)/shard_map/ppermute | solution.py:358
  60.7 3.6 %collective-permute-start.12 = (f32[512]{0:T(512)S(1)}, f32[512]{0:T(512)S(1)}, u32[]{:S(2)}, u32[]{:S(2)}) collective-permute-start(f32[512]{0:T(512)S(1)} %bitcast.28), channel_id=1, source_target_pairs={{0,4},{1,5},{2,6},{3,7},{4,0},{5,1},{6,2},{7,3},{8,12},{9,13},{10,... | collective-permute-start | bytes 6152 | tf_op jit(solution)/shard_map/ppermute | solution.py:358
  60.9 4.5 %collective-permute-start.13 = (f32[512]{0:T(512)S(1)}, f32[512]{0:T(512)S(1)}, u32[]{:S(2)}, u32[]{:S(2)}) collective-permute-start(f32[512]{0:T(512)S(1)} %bitcast.27), channel_id=1, source_target_pairs={{0,8},{1,9},{2,10},{3,11},{4,12},{5,13},{6,14},{7,15},{8,0},{9,1},... | collective-permute-start | bytes 6152 | tf_op jit(solution)/shard_map/ppermute | solution.py:358
  65.4 1.0 %copy-start = (bf16[256,1024]{1,0:T(8,128)(2,1)S(1)}, bf16[256,1024]{1,0:T(8,128)(2,1)}, u32[]{:S(2)}) copy-start(bf16[256,1024]{1,0:T(8,128)(2,1)} %place.1.refs_4_) | copy-start | bytes 1572868

commit v6 on v5

--- a/solution.py
+++ b/solution.py
@@ -112,18 +112,13 @@
     return list(range(0, size // CHIPS, 2))
 
 
-def front_kernel(cells, stride, keys, me_ref, *refs):
-    count_refs, (keys_ref, q_ref), out_refs = refs[:cells], refs[cells : cells + 2], refs[cells + 2 :]
+def front_kernel(stride, keys, me_ref, count_ref, keys_ref, q_ref, *out_refs):
     me = me_ref[0]
+    count = count_ref[0]
     tokens = q_ref.shape[0]
     heads = q_ref.shape[1] // HD // CHIPS
-    lane = lax.broadcasted_iota(jnp.int32, (EXTRA, 128), 1)
-    high = lax.broadcasted_iota(jnp.int32, (EXTRA, 128), 0) < EXTRA // 2
-    extra = jnp.zeros((EXTRA, 128), jnp.int32)
-    for c in range(cells):
-        count = count_refs[c][0]
-        extra = jnp.where(lane == c, jnp.where(high, count // 8, count % 8), extra)
-    extra = extra.astype(F32).astype(BF16)
+    high = lax.broadcasted_iota(jnp.int32, (EXTRA, HD), 0) < EXTRA // 2
+    extra = jnp.where(high, count // 8, count % 8).astype(F32).astype(BF16)
     first = (1 - me % 2) * (heads // 2)
     for i, out_ref in enumerate(out_refs):
         head = (me ^ (stride * i)) // stride
@@ -135,84 +130,103 @@
             out_ref[at : at + tokens, :] = q_ref[:, pl.ds(pl.multiple_of(q_head * HD, HD), HD)]
 
 
-def front(me, counts, keys, queries, size):
+def front(me, count, keys, queries, size):
     rows = keys.shape[0] + EXTRA + queries.size // HD // CHIPS
     return pl.pallas_call(
-        functools.partial(front_kernel, len(counts), size // CHIPS, keys.shape[0]),
-        in_specs=[SMEM] * (1 + len(counts)) + [VMEM] * 2,
+        functools.partial(front_kernel, size // CHIPS, keys.shape[0]),
+        in_specs=[SMEM] * 2 + [VMEM] * 2,
         out_specs=[VMEM] * CHIPS,
         out_shape=[jax.ShapeDtypeStruct((rows, HD), BF16)] * CHIPS,
         compiler_params=params(16),
         cost_estimate=cost(0, 4 * keys.size + 4 * queries.size),
         name="front",
-    )(me, *counts, in_hbm(keys), in_hbm(queries))
-
-
-def collect_kernel(*refs):
-    block_refs, out_ref = refs[:CELL], refs[CELL]
+    )(me, count, in_hbm(keys), in_hbm(queries))
+
+
+def collect_kernel(keys, *refs):
+    block_refs, (out_ref, counts_ref) = refs[:CELL], refs[CELL:]
     rows = out_ref.shape[0] // CELL
+    lane = lax.broadcasted_iota(jnp.int32, counts_ref.shape, 1)
+    counts = jnp.zeros(counts_ref.shape, F32)
     for i, ref in enumerate(block_refs):
         at = ref.shape[0] - rows * (2 if i % 2 else 1)
         out_ref[i * rows : (i + 1) * rows, :] = ref[at : at + rows, :]
+        extra = ref[keys : keys + EXTRA, :].astype(F32)
+        counts = jnp.where(lane == i, extra[:1] * 8.0 + extra[EXTRA // 2 : EXTRA // 2 + 1], counts)
+    counts_ref[...] = counts.astype(jnp.int32)
 
 
 def collect(blocks, keys):
     rows = (blocks[0].shape[0] - keys - EXTRA) // 2
     return pl.pallas_call(
-        collect_kernel,
+        functools.partial(collect_kernel, keys),
         in_specs=[VMEM] * CELL,
-        out_specs=VMEM,
-        out_shape=jax.ShapeDtypeStruct((CELL * rows, HD), BF16),
+        out_specs=[VMEM] * 2,
+        out_shape=[
+            jax.ShapeDtypeStruct((CELL * rows, HD), BF16),
+            jax.ShapeDtypeStruct((1, HD), jnp.int32),
+        ],
         compiler_params=params(16),
         cost_estimate=cost(0, 4 * CELL * rows * HD),
         name="collect",
     )(*blocks)
 
 
-def counts_of(me, refs, size, keys):
-    pairs = []
-    for r, ref in zip(cell_steps(size), refs):
-        extra = ref[keys : keys + EXTRA, :].astype(F32)
-        count = (extra[:1] * 8.0 + extra[EXTRA // 2 : EXTRA // 2 + 1]).astype(jnp.int32)
-        for c, cross in enumerate(cross_steps(size)):
-            pairs.append((me ^ r ^ cross, count[:, c : c + 1]))
-    return pairs
-
-
-def pick_kernel(size, me_ref, *refs):
-    count_refs, (keep_ref, rows_ref, out_ref) = refs[:CELL], refs[CELL:]
-    me = me_ref[0]
+def choose_kernel(size, keep_ref, rows_ref, out_ref):
     n = rows_ref.shape[0]
-    start = jnp.zeros((1, 1), jnp.int32)
-    for device, count in counts_of(me, count_refs, size, n):
-        start += jnp.where(device < me, count, 0)
     cap = n // size
     slot = lax.broadcasted_iota(jnp.int32, (n, n), 0)
     entry = lax.broadcasted_iota(jnp.int32, (n, n), 1)
-    wanted = ((slot // cap - start) & (size - 1)) + (slot & (cap - 1)) * size
-    chooses = (wanted == entry).astype(F32).astype(BF16)
+    chooses = (slot // cap + (slot & (cap - 1)) * size == entry).astype(F32).astype(BF16)
     listed = (keep_ref[...] == slot).astype(F32).astype(BF16)
     select = lax.dot_general(
         chooses, listed, (((1,), (1,)), ((), ())), preferred_element_type=F32
     ).astype(BF16)
-    out_ref[...] = jnp.dot(select, rows_ref[...], preferred_element_type=F32).astype(BF16)
-
-
-def pick(me, blocks, keep_index, rows, size):
-    n = rows.shape[0]
-    return pl.pallas_call(
-        functools.partial(pick_kernel, size),
-        in_specs=[SMEM] + [VMEM] * (CELL + 2),
+    rows = jnp.dot(select, rows_ref[...], preferred_element_type=F32).astype(BF16)
+    out_ref[...] = rows.reshape(out_ref.shape)
+
+
+def choose(keep_index, rows, size):
+    n, width = rows.shape
+    return pl.pallas_call(
+        functools.partial(choose_kernel, size),
+        in_specs=[VMEM] * 2,
+        out_specs=VMEM,
+        out_shape=jax.ShapeDtypeStruct((size, n // size, width), BF16),
+        compiler_params=params(32),
+        cost_estimate=cost(2 * n * n * (n + width), 4 * rows.size),
+        name="choose",
+    )(keep_index.reshape(1, -1), rows)
+
+
+def deal_kernel(me_ref, *refs):
+    count_refs, (rows_ref, out_ref) = refs[:-2], refs[-2:]
+    me = me_ref[0]
+    size = rows_ref.shape[0]
+    lane = lax.broadcasted_iota(jnp.int32, (1, HD), 1)
+    here = me ^ ((lane >> 1) * (size // CHIPS) + (lane & 1))
+    start = jnp.int32(0)
+    for step, ref in zip(cross_steps(size), count_refs):
+        before = (lane < CELL) & ((here ^ step) < me)
+        start += jnp.sum(jnp.where(before, ref[...], 0))
+    for owner in range(size):
+        out_ref[owner] = rows_ref[(owner - start) & (size - 1)]
+
+
+def deal(me, counts, rows):
+    return pl.pallas_call(
+        deal_kernel,
+        in_specs=[SMEM] + [VMEM] * (len(counts) + 1),
         out_specs=VMEM,
         out_shape=jax.ShapeDtypeStruct(rows.shape, BF16),
-        compiler_params=params(32),
-        cost_estimate=cost(2 * n * n * (n + rows.shape[1]), 4 * rows.size),
-        name="pick",
-    )(me, *blocks, keep_index.reshape(1, -1), rows)
+        compiler_params=params(16),
+        cost_estimate=cost(2e10, 4 * rows.size),
+        name="deal",
+    )(me, *counts, rows)
 
 
 def place_kernel(size, me_ref, *refs):
-    count_refs, (rows_ref, out_ref) = refs[:CELL], refs[CELL:]
+    count_refs, (rows_ref, out_ref) = refs[:-2], refs[-2:]
     me = me_ref[0]
     keep, n = out_ref.shape[0], rows_ref.shape[0]
     cap = n // size
@@ -220,9 +234,12 @@
     source = slot // cap
     starts = jnp.zeros((1, n), jnp.int32)
     counts = jnp.zeros((1, n), jnp.int32)
-    for device, count in counts_of(me, count_refs, size, n):
-        starts += jnp.where(source > device, count, 0)
-        counts = jnp.where(source == device, count, counts)
+    for cross, ref in zip(cross_steps(size), count_refs):
+        for lane, step in enumerate(cell_steps(size)):
+            device = me ^ cross ^ step
+            count = ref[:, lane : lane + 1]
+            starts += jnp.where(source > device, count, 0)
+            counts = jnp.where(source == device, count, counts)
     pos = ((me - starts) & (size - 1)) + (slot & (cap - 1)) * size
     target = jnp.where(pos < counts, (starts + pos) // size, keep)
     row = lax.broadcasted_iota(jnp.int32, (keep, n), 0)
@@ -230,16 +247,16 @@
     out_ref[...] = jnp.dot(select, rows_ref[...], preferred_element_type=F32).astype(BF16)
 
 
-def place(me, blocks, rows, keep, size):
+def place(me, counts, rows, keep, size):
     return pl.pallas_call(
         functools.partial(place_kernel, size),
-        in_specs=[SMEM] + [VMEM] * (CELL + 1),
+        in_specs=[SMEM] + [VMEM] * (len(counts) + 1),
         out_specs=VMEM,
         out_shape=jax.ShapeDtypeStruct((keep, rows.shape[1]), BF16),
         compiler_params=params(32),
         cost_estimate=cost(2 * keep * rows.size, 3 * rows.size),
         name="place",
-    )(me, *blocks, rows)
+    )(me, *counts, rows)
 
 
 def score_kernel(keys, chunk, tile, q_ref, *refs):
@@ -346,7 +363,7 @@
         compiler_params=params(16),
         cost_estimate=cost(CHIPS * keys, 4 * CHIPS * keys),
         name="finish",
-    )(*[part.reshape(row) for part in parts], after).reshape(keys)
+    )(*[part.reshape(row) for part in parts], in_hbm(after)).reshape(keys)
 
 
 def shards(queries, visual_keys, hidden, keep_count, keep_index, norm_gain, kv_weight, kv_bias):
@@ -357,26 +374,25 @@
     def swap(x, r):
         return lax.ppermute(x, "seq", [(i, i ^ r) for i in range(size)])
 
-    steps = cross_steps(size)
-    counts = [keep_count] + [swap(keep_count, r) for r in steps[1:]]
-
     far = [chip * (size // CHIPS) for chip in range(1, CHIPS)]
-    evens = front(me, counts, visual_keys, queries, size)
+    evens = front(me, keep_count, visual_keys, queries, size)
     evens = [evens[0]] + [swap(block, r) for block, r in zip(evens[1:], far)]
 
     projected = project(hidden, norm_gain, kv_weight, kv_bias)
-    *evens, projected = lax.optimization_barrier((*evens, projected))
+    chosen = choose(keep_index, projected, size)
+    *evens, chosen = lax.optimization_barrier((*evens, chosen))
     odds = [swap(block, 1) for block in evens]
     blocks = [block for pair in zip(evens, odds) for block in pair]
 
-    my_q = collect(blocks, own_keys)
+    steps = cross_steps(size)
+    my_q, my_counts = collect(blocks, own_keys)
+    counts = [my_counts] + [swap(my_counts, r) for r in steps[1:]]
     all_q = [my_q] + [swap(my_q, r) for r in steps[1:]]
 
-    picked = pick(me, blocks, keep_index, projected, size)
-    arrived = lax.all_to_all(
-        picked.reshape(size, own_keys // size, -1), "seq", split_axis=0, concat_axis=0, tiled=True
-    ).reshape(own_keys, -1)
-    layer_kv = place(me, blocks, arrived, own_keys // 2, size)
+    picked = deal(me, counts, chosen)
+    arrived = lax.all_to_all(picked, "seq", split_axis=0, concat_axis=0, tiled=True)
+    arrived = arrived.reshape(own_keys, -1)
+    layer_kv = place(me, counts, arrived, own_keys // 2, size)
 
     total_rows = size * queries.shape[0] * (queries.shape[1] // HD)
     factor = own_keys * size / total_rows

time: 67.3 us -> 65.4 us (0.972)
  local copies, waits for them, and re-layouts: 1.09 us -> 0.05 us
    ppermute x15, starting transfers between devices: 17 us -> 15 us  [swap(): return lax.ppermute(x, 'seq', [(i, i ^ r) for i in range(size)])]
    all_to_all x1, starting transfers between devices: 5.11 us -> 6.79 us  [shards(): lax.all_to_all(picked, 'seq', split_axis=0, concat_axis=0, tiled=True)]
    unnamed x5 -> x3, local copies, waits for them, and re-layouts: 1.05 us -> 0.01 us
    pallas_call x3 -> x4, Pallas kernels: 4.12 us -> 3.54 us  [the longest x1 1.29 us: front(): pl.pallas_call(functools.partial(front_kernel, size // CHIPS, keys.shape[...]
  transfers between devices with their start and end apart: 16 -> 16, of which waited for: 10 -> 10; matrix products, arithmetic and copies ran while one was open for 0% -> 0% of each run, Pallas kernels for 45% -> 47%
where the time goes in v6:
time: 65.4 us; the launch traced here: 65.2 us
  Pallas kernels  32.3 us (49%)
  starting transfers between devices  21.8 us (33%)
  waiting for transfers between devices  9.66 us (15%)
  between operations  1.41 us (2%)
    ppermute x15, starting transfers between devices, swap(): return lax.ppermute(x, 'seq', [(i, i ^ r) for i in range(size)])  15 us
    pallas_call x1, Pallas kernels, project(): pl.pallas_call(functools.partial(project_kernel, cuts), in_specs=[ANY] *...  11.8 us
    pallas_call x2, Pallas kernels, score(): pl.pallas_call(functools.partial(score_kernel, keys, chunk, tile), in_spe...  10.5 us
    ppermute x15, waiting for transfers between devices, swap(): return lax.ppermute(x, 'seq', [(i, i ^ r) for i in range(size)])  9.66 us
    all_to_all x1, starting transfers between devices, shards(): lax.all_to_all(picked, 'seq', split_axis=0, concat_axis=0, tiled=True)  6.79 us
    pallas_call x2, Pallas kernels, weigh(): pl.pallas_call(functools.partial(weigh_kernel, factor, 1 + len(others)),...  4.58 us
    pallas_call x1, Pallas kernels, place(): pl.pallas_call(functools.partial(place_kernel, size), in_specs=[SMEM] + [...  1.35 us
  transfers between devices with their start and end apart: 16, of which 10 were waited for; matrix products, arithmetic and copies ran while one was open for 0% of the time, Pallas kernels for 47%

profile of v6, /device:TPU:0, one launch (start us, length us, event | category | flops | bytes accessed | tf_op | source)
XLA Modules:
  0.0 65.2 jit_solution(4203186518428463335)
XLA Ops:
  1.3 1.3 %front.1 = (bf16[784,128]{1,0:T(8,128)(2,1)S(1)}, bf16[784,128]{1,0:T(8,128)(2,1)S(1)}, bf16[784,128]{1,0:T(8,128)(2,1)S(1)}, bf16[784,128]{1,0:T(8,128)(2,1)S(1)}) custom-call(s32[1]{0:T(128)} %bitcast.me_ref, s32[1]{0:T(128)S(6)} %copy.19.count_ref, bf16[512,512]{1,0:T(8,128)(2,1)} %keys_ref.1, bf16[32,4096]{1,0:T(8,128)(2,1)} %q_ref.1), custom_call_target="tpu_custom_call" | custom-call | bytes 1572864 | tf_op jit(solution)/shard_map/front/pallas_call | solution.py:135
  2.6 3.1 %collective-permute-start = (bf16[784,128]{1,0:T(8,128)(2,1)S(1)}, bf16[784,128]{1,0:T(8,128)(2,1)S(1)}, u32[]{:S(2)}, u32[]{:S(2)}) collective-permute-start(bf16[784,128]{1,0:T(8,128)(2,1)S(1)} %get-tuple-element.20), channel_id=1, source_target_pairs={{0,4},{1,5},{2,6},{3,7},{4,0},{5,1},{6,2},{7,3},{8,12},{9,13},{10,... | collective-permute-start | bytes 602120 | tf_op jit(solution)/shard_map/ppermute | solution.py:375
  5.7 2.6 %collective-permute-start.1 = (bf16[784,128]{1,0:T(8,128)(2,1)S(1)}, bf16[784,128]{1,0:T(8,128)(2,1)S(1)}, u32[]{:S(2)}, u32[]{:S(2)}) collective-permute-start(bf16[784,128]{1,0:T(8,128)(2,1)S(1)} %get-tuple-element.21), channel_id=1, source_target_pairs={{0,8},{1,9},{2,10},{3,11},{4,12},{5,13},{6,14},{7,15},{8,0},{9,1},... | collective-permute-start | bytes 602120 | tf_op jit(solution)/shard_map/ppermute | solution.py:375
  8.3 0.0 collective-permute-start.2
  8.3 0.0 copy-start
  8.3 11.8 %project.1.rows_ref = bf16[512,1024]{1,0:T(8,128)(2,1)S(1)} custom-call(bf16[512,8192]{1,0:T(8,128)(2,1)} %x_hbm.1, f32[1,8192]{1,0:T(1,128)} %bitcast.29, bf16[8192,1024]{1,0:T(8,128)(2,1)} %weight_hbm.1, f32[1,1024]{1,0:T(1,128)} %bitcast.30), custom_call_target="tpu_custom_call" | custom-call | flops 8589934592 | bytes 25165824 | tf_op jit(solution)/shard_map/project/pallas_call | solution.py:88
  20.1 0.0 copy-done
  20.1 1.0 %choose.1.refs_2_ = bf16[16,32,1024]{2,1,0:T(8,128)(2,1)S(1)} custom-call(s32[1,512]{1,0:T(1,128)S(1)} %bitcast.23, bf16[512,1024]{1,0:T(8,128)(2,1)S(1)} %project.1.rows_ref), custom_call_target="tpu_custom_call" | custom-call | flops 805306368 | bytes 2097152 | tf_op jit(solution)/shard_map/choose/pallas_call | solution.py:191
  21.1 0.0 collective-permute-done.refs_2_
  21.1 2.0 %collective-permute-done.1.refs_4_ = bf16[784,128]{1,0:T(8,128)(2,1)S(1)} collective-permute-done((bf16[784,128]{1,0:T(8,128)(2,1)S(1)}, bf16[784,128]{1,0:T(8,128)(2,1)S(1)}, u32[]{:S(2)}, u32[]{:S(2)}) %collective-permute-start.1) | collective-permute-done | bytes 200736 | tf_op jit(solution)/shard_map/ppermute | solution.py:375
  23.1 0.0 collective-permute-done.2.refs_6_
  23.1 0.0 collective-permute-start.3
  23.1 0.5 collective-permute-start.4
  23.6 0.0 collective-permute-start.5
  23.6 0.5 collective-permute-start.6
  24.1 0.4 collective-permute-done.3.refs_1_
  24.5 0.3 collective-permute-done.4.refs_3_
  24.8 0.3 collective-permute-done.5.refs_5_
  25.1 0.3 collective-permute-done.6.refs_7_
  25.4 1.6 %collective-permute-start.8 = (s32[1,128]{1,0:T(1,128)S(1)}, s32[1,128]{1,0:T(1,128)S(1)}, u32[]{:S(2)}, u32[]{:S(2)}) collective-permute-start(s32[1,128]{1,0:T(1,128)S(1)} %get-tuple-element.28.refs_0_), channel_id=1, source_target_pairs={{0,2},{1,3},{2,0},{3,1},{4,6},{5,7},{6,4},{7,5},{8,10},{9,11},{10,... | collective-permute-start | bytes 1544 | tf_op jit(solution)/shard_map/ppermute | solution.py:375
  27.0 0.5 collective-permute-start.7
  27.5 1.5 %collective-permute-done.8.refs_1_ = s32[1,128]{1,0:T(1,128)S(1)} collective-permute-done((s32[1,128]{1,0:T(1,128)S(1)}, s32[1,128]{1,0:T(1,128)S(1)}, u32[]{:S(2)}, u32[]{:S(2)}) %collective-permute-start.8) | collective-permute-done | bytes 544 | tf_op jit(solution)/shard_map/ppermute | solution.py:375
  29.0 1.2 %deal.1.refs_8_ = bf16[16,32,1024]{2,1,0:T(8,128)(2,1)} custom-call(s32[1]{0:T(128)} %bitcast.me_ref, s32[1,128]{1,0:T(1,128)S(1)} %get-tuple-element.28.refs_0_, s32[1,128]{1,0:T(1,128)S(1)} %collective-permute-done.8.refs_1_, bf16[16,32,1024]{2,1,0:T(8,128)(2,1)S(1)} %choose.1.refs_2_), custom_call_target="tpu_custom_call" | custom-call | flops 20000000000 | bytes 2097152 | tf_op jit(solution)/shard_map/deal/pallas_call | solution.py:217
  30.2 6.8 %all-to-all-start = ((bf16[16,32,1024]{2,1,0:T(8,128)(2,1)}), bf16[16,32,1024]{2,1,0:T(8,128)(2,1)S(1)}, u32[]{:S(2)}, u32[]{:S(2)}) async-start(bf16[16,32,1024]{2,1,0:T(8,128)(2,1)} %deal.1.refs_8_), calls=%async_computation | async-start | bytes 2097152 | tf_op jit(solution)/shard_map/all_to_all | solution.py:393
  37.0 0.0 collective-permute-done.7.q_ref
  37.0 5.2 %score.2 = (bf16[4096,1024]{1,0:T(8,128)(2,1)S(1)}, f32[16,1024]{1,0:T(8,128)S(1)}, f32[1,1024]{1,0:T(1,128)S(1)}) custom-call(bf16[1024,128]{1,0:T(8,128)(2,1)S(1)} %collective-permute-done.7.q_ref, bf16[784,128]{1,0:T(8,128)(2,1)S(1)} %get-tuple-element.23.refs_0_, bf16[784,128]{1,0:T(8,128)(2,1)S(1)} %collective-permute-done.3.refs_1_, ...), custom_call_target="tpu_custom_call" | custom-call | flops 8589934592 | bytes 8388608 | tf_op jit(solution)/shard_map/score/pallas_call | solution.py:296
  42.3 2.0 %collective-permute-start.10 = (f32[1,1024]{1,0:T(1,128)S(1)}, f32[1,1024]{1,0:T(1,128)S(1)}, u32[]{:S(2)}, u32[]{:S(2)}) collective-permute-start(f32[1,1024]{1,0:T(1,128)S(1)} %get-tuple-element.32.refs_8_.lse_ref), channel_id=1, source_target_pairs={{0,2},{1,3},{2,0},{3,1},{4,6},{5,7},{6,4},{7,5},{8,10},{9,11},{10,... | collective-permute-start | bytes 12296 | tf_op jit(solution)/shard_map/ppermute | solution.py:375
  44.3 5.2 %score.3 = (bf16[4096,1024]{1,0:T(8,128)(2,1)S(1)}, f32[16,1024]{1,0:T(8,128)S(1)}, f32[1,1024]{1,0:T(1,128)S(1)}) custom-call(bf16[1024,128]{1,0:T(8,128)(2,1)S(1)} %get-tuple-element.27.q_ref, bf16[784,128]{1,0:T(8,128)(2,1)S(1)} %get-tuple-element.23.refs_0_, bf16[784,128]{1,0:T(8,128)(2,1)S(1)} %collective-permute-done.3.refs_1_, ...), custom_call_target="tpu_custom_call" | custom-call | flops 8589934592 | bytes 8388608 | tf_op jit(solution)/shard_map/score/pallas_call | solution.py:296
  49.5 0.2 collective-permute-start.9
  49.7 0.0 collective-permute-done.10.rest_0_
  49.7 2.3 %weigh.2.rest_1_ = f32[16,256]{1,0:T(8,128)S(1)} custom-call(bf16[4096,1024]{1,0:T(8,128)(2,1)S(1)} %get-tuple-element.34.prob_ref, f32[16,1024]{1,0:T(8,128)S(1)} %get-tuple-element.35.top_ref, f32[1,1024]{1,0:T(1,128)S(1)} %get-tuple-element.33.lse_ref, f32[1,1024]{1,0:T(1,128)S(1)} %collective-permute-done.10.rest_0_), custom_call_target="tpu_custom_call" | custom-call | flops 16777216 | bytes 8388608 | tf_op jit(solution)/shard_map/weigh/pallas_call | solution.py:339
  52.0 1.2 %collective-permute-done.9.rest_0_ = f32[1,1024]{1,0:T(1,128)S(1)} collective-permute-done((f32[1,1024]{1,0:T(1,128)S(1)}, f32[1,1024]{1,0:T(1,128)S(1)}, u32[]{:S(2)}, u32[]{:S(2)}) %collective-permute-start.9) | collective-permute-done | bytes 4128 | tf_op jit(solution)/shard_map/ppermute | solution.py:375
  53.2 2.3 %weigh.3 = f32[16,256]{1,0:T(8,128)S(1)} custom-call(bf16[4096,1024]{1,0:T(8,128)(2,1)S(1)} %get-tuple-element.30.prob_ref, f32[16,1024]{1,0:T(8,128)S(1)} %get-tuple-element.31.top_ref, f32[1,1024]{1,0:T(1,128)S(1)} %get-tuple-element.32.refs_8_.lse_ref, f32[1,1024]{1,0:T(1,128)S(1)} %collective-permute-done.9.rest_0_, f32[16,256]{1,0:T(8,128)S(1)} %weigh.2.rest_1_), custom_call_target="tpu_custom_call" | custom-call | flops 16777216 | bytes 8388608 | tf_op jit(solution)/shard_map/weigh/pallas_call | solution.py:339
  55.5 0.1 collective-permute-start.11
  55.6 1.2 %collective-permute-done.11 = f32[4,512]{1,0:T(4,128)S(1)} collective-permute-done((f32[4,512]{1,0:T(4,128)S(1)}, f32[4,512]{1,0:T(4,128)S(1)}, u32[]{:S(2)}, u32[]{:S(2)}) %collective-permute-start.11) | collective-permute-done | bytes 8224 | tf_op jit(solution)/shard_map/ppermute | solution.py:375
  56.8 2.4 %collective-permute-start.13 = (f32[512]{0:T(512)S(1)}, f32[512]{0:T(512)S(1)}, u32[]{:S(2)}, u32[]{:S(2)}) collective-permute-start(f32[512]{0:T(512)S(1)} %bitcast.28), channel_id=1, source_target_pairs={{0,8},{1,9},{2,10},{3,11},{4,12},{5,13},{6,14},{7,15},{8,0},{9,1},... | collective-permute-start | bytes 6152 | tf_op jit(solution)/shard_map/ppermute | solution.py:375
  59.2 1.5 %collective-permute-start.14 = (f32[512]{0:T(512)S(1)}, f32[512]{0:T(512)S(1)}, u32[]{:S(2)}, u32[]{:S(2)}) collective-permute-start(f32[512]{0:T(512)S(1)} %bitcast.27), channel_id=1, source_target_pairs={{0,12},{1,13},{2,14},{3,15},{4,8},{5,9},{6,10},{7,11},{8,4},{9,5},... | collective-permute-start | bytes 6152 | tf_op jit(solution)/shard_map/ppermute | solution.py:375
  60.7 0.0 collective-permute-start.12
  60.7 0.0 all-to-all-done
  60.7 1.3 %place.1.refs_4_ = bf16[256,1024]{1,0:T(8,128)(2,1)} custom-call(s32[1]{0:T(128)} %bitcast.me_ref, s32[1,128]{1,0:T(1,128)S(1)} %get-tuple-element.28.refs_0_, s32[1,128]{1,0:T(1,128)S(1)} %collective-permute-done.8.refs_1_, bf16[512,1024]{1,0:T(8,128)(2,1)S(1)} %bitcast.19), custom_call_target="tpu_custom_call" | custom-call | flops 268435456 | bytes 1572864 | tf_op jit(solution)/shard_map/place/pallas_call | solution.py:251
  62.1 1.6 %collective-permute-done.13 = f32[512]{0:T(512)S(1)} collective-permute-done((f32[512]{0:T(512)S(1)}, f32[512]{0:T(512)S(1)}, u32[]{:S(2)}, u32[]{:S(2)}) %collective-permute-start.13) | collective-permute-done | bytes 2080 | tf_op jit(solution)/shard_map/ppermute | solution.py:375
  63.7 0.9 %collective-permute-done.14 = f32[512]{0:T(512)S(1)} collective-permute-done((f32[512]{0:T(512)S(1)}, f32[512]{0:T(512)S(1)}, u32[]{:S(2)}, u32[]{:S(2)}) %collective-permute-start.14) | collective-permute-done | bytes 2080 | tf_op jit(solution)/shard_map/ppermute | solution.py:375
  64.6 0.0 collective-permute-done.12
  64.6 0.6 finish.1
  (6 shorter events, 0.1 us)
Async XLA Ops:
  2.6 18.5 %collective-permute-start = (bf16[784,128]{1,0:T(8,128)(2,1)S(1)}, bf16[784,128]{1,0:T(8,128)(2,1)S(1)}, u32[]{:S(2)}, u32[]{:S(2)}) collective-permute-start(bf16[784,128]{1,0:T(8,128)(2,1)S(1)} %get-tuple-element.20), channel_id=1, source_target_pairs={{0,4},{1,5},{2,6},{3,7},{4,0},{5,1},{6,2},{7,3},{8,12},{9,13},{10,... | collective-permute-start | bytes 602120 | tf_op jit(solution)/shard_map/ppermute | solution.py:375
  5.7 17.4 %collective-permute-start.1 = (bf16[784,128]{1,0:T(8,128)(2,1)S(1)}, bf16[784,128]{1,0:T(8,128)(2,1)S(1)}, u32[]{:S(2)}, u32[]{:S(2)}) collective-permute-start(bf16[784,128]{1,0:T(8,128)(2,1)S(1)} %get-tuple-element.21), channel_id=1, source_target_pairs={{0,8},{1,9},{2,10},{3,11},{4,12},{5,13},{6,14},{7,15},{8,0},{9,1},... | collective-permute-start | bytes 602120 | tf_op jit(solution)/shard_map/ppermute | solution.py:375
  8.3 14.8 %collective-permute-start.2 = (bf16[784,128]{1,0:T(8,128)(2,1)S(1)}, bf16[784,128]{1,0:T(8,128)(2,1)S(1)}, u32[]{:S(2)}, u32[]{:S(2)}) collective-permute-start(bf16[784,128]{1,0:T(8,128)(2,1)S(1)} %get-tuple-element.22), channel_id=1, source_target_pairs={{0,12},{1,13},{2,14},{3,15},{4,8},{5,9},{6,10},{7,11},{8,4},{9,5},... | collective-permute-start | bytes 602120 | tf_op jit(solution)/shard_map/ppermute | solution.py:375
  8.3 11.8 %copy-start = (s32[512]{0:T(512)S(1)}, s32[512]{0:T(512)}, u32[]{:S(2)}) copy-start(s32[512]{0:T(512)} %param.12) | copy-start | bytes 6148
  23.1 1.4 %collective-permute-start.3 = (bf16[784,128]{1,0:T(8,128)(2,1)S(1)}, bf16[784,128]{1,0:T(8,128)(2,1)S(1)}, u32[]{:S(2)}, u32[]{:S(2)}) collective-permute-start(bf16[784,128]{1,0:T(8,128)(2,1)S(1)} %get-tuple-element.23.refs_0_), channel_id=1, source_target_pairs={{0,1},{1,0},{2,3},{3,2},{4,5},{5,4},{6,7},{7,6},{8,9},{9,8},{10,11... | collective-permute-start | bytes 602120 | tf_op jit(solution)/shard_map/ppermute | solution.py:375
  23.1 1.7 %collective-permute-start.4 = (bf16[784,128]{1,0:T(8,128)(2,1)S(1)}, bf16[784,128]{1,0:T(8,128)(2,1)S(1)}, u32[]{:S(2)}, u32[]{:S(2)}) collective-permute-start(bf16[784,128]{1,0:T(8,128)(2,1)S(1)} %collective-permute-done.refs_2_), channel_id=1, source_target_pairs={{0,1},{1,0},{2,3},{3,2},{4,5},{5,4},{6,7},{7,6},{8,9},{9,8},{10,11... | collective-permute-start | bytes 602120 | tf_op jit(solution)/shard_map/ppermute | solution.py:375
  23.6 1.5 %collective-permute-start.5 = (bf16[784,128]{1,0:T(8,128)(2,1)S(1)}, bf16[784,128]{1,0:T(8,128)(2,1)S(1)}, u32[]{:S(2)}, u32[]{:S(2)}) collective-permute-start(bf16[784,128]{1,0:T(8,128)(2,1)S(1)} %collective-permute-done.1.refs_4_), channel_id=1, source_target_pairs={{0,1},{1,0},{2,3},{3,2},{4,5},{5,4},{6,7},{7,6},{8,9},{9,8},{10,11... | collective-permute-start | bytes 602120 | tf_op jit(solution)/shard_map/ppermute | solution.py:375
  23.6 1.8 %collective-permute-start.6 = (bf16[784,128]{1,0:T(8,128)(2,1)S(1)}, bf16[784,128]{1,0:T(8,128)(2,1)S(1)}, u32[]{:S(2)}, u32[]{:S(2)}) collective-permute-start(bf16[784,128]{1,0:T(8,128)(2,1)S(1)} %collective-permute-done.2.refs_6_), channel_id=1, source_target_pairs={{0,1},{1,0},{2,3},{3,2},{4,5},{5,4},{6,7},{7,6},{8,9},{9,8},{10,11... | collective-permute-start | bytes 602120 | tf_op jit(solution)/shard_map/ppermute | solution.py:375
  25.4 3.6 %collective-permute-start.8 = (s32[1,128]{1,0:T(1,128)S(1)}, s32[1,128]{1,0:T(1,128)S(1)}, u32[]{:S(2)}, u32[]{:S(2)}) collective-permute-start(s32[1,128]{1,0:T(1,128)S(1)} %get-tuple-element.28.refs_0_), channel_id=1, source_target_pairs={{0,2},{1,3},{2,0},{3,1},{4,6},{5,7},{6,4},{7,5},{8,10},{9,11},{10,... | collective-permute-start | bytes 1544 | tf_op jit(solution)/shard_map/ppermute | solution.py:375
  27.0 10.0 %collective-permute-start.7 = (bf16[1024,128]{1,0:T(8,128)(2,1)S(1)}, bf16[1024,128]{1,0:T(8,128)(2,1)S(1)}, u32[]{:S(2)}, u32[]{:S(2)}) collective-permute-start(bf16[1024,128]{1,0:T(8,128)(2,1)S(1)} %get-tuple-element.27.q_ref), channel_id=1, source_target_pairs={{0,2},{1,3},{2,0},{3,1},{4,6},{5,7},{6,4},{7,5},{8,10},{9,11},{10,... | collective-permute-start | bytes 786440 | tf_op jit(solution)/shard_map/ppermute | solution.py:375
  30.2 30.5 %all-to-all-start = ((bf16[16,32,1024]{2,1,0:T(8,128)(2,1)}), bf16[16,32,1024]{2,1,0:T(8,128)(2,1)S(1)}, u32[]{:S(2)}, u32[]{:S(2)}) async-start(bf16[16,32,1024]{2,1,0:T(8,128)(2,1)} %deal.1.refs_8_), calls=%async_computation | async-start | bytes 2097152 | tf_op jit(solution)/shard_map/all_to_all | solution.py:393
  42.3 7.4 %collective-permute-start.10 = (f32[1,1024]{1,0:T(1,128)S(1)}, f32[1,1024]{1,0:T(1,128)S(1)}, u32[]{:S(2)}, u32[]{:S(2)}) collective-permute-start(f32[1,1024]{1,0:T(1,128)S(1)} %get-tuple-element.32.refs_8_.lse_ref), channel_id=1, source_target_pairs={{0,2},{1,3},{2,0},{3,1},{4,6},{5,7},{6,4},{7,5},{8,10},{9,11},{10,... | collective-permute-start | bytes 12296 | tf_op jit(solution)/shard_map/ppermute | solution.py:375
  49.5 3.7 %collective-permute-start.9 = (f32[1,1024]{1,0:T(1,128)S(1)}, f32[1,1024]{1,0:T(1,128)S(1)}, u32[]{:S(2)}, u32[]{:S(2)}) collective-permute-start(f32[1,1024]{1,0:T(1,128)S(1)} %get-tuple-element.33.lse_ref), channel_id=1, source_target_pairs={{0,2},{1,3},{2,0},{3,1},{4,6},{5,7},{6,4},{7,5},{8,10},{9,11},{10,... | collective-permute-start | bytes 12296 | tf_op jit(solution)/shard_map/ppermute | solution.py:375
  55.5 1.2 %collective-permute-start.11 = (f32[4,512]{1,0:T(4,128)S(1)}, f32[4,512]{1,0:T(4,128)S(1)}, u32[]{:S(2)}, u32[]{:S(2)}) collective-permute-start(f32[4,512]{1,0:T(4,128)S(1)} %bitcast.24), channel_id=1, source_target_pairs={{0,1},{1,0},{2,3},{3,2},{4,5},{5,4},{6,7},{7,6},{8,9},{9,8},{10,11... | collective-permute-start | bytes 24584 | tf_op jit(solution)/shard_map/ppermute | solution.py:375
  56.8 6.9 %collective-permute-start.13 = (f32[512]{0:T(512)S(1)}, f32[512]{0:T(512)S(1)}, u32[]{:S(2)}, u32[]{:S(2)}) collective-permute-start(f32[512]{0:T(512)S(1)} %bitcast.28), channel_id=1, source_target_pairs={{0,8},{1,9},{2,10},{3,11},{4,12},{5,13},{6,14},{7,15},{8,0},{9,1},... | collective-permute-start | bytes 6152 | tf_op jit(solution)/shard_map/ppermute | solution.py:375
  59.2 5.4 %collective-permute-start.14 = (f32[512]{0:T(512)S(1)}, f32[512]{0:T(512)S(1)}, u32[]{:S(2)}, u32[]{:S(2)}) collective-permute-start(f32[512]{0:T(512)S(1)} %bitcast.27), channel_id=1, source_target_pairs={{0,12},{1,13},{2,14},{3,15},{4,8},{5,9},{6,10},{7,11},{8,4},{9,5},... | collective-permute-start | bytes 6152 | tf_op jit(solution)/shard_map/ppermute | solution.py:375
  60.7 3.9 %collective-permute-start.12 = (f32[512]{0:T(512)S(1)}, f32[512]{0:T(512)S(1)}, u32[]{:S(2)}, u32[]{:S(2)}) collective-permute-start(f32[512]{0:T(512)S(1)} %bitcast.26), channel_id=1, source_target_pairs={{0,4},{1,5},{2,6},{3,7},{4,0},{5,1},{6,2},{7,3},{8,12},{9,13},{10,... | collective-permute-start | bytes 6152 | tf_op jit(solution)/shard_map/ppermute | solution.py:375

commit v7 on v6

--- a/solution.py
+++ b/solution.py
@@ -104,15 +104,19 @@
     )(*map(in_hbm, (hidden, gain.reshape(1, -1), weight, bias.reshape(1, -1))))
 
 
+def chip_steps(size):
+    return [chip * (size // CHIPS) for chip in (0, 2, 3, 1)]
+
+
 def cell_steps(size):
-    return [chip * (size // CHIPS) + core for chip in range(CHIPS) for core in range(2)]
+    return [step + core for step in chip_steps(size) for core in range(2)]
 
 
 def cross_steps(size):
     return list(range(0, size // CHIPS, 2))
 
 
-def front_kernel(stride, keys, me_ref, count_ref, keys_ref, q_ref, *out_refs):
+def front_kernel(size, keys, me_ref, count_ref, keys_ref, q_ref, *out_refs):
     me = me_ref[0]
     count = count_ref[0]
     tokens = q_ref.shape[0]
@@ -120,8 +124,8 @@
     high = lax.broadcasted_iota(jnp.int32, (EXTRA, HD), 0) < EXTRA // 2
     extra = jnp.where(high, count // 8, count % 8).astype(F32).astype(BF16)
     first = (1 - me % 2) * (heads // 2)
-    for i, out_ref in enumerate(out_refs):
-        head = (me ^ (stride * i)) // stride
+    for step, out_ref in zip(chip_steps(size), out_refs):
+        head = (me ^ step) // (size // CHIPS)
         out_ref[:keys, :] = keys_ref[:, pl.ds(pl.multiple_of(head * HD, HD), HD)]
         out_ref[keys : keys + EXTRA, :] = extra
         for h in range(heads):
@@ -133,7 +137,7 @@
 def front(me, count, keys, queries, size):
     rows = keys.shape[0] + EXTRA + queries.size // HD // CHIPS
     return pl.pallas_call(
-        functools.partial(front_kernel, size // CHIPS, keys.shape[0]),
+        functools.partial(front_kernel, size, keys.shape[0]),
         in_specs=[SMEM] * 2 + [VMEM] * 2,
         out_specs=[VMEM] * CHIPS,
         out_shape=[jax.ShapeDtypeStruct((rows, HD), BF16)] * CHIPS,
@@ -203,12 +207,11 @@
     count_refs, (rows_ref, out_ref) = refs[:-2], refs[-2:]
     me = me_ref[0]
     size = rows_ref.shape[0]
-    lane = lax.broadcasted_iota(jnp.int32, (1, HD), 1)
-    here = me ^ ((lane >> 1) * (size // CHIPS) + (lane & 1))
-    start = jnp.int32(0)
-    for step, ref in zip(cross_steps(size), count_refs):
-        before = (lane < CELL) & ((here ^ step) < me)
-        start += jnp.sum(jnp.where(before, ref[...], 0))
+    start = jnp.zeros((1, 1), jnp.int32)
+    for cross, ref in zip(cross_steps(size), count_refs):
+        for lane, step in enumerate(cell_steps(size)):
+            start += jnp.where((me ^ cross ^ step) < me, ref[:, lane : lane + 1], 0)
+    start = jnp.sum(start)
     for owner in range(size):
         out_ref[owner] = rows_ref[(owner - start) & (size - 1)]
 
@@ -308,7 +311,7 @@
     )(q, *blocks, after)
 
 
-def weigh_kernel(factor, cells, prob_ref, top_ref, lse_ref, *rest):
+def weigh_kernel(factor, cells, vector, prob_ref, top_ref, lse_ref, *rest):
     others, earlier, out_ref = rest[: cells - 1], rest[cells - 1 : -1], rest[-1]
     mine = lse_ref[...]
     top = functools.reduce(jnp.maximum, [ref[...] for ref in others], mine)
@@ -320,24 +323,37 @@
     high = weight.astype(BF16).astype(F32)
     low = weight - high
     chunk = out_ref.shape[1]
+    ones = jnp.ones((8, 128), BF16)
     for c in range(out_ref.shape[0]):
-        both = jnp.concatenate([high[c : c + 1], low[c : c + 1]], axis=0).astype(BF16)
-        got = lax.dot_general(
-            both,
-            prob_ref[c * chunk : (c + 1) * chunk, :],
-            (((1,), (1,)), ((), ())),
-            preferred_element_type=F32,
-        )
-        got = jnp.sum(got, axis=0, keepdims=True)
+        keys = pl.ds(c * chunk, chunk)
+        if c * vector % 8 < vector:
+            sums = jnp.zeros((chunk, 128), F32)
+            for at in range(0, prob_ref.shape[1], 128):
+                rows = slice(at, at + 128)
+                sums += prob_ref[keys, rows].astype(F32) * weight[c : c + 1, rows]
+            sums_high = sums.astype(BF16)
+            sums_low = (sums - sums_high.astype(F32)).astype(BF16)
+            got = sum(
+                lax.dot_general(
+                    ones, part, (((1,), (1,)), ((), ())), preferred_element_type=F32
+                )[:1]
+                for part in (sums_high, sums_low)
+            )
+        else:
+            both = jnp.concatenate([high[c : c + 1], low[c : c + 1]], axis=0).astype(BF16)
+            got = lax.dot_general(
+                both, prob_ref[keys, :], (((1,), (1,)), ((), ())), preferred_element_type=F32
+            )
+            got = jnp.sum(got, axis=0, keepdims=True)
         out_ref[c : c + 1, :] = sum([ref[c : c + 1, :] for ref in earlier], got)
 
 
-def weigh(prob, tops, lse, others, factor, earlier):
+def weigh(prob, tops, lse, others, factor, earlier, vector=5):
     keys, rows = prob.shape
     earlier = [] if earlier is None else [earlier]
     chunks = tops.shape[0]
     return pl.pallas_call(
-        functools.partial(weigh_kernel, factor, 1 + len(others)),
+        functools.partial(weigh_kernel, factor, 1 + len(others), vector),
         in_specs=[VMEM] * (3 + len(others) + len(earlier)),
         out_specs=VMEM,
         out_shape=jax.ShapeDtypeStruct((chunks, keys // chunks), F32),
@@ -374,7 +390,7 @@
     def swap(x, r):
         return lax.ppermute(x, "seq", [(i, i ^ r) for i in range(size)])
 
-    far = [chip * (size // CHIPS) for chip in range(1, CHIPS)]
+    far = chip_steps(size)[1:]
     evens = front(me, keep_count, visual_keys, queries, size)
     evens = [evens[0]] + [swap(block, r) for block, r in zip(evens[1:], far)]
 

time: 65.4 us -> 64.8 us (level)
  starting transfers between devices: 21.8 us -> 23.5 us
  waiting for transfers between devices: 9.66 us -> 8.23 us
  Pallas kernels: 32.3 us -> 31.5 us
    ppermute x15, waiting for transfers between devices: 9.66 us -> 8.22 us  [swap(): return lax.ppermute(x, 'seq', [(i, i ^ r) for i in range(size)])]
    all_to_all x1, starting transfers between devices: 6.79 us -> 7.95 us  [shards(): lax.all_to_all(picked, 'seq', split_axis=0, concat_axis=0, tiled=True)]
    pallas_call x3, Pallas kernels: 5.87 us -> 4.99 us  [the longest x2 3.7 us: weigh(): pl.pallas_call(functools.partial(weigh_kernel, factor, 1 + len(others), v...]
  transfers between devices with their start and end apart: 16 -> 16, of which waited for: 10 -> 10; matrix products, arithmetic and copies ran while one was open for 0% -> 0% of each run, Pallas kernels for 47% -> 46%
where the time goes in v7:
time: 64.8 us; the launch traced here: 64.6 us
  Pallas kernels  31.5 us (49%)
  starting transfers between devices  23.5 us (36%)
  waiting for transfers between devices  8.23 us (13%)
  between operations  1.4 us (2%)
    ppermute x15, starting transfers between devices, swap(): return lax.ppermute(x, 'seq', [(i, i ^ r) for i in range(size)])  15.5 us
    pallas_call x1, Pallas kernels, project(): pl.pallas_call(functools.partial(project_kernel, cuts), in_specs=[ANY] *...  11.8 us
    pallas_call x2, Pallas kernels, score(): pl.pallas_call(functools.partial(score_kernel, keys, chunk, tile), in_spe...  10.5 us
    ppermute x15, waiting for transfers between devices, swap(): return lax.ppermute(x, 'seq', [(i, i ^ r) for i in range(size)])  8.22 us
    all_to_all x1, starting transfers between devices, shards(): lax.all_to_all(picked, 'seq', split_axis=0, concat_axis=0, tiled=True)  7.95 us
    pallas_call x2, Pallas kernels, weigh(): pl.pallas_call(functools.partial(weigh_kernel, factor, 1 + len(others), v...  3.7 us
    pallas_call x1, Pallas kernels, place(): pl.pallas_call(functools.partial(place_kernel, size), in_specs=[SMEM] + [...  1.35 us
  transfers between devices with their start and end apart: 16, of which 10 were waited for; matrix products, arithmetic and copies ran while one was open for 0% of the time, Pallas kernels for 46%

profile of v7, /device:TPU:0, one launch (start us, length us, event | category | flops | bytes accessed | tf_op | source)
XLA Modules:
  0.0 64.6 jit_solution(15958298519121169413)
XLA Ops:
  1.3 1.3 %front.1 = (bf16[784,128]{1,0:T(8,128)(2,1)S(1)}, bf16[784,128]{1,0:T(8,128)(2,1)S(1)}, bf16[784,128]{1,0:T(8,128)(2,1)S(1)}, bf16[784,128]{1,0:T(8,128)(2,1)S(1)}) custom-call(s32[1]{0:T(128)} %bitcast.me_ref, s32[1]{0:T(128)S(6)} %copy.19.count_ref, bf16[512,512]{1,0:T(8,128)(2,1)} %keys_ref.1, bf16[32,4096]{1,0:T(8,128)(2,1)} %q_ref.1), custom_call_target="tpu_custom_call" | custom-call | bytes 1572864 | tf_op jit(solution)/shard_map/front/pallas_call | solution.py:139
  2.6 4.1 %collective-permute-start = (bf16[784,128]{1,0:T(8,128)(2,1)S(1)}, bf16[784,128]{1,0:T(8,128)(2,1)S(1)}, u32[]{:S(2)}, u32[]{:S(2)}) collective-permute-start(bf16[784,128]{1,0:T(8,128)(2,1)S(1)} %get-tuple-element.20), channel_id=1, source_target_pairs={{0,8},{1,9},{2,10},{3,11},{4,12},{5,13},{6,14},{7,15},{8,0},{9,1},... | collective-permute-start | bytes 602120 | tf_op jit(solution)/shard_map/ppermute | solution.py:391
  6.7 1.3 %collective-permute-start.1 = (bf16[784,128]{1,0:T(8,128)(2,1)S(1)}, bf16[784,128]{1,0:T(8,128)(2,1)S(1)}, u32[]{:S(2)}, u32[]{:S(2)}) collective-permute-start(bf16[784,128]{1,0:T(8,128)(2,1)S(1)} %get-tuple-element.21), channel_id=1, source_target_pairs={{0,12},{1,13},{2,14},{3,15},{4,8},{5,9},{6,10},{7,11},{8,4},{9,5},... | collective-permute-start | bytes 602120 | tf_op jit(solution)/shard_map/ppermute | solution.py:391
  8.0 0.2 collective-permute-start.2
  8.3 0.0 copy-start
  8.3 11.8 %project.1.rows_ref = bf16[512,1024]{1,0:T(8,128)(2,1)S(1)} custom-call(bf16[512,8192]{1,0:T(8,128)(2,1)} %x_hbm.1, f32[1,8192]{1,0:T(1,128)} %bitcast.29, bf16[8192,1024]{1,0:T(8,128)(2,1)} %weight_hbm.1, f32[1,1024]{1,0:T(1,128)} %bitcast.30), custom_call_target="tpu_custom_call" | custom-call | flops 8589934592 | bytes 25165824 | tf_op jit(solution)/shard_map/project/pallas_call | solution.py:88
  20.1 0.0 copy-done
  20.1 1.0 %choose.1.refs_2_ = bf16[16,32,1024]{2,1,0:T(8,128)(2,1)S(1)} custom-call(s32[1,512]{1,0:T(1,128)S(1)} %bitcast.23, bf16[512,1024]{1,0:T(8,128)(2,1)S(1)} %project.1.rows_ref), custom_call_target="tpu_custom_call" | custom-call | flops 805306368 | bytes 2097152 | tf_op jit(solution)/shard_map/choose/pallas_call | solution.py:195
  21.1 0.0 collective-permute-done.refs_2_
  21.1 0.0 collective-permute-done.1.refs_4_
  21.1 0.5 collective-permute-done.2.refs_6_
  21.7 0.0 collective-permute-start.3
  21.7 0.5 collective-permute-start.4
  22.2 0.0 collective-permute-start.5
  22.2 0.5 collective-permute-start.6
  22.7 0.4 collective-permute-done.3.refs_1_
  23.1 0.3 collective-permute-done.4.refs_3_
  23.4 0.3 collective-permute-done.5.refs_5_
  23.7 0.3 collective-permute-done.6.refs_7_
  24.0 1.6 %collective-permute-start.8 = (s32[1,128]{1,0:T(1,128)S(1)}, s32[1,128]{1,0:T(1,128)S(1)}, u32[]{:S(2)}, u32[]{:S(2)}) collective-permute-start(s32[1,128]{1,0:T(1,128)S(1)} %get-tuple-element.28.refs_0_), channel_id=1, source_target_pairs={{0,2},{1,3},{2,0},{3,1},{4,6},{5,7},{6,4},{7,5},{8,10},{9,11},{10,... | collective-permute-start | bytes 1544 | tf_op jit(solution)/shard_map/ppermute | solution.py:391
  25.6 0.5 collective-permute-start.7
  26.1 1.5 %collective-permute-done.8.refs_1_ = s32[1,128]{1,0:T(1,128)S(1)} collective-permute-done((s32[1,128]{1,0:T(1,128)S(1)}, s32[1,128]{1,0:T(1,128)S(1)}, u32[]{:S(2)}, u32[]{:S(2)}) %collective-permute-start.8) | collective-permute-done | bytes 544 | tf_op jit(solution)/shard_map/ppermute | solution.py:391
  27.6 1.3 %deal.1.refs_8_ = bf16[16,32,1024]{2,1,0:T(8,128)(2,1)} custom-call(s32[1]{0:T(128)} %bitcast.me_ref, s32[1,128]{1,0:T(1,128)S(1)} %get-tuple-element.28.refs_0_, s32[1,128]{1,0:T(1,128)S(1)} %collective-permute-done.8.refs_1_, bf16[16,32,1024]{2,1,0:T(8,128)(2,1)S(1)} %choose.1.refs_2_), custom_call_target="tpu_custom_call" | custom-call | flops 20000000000 | bytes 2097152 | tf_op jit(solution)/shard_map/deal/pallas_call | solution.py:220
  28.9 7.9 %all-to-all-start = ((bf16[16,32,1024]{2,1,0:T(8,128)(2,1)}), bf16[16,32,1024]{2,1,0:T(8,128)(2,1)S(1)}, u32[]{:S(2)}, u32[]{:S(2)}) async-start(bf16[16,32,1024]{2,1,0:T(8,128)(2,1)} %deal.1.refs_8_), calls=%async_computation | async-start | bytes 2097152 | tf_op jit(solution)/shard_map/all_to_all | solution.py:409
  36.8 0.0 collective-permute-done.7.q_ref
  36.8 5.2 %score.2 = (bf16[4096,1024]{1,0:T(8,128)(2,1)S(1)}, f32[16,1024]{1,0:T(8,128)S(1)}, f32[1,1024]{1,0:T(1,128)S(1)}) custom-call(bf16[1024,128]{1,0:T(8,128)(2,1)S(1)} %collective-permute-done.7.q_ref, bf16[784,128]{1,0:T(8,128)(2,1)S(1)} %get-tuple-element.23.refs_0_, bf16[784,128]{1,0:T(8,128)(2,1)S(1)} %collective-permute-done.3.refs_1_, ...), custom_call_target="tpu_custom_call" | custom-call | flops 8589934592 | bytes 8388608 | tf_op jit(solution)/shard_map/score/pallas_call | solution.py:299
  42.1 2.0 %collective-permute-start.10 = (f32[1,1024]{1,0:T(1,128)S(1)}, f32[1,1024]{1,0:T(1,128)S(1)}, u32[]{:S(2)}, u32[]{:S(2)}) collective-permute-start(f32[1,1024]{1,0:T(1,128)S(1)} %get-tuple-element.32.refs_8_.lse_ref), channel_id=1, source_target_pairs={{0,2},{1,3},{2,0},{3,1},{4,6},{5,7},{6,4},{7,5},{8,10},{9,11},{10,... | collective-permute-start | bytes 12296 | tf_op jit(solution)/shard_map/ppermute | solution.py:391
  44.0 5.2 %score.3 = (bf16[4096,1024]{1,0:T(8,128)(2,1)S(1)}, f32[16,1024]{1,0:T(8,128)S(1)}, f32[1,1024]{1,0:T(1,128)S(1)}) custom-call(bf16[1024,128]{1,0:T(8,128)(2,1)S(1)} %get-tuple-element.27.q_ref, bf16[784,128]{1,0:T(8,128)(2,1)S(1)} %get-tuple-element.23.refs_0_, bf16[784,128]{1,0:T(8,128)(2,1)S(1)} %collective-permute-done.3.refs_1_, ...), custom_call_target="tpu_custom_call" | custom-call | flops 8589934592 | bytes 8388608 | tf_op jit(solution)/shard_map/score/pallas_call | solution.py:299
  49.3 0.2 collective-permute-start.9
  49.5 0.0 collective-permute-done.10.rest_0_
  49.5 1.8 %weigh.2.rest_1_ = f32[16,256]{1,0:T(8,128)S(1)} custom-call(bf16[4096,1024]{1,0:T(8,128)(2,1)S(1)} %get-tuple-element.34.prob_ref, f32[16,1024]{1,0:T(8,128)S(1)} %get-tuple-element.35.top_ref, f32[1,1024]{1,0:T(1,128)S(1)} %get-tuple-element.33.lse_ref, f32[1,1024]{1,0:T(1,128)S(1)} %collective-permute-done.10.rest_0_), custom_call_target="tpu_custom_call" | custom-call | flops 16777216 | bytes 8388608 | tf_op jit(solution)/shard_map/weigh/pallas_call | solution.py:355
  51.3 1.7 %collective-permute-done.9.rest_0_ = f32[1,1024]{1,0:T(1,128)S(1)} collective-permute-done((f32[1,1024]{1,0:T(1,128)S(1)}, f32[1,1024]{1,0:T(1,128)S(1)}, u32[]{:S(2)}, u32[]{:S(2)}) %collective-permute-start.9) | collective-permute-done | bytes 4128 | tf_op jit(solution)/shard_map/ppermute | solution.py:391
  52.9 1.9 %weigh.3 = f32[16,256]{1,0:T(8,128)S(1)} custom-call(bf16[4096,1024]{1,0:T(8,128)(2,1)S(1)} %get-tuple-element.30.prob_ref, f32[16,1024]{1,0:T(8,128)S(1)} %get-tuple-element.31.top_ref, f32[1,1024]{1,0:T(1,128)S(1)} %get-tuple-element.32.refs_8_.lse_ref, f32[1,1024]{1,0:T(1,128)S(1)} %collective-permute-done.9.rest_0_, f32[16,256]{1,0:T(8,128)S(1)} %weigh.2.rest_1_), custom_call_target="tpu_custom_call" | custom-call | flops 16777216 | bytes 8388608 | tf_op jit(solution)/shard_map/weigh/pallas_call | solution.py:355
  54.9 0.1 collective-permute-start.11
  55.0 1.2 %collective-permute-done.11 = f32[4,512]{1,0:T(4,128)S(1)} collective-permute-done((f32[4,512]{1,0:T(4,128)S(1)}, f32[4,512]{1,0:T(4,128)S(1)}, u32[]{:S(2)}, u32[]{:S(2)}) %collective-permute-start.11) | collective-permute-done | bytes 8224 | tf_op jit(solution)/shard_map/ppermute | solution.py:391
  56.2 3.4 %collective-permute-start.13 = (f32[512]{0:T(512)S(1)}, f32[512]{0:T(512)S(1)}, u32[]{:S(2)}, u32[]{:S(2)}) collective-permute-start(f32[512]{0:T(512)S(1)} %bitcast.28), channel_id=1, source_target_pairs={{0,12},{1,13},{2,14},{3,15},{4,8},{5,9},{6,10},{7,11},{8,4},{9,5},... | collective-permute-start | bytes 6152 | tf_op jit(solution)/shard_map/ppermute | solution.py:391
  59.5 0.0 collective-permute-start.14
  59.5 1.1 %collective-permute-start.12 = (f32[512]{0:T(512)S(1)}, f32[512]{0:T(512)S(1)}, u32[]{:S(2)}, u32[]{:S(2)}) collective-permute-start(f32[512]{0:T(512)S(1)} %bitcast.26), channel_id=1, source_target_pairs={{0,8},{1,9},{2,10},{3,11},{4,12},{5,13},{6,14},{7,15},{8,0},{9,1},... | collective-permute-start | bytes 6152 | tf_op jit(solution)/shard_map/ppermute | solution.py:391
  60.6 0.0 all-to-all-done
  60.6 1.3 %place.1.refs_4_ = bf16[256,1024]{1,0:T(8,128)(2,1)} custom-call(s32[1]{0:T(128)} %bitcast.me_ref, s32[1,128]{1,0:T(1,128)S(1)} %get-tuple-element.28.refs_0_, s32[1,128]{1,0:T(1,128)S(1)} %collective-permute-done.8.refs_1_, bf16[512,1024]{1,0:T(8,128)(2,1)S(1)} %bitcast.19), custom_call_target="tpu_custom_call" | custom-call | flops 268435456 | bytes 1572864 | tf_op jit(solution)/shard_map/place/pallas_call | solution.py:254
  62.0 0.0 collective-permute-done.13
  62.0 1.1 %collective-permute-done.14 = f32[512]{0:T(512)S(1)} collective-permute-done((f32[512]{0:T(512)S(1)}, f32[512]{0:T(512)S(1)}, u32[]{:S(2)}, u32[]{:S(2)}) %collective-permute-start.14) | collective-permute-done | bytes 2080 | tf_op jit(solution)/shard_map/ppermute | solution.py:391
  63.1 0.9 %collective-permute-done.12 = f32[512]{0:T(512)S(1)} collective-permute-done((f32[512]{0:T(512)S(1)}, f32[512]{0:T(512)S(1)}, u32[]{:S(2)}, u32[]{:S(2)}) %collective-permute-start.12) | collective-permute-done | bytes 2080 | tf_op jit(solution)/shard_map/ppermute | solution.py:391
  64.0 0.6 finish.1
  (6 shorter events, 0.1 us)
Async XLA Ops:
  2.6 18.6 %collective-permute-start = (bf16[784,128]{1,0:T(8,128)(2,1)S(1)}, bf16[784,128]{1,0:T(8,128)(2,1)S(1)}, u32[]{:S(2)}, u32[]{:S(2)}) collective-permute-start(bf16[784,128]{1,0:T(8,128)(2,1)S(1)} %get-tuple-element.20), channel_id=1, source_target_pairs={{0,8},{1,9},{2,10},{3,11},{4,12},{5,13},{6,14},{7,15},{8,0},{9,1},... | collective-permute-start | bytes 602120 | tf_op jit(solution)/shard_map/ppermute | solution.py:391
  6.7 14.5 %collective-permute-start.1 = (bf16[784,128]{1,0:T(8,128)(2,1)S(1)}, bf16[784,128]{1,0:T(8,128)(2,1)S(1)}, u32[]{:S(2)}, u32[]{:S(2)}) collective-permute-start(bf16[784,128]{1,0:T(8,128)(2,1)S(1)} %get-tuple-element.21), channel_id=1, source_target_pairs={{0,12},{1,13},{2,14},{3,15},{4,8},{5,9},{6,10},{7,11},{8,4},{9,5},... | collective-permute-start | bytes 602120 | tf_op jit(solution)/shard_map/ppermute | solution.py:391
  8.0 13.6 %collective-permute-start.2 = (bf16[784,128]{1,0:T(8,128)(2,1)S(1)}, bf16[784,128]{1,0:T(8,128)(2,1)S(1)}, u32[]{:S(2)}, u32[]{:S(2)}) collective-permute-start(bf16[784,128]{1,0:T(8,128)(2,1)S(1)} %get-tuple-element.22), channel_id=1, source_target_pairs={{0,4},{1,5},{2,6},{3,7},{4,0},{5,1},{6,2},{7,3},{8,12},{9,13},{10,... | collective-permute-start | bytes 602120 | tf_op jit(solution)/shard_map/ppermute | solution.py:391
  8.3 11.8 %copy-start = (s32[512]{0:T(512)S(1)}, s32[512]{0:T(512)}, u32[]{:S(2)}) copy-start(s32[512]{0:T(512)} %param.12) | copy-start | bytes 6148
  21.7 1.4 %collective-permute-start.3 = (bf16[784,128]{1,0:T(8,128)(2,1)S(1)}, bf16[784,128]{1,0:T(8,128)(2,1)S(1)}, u32[]{:S(2)}, u32[]{:S(2)}) collective-permute-start(bf16[784,128]{1,0:T(8,128)(2,1)S(1)} %get-tuple-element.23.refs_0_), channel_id=1, source_target_pairs={{0,1},{1,0},{2,3},{3,2},{4,5},{5,4},{6,7},{7,6},{8,9},{9,8},{10,11... | collective-permute-start | bytes 602120 | tf_op jit(solution)/shard_map/ppermute | solution.py:391
  21.7 1.7 %collective-permute-start.4 = (bf16[784,128]{1,0:T(8,128)(2,1)S(1)}, bf16[784,128]{1,0:T(8,128)(2,1)S(1)}, u32[]{:S(2)}, u32[]{:S(2)}) collective-permute-start(bf16[784,128]{1,0:T(8,128)(2,1)S(1)} %collective-permute-done.refs_2_), channel_id=1, source_target_pairs={{0,1},{1,0},{2,3},{3,2},{4,5},{5,4},{6,7},{7,6},{8,9},{9,8},{10,11... | collective-permute-start | bytes 602120 | tf_op jit(solution)/shard_map/ppermute | solution.py:391
  22.2 1.5 %collective-permute-start.5 = (bf16[784,128]{1,0:T(8,128)(2,1)S(1)}, bf16[784,128]{1,0:T(8,128)(2,1)S(1)}, u32[]{:S(2)}, u32[]{:S(2)}) collective-permute-start(bf16[784,128]{1,0:T(8,128)(2,1)S(1)} %collective-permute-done.1.refs_4_), channel_id=1, source_target_pairs={{0,1},{1,0},{2,3},{3,2},{4,5},{5,4},{6,7},{7,6},{8,9},{9,8},{10,11... | collective-permute-start | bytes 602120 | tf_op jit(solution)/shard_map/ppermute | solution.py:391
  22.2 1.8 %collective-permute-start.6 = (bf16[784,128]{1,0:T(8,128)(2,1)S(1)}, bf16[784,128]{1,0:T(8,128)(2,1)S(1)}, u32[]{:S(2)}, u32[]{:S(2)}) collective-permute-start(bf16[784,128]{1,0:T(8,128)(2,1)S(1)} %collective-permute-done.2.refs_6_), channel_id=1, source_target_pairs={{0,1},{1,0},{2,3},{3,2},{4,5},{5,4},{6,7},{7,6},{8,9},{9,8},{10,11... | collective-permute-start | bytes 602120 | tf_op jit(solution)/shard_map/ppermute | solution.py:391
  24.0 3.6 %collective-permute-start.8 = (s32[1,128]{1,0:T(1,128)S(1)}, s32[1,128]{1,0:T(1,128)S(1)}, u32[]{:S(2)}, u32[]{:S(2)}) collective-permute-start(s32[1,128]{1,0:T(1,128)S(1)} %get-tuple-element.28.refs_0_), channel_id=1, source_target_pairs={{0,2},{1,3},{2,0},{3,1},{4,6},{5,7},{6,4},{7,5},{8,10},{9,11},{10,... | collective-permute-start | bytes 1544 | tf_op jit(solution)/shard_map/ppermute | solution.py:391
  25.6 11.2 %collective-permute-start.7 = (bf16[1024,128]{1,0:T(8,128)(2,1)S(1)}, bf16[1024,128]{1,0:T(8,128)(2,1)S(1)}, u32[]{:S(2)}, u32[]{:S(2)}) collective-permute-start(bf16[1024,128]{1,0:T(8,128)(2,1)S(1)} %get-tuple-element.27.q_ref), channel_id=1, source_target_pairs={{0,2},{1,3},{2,0},{3,1},{4,6},{5,7},{6,4},{7,5},{8,10},{9,11},{10,... | collective-permute-start | bytes 786440 | tf_op jit(solution)/shard_map/ppermute | solution.py:391
  28.9 31.8 %all-to-all-start = ((bf16[16,32,1024]{2,1,0:T(8,128)(2,1)}), bf16[16,32,1024]{2,1,0:T(8,128)(2,1)S(1)}, u32[]{:S(2)}, u32[]{:S(2)}) async-start(bf16[16,32,1024]{2,1,0:T(8,128)(2,1)} %deal.1.refs_8_), calls=%async_computation | async-start | bytes 2097152 | tf_op jit(solution)/shard_map/all_to_all | solution.py:409
  42.1 7.4 %collective-permute-start.10 = (f32[1,1024]{1,0:T(1,128)S(1)}, f32[1,1024]{1,0:T(1,128)S(1)}, u32[]{:S(2)}, u32[]{:S(2)}) collective-permute-start(f32[1,1024]{1,0:T(1,128)S(1)} %get-tuple-element.32.refs_8_.lse_ref), channel_id=1, source_target_pairs={{0,2},{1,3},{2,0},{3,1},{4,6},{5,7},{6,4},{7,5},{8,10},{9,11},{10,... | collective-permute-start | bytes 12296 | tf_op jit(solution)/shard_map/ppermute | solution.py:391
  49.3 3.7 %collective-permute-start.9 = (f32[1,1024]{1,0:T(1,128)S(1)}, f32[1,1024]{1,0:T(1,128)S(1)}, u32[]{:S(2)}, u32[]{:S(2)}) collective-permute-start(f32[1,1024]{1,0:T(1,128)S(1)} %get-tuple-element.33.lse_ref), channel_id=1, source_target_pairs={{0,2},{1,3},{2,0},{3,1},{4,6},{5,7},{6,4},{7,5},{8,10},{9,11},{10,... | collective-permute-start | bytes 12296 | tf_op jit(solution)/shard_map/ppermute | solution.py:391
  54.9 1.2 %collective-permute-start.11 = (f32[4,512]{1,0:T(4,128)S(1)}, f32[4,512]{1,0:T(4,128)S(1)}, u32[]{:S(2)}, u32[]{:S(2)}) collective-permute-start(f32[4,512]{1,0:T(4,128)S(1)} %bitcast.24), channel_id=1, source_target_pairs={{0,1},{1,0},{2,3},{3,2},{4,5},{5,4},{6,7},{7,6},{8,9},{9,8},{10,11... | collective-permute-start | bytes 24584 | tf_op jit(solution)/shard_map/ppermute | solution.py:391
  56.2 5.8 %collective-permute-start.13 = (f32[512]{0:T(512)S(1)}, f32[512]{0:T(512)S(1)}, u32[]{:S(2)}, u32[]{:S(2)}) collective-permute-start(f32[512]{0:T(512)S(1)} %bitcast.28), channel_id=1, source_target_pairs={{0,12},{1,13},{2,14},{3,15},{4,8},{5,9},{6,10},{7,11},{8,4},{9,5},... | collective-permute-start | bytes 6152 | tf_op jit(solution)/shard_map/ppermute | solution.py:391
  59.5 3.6 %collective-permute-start.14 = (f32[512]{0:T(512)S(1)}, f32[512]{0:T(512)S(1)}, u32[]{:S(2)}, u32[]{:S(2)}) collective-permute-start(f32[512]{0:T(512)S(1)} %bitcast.27), channel_id=1, source_target_pairs={{0,4},{1,5},{2,6},{3,7},{4,0},{5,1},{6,2},{7,3},{8,12},{9,13},{10,... | collective-permute-start | bytes 6152 | tf_op jit(solution)/shard_map/ppermute | solution.py:391
  59.5 4.5 %collective-permute-start.12 = (f32[512]{0:T(512)S(1)}, f32[512]{0:T(512)S(1)}, u32[]{:S(2)}, u32[]{:S(2)}) collective-permute-start(f32[512]{0:T(512)S(1)} %bitcast.26), channel_id=1, source_target_pairs={{0,8},{1,9},{2,10},{3,11},{4,12},{5,13},{6,14},{7,15},{8,0},{9,1},... | collective-permute-start | bytes 6152 | tf_op jit(solution)/shard_map/ppermute | solution.py:391

commit v8 on v7

--- a/solution.py
+++ b/solution.py
@@ -396,8 +396,10 @@
 
     projected = project(hidden, norm_gain, kv_weight, kv_bias)
     chosen = choose(keep_index, projected, size)
-    *evens, chosen = lax.optimization_barrier((*evens, chosen))
-    odds = [swap(block, 1) for block in evens]
+    odds = [swap(evens[0], 1)]
+    for i in range(1, CHIPS):
+        evens[i], chosen = lax.optimization_barrier((evens[i], chosen))
+        odds.append(swap(evens[i], 1))
     blocks = [block for pair in zip(evens, odds) for block in pair]
 
     steps = cross_steps(size)

time: 64.8 us -> 64.6 us (level)
  transfers between devices with their start and end apart: 16 -> 16, of which waited for: 10 -> 9; matrix products, arithmetic and copies ran while one was open for 0% -> 0% of each run, Pallas kernels for 46% -> 46%
where the time goes in v8:
time: 64.6 us; the launch traced here: 64.3 us
  Pallas kernels  31.5 us (49%)
  starting transfers between devices  23 us (36%)
  waiting for transfers between devices  8.43 us (13%)
  between operations  1.4 us (2%)
    ppermute x15, starting transfers between devices, swap(): return lax.ppermute(x, 'seq', [(i, i ^ r) for i in range(size)])  15 us
    pallas_call x1, Pallas kernels, project(): pl.pallas_call(functools.partial(project_kernel, cuts), in_specs=[ANY] *...  11.8 us
    pallas_call x2, Pallas kernels, score(): pl.pallas_call(functools.partial(score_kernel, keys, chunk, tile), in_spe...  10.5 us
    ppermute x15, waiting for transfers between devices, swap(): return lax.ppermute(x, 'seq', [(i, i ^ r) for i in range(size)])  8.42 us
    all_to_all x1, starting transfers between devices, shards(): lax.all_to_all(picked, 'seq', split_axis=0, concat_axis=0, tiled=True)  7.95 us
    pallas_call x2, Pallas kernels, weigh(): pl.pallas_call(functools.partial(weigh_kernel, factor, 1 + len(others), v...  3.7 us
    pallas_call x1, Pallas kernels, place(): pl.pallas_call(functools.partial(place_kernel, size), in_specs=[SMEM] + [...  1.35 us
    pallas_call x1, Pallas kernels, front(): pl.pallas_call(functools.partial(front_kernel, size, keys.shape[0]), in_s...  1.29 us
  transfers between devices with their start and end apart: 16, of which 9 were waited for; matrix products, arithmetic and copies ran while one was open for 0% of the time, Pallas kernels for 46%

profile of v8, /device:TPU:0, one launch (start us, length us, event | category | flops | bytes accessed | tf_op | source)
XLA Modules:
  0.0 64.3 jit_solution(17800930842436700959)
XLA Ops:
  1.3 1.3 %front.1 = (bf16[784,128]{1,0:T(8,128)(2,1)S(1)}, bf16[784,128]{1,0:T(8,128)(2,1)S(1)}, bf16[784,128]{1,0:T(8,128)(2,1)S(1)}, bf16[784,128]{1,0:T(8,128)(2,1)S(1)}) custom-call(s32[1]{0:T(128)} %bitcast.me_ref, s32[1]{0:T(128)S(6)} %copy.19.count_ref, bf16[512,512]{1,0:T(8,128)(2,1)} %keys_ref.1, bf16[32,4096]{1,0:T(8,128)(2,1)} %q_ref.1), custom_call_target="tpu_custom_call" | custom-call | bytes 1572864 | tf_op jit(solution)/shard_map/front/pallas_call | solution.py:139
  2.6 4.1 %collective-permute-start.1 = (bf16[784,128]{1,0:T(8,128)(2,1)S(1)}, bf16[784,128]{1,0:T(8,128)(2,1)S(1)}, u32[]{:S(2)}, u32[]{:S(2)}) collective-permute-start(bf16[784,128]{1,0:T(8,128)(2,1)S(1)} %get-tuple-element.21), channel_id=1, source_target_pairs={{0,8},{1,9},{2,10},{3,11},{4,12},{5,13},{6,14},{7,15},{8,0},{9,1},... | collective-permute-start | bytes 602120 | tf_op jit(solution)/shard_map/ppermute | solution.py:391
  6.7 1.3 %collective-permute-start.3 = (bf16[784,128]{1,0:T(8,128)(2,1)S(1)}, bf16[784,128]{1,0:T(8,128)(2,1)S(1)}, u32[]{:S(2)}, u32[]{:S(2)}) collective-permute-start(bf16[784,128]{1,0:T(8,128)(2,1)S(1)} %get-tuple-element.23), channel_id=1, source_target_pairs={{0,12},{1,13},{2,14},{3,15},{4,8},{5,9},{6,10},{7,11},{8,4},{9,5},... | collective-permute-start | bytes 602120 | tf_op jit(solution)/shard_map/ppermute | solution.py:391
  8.0 0.2 collective-permute-start.5
  8.3 0.0 collective-permute-start
  8.3 0.0 copy-start
  8.3 11.8 %project.1.rows_ref = bf16[512,1024]{1,0:T(8,128)(2,1)S(1)} custom-call(bf16[512,8192]{1,0:T(8,128)(2,1)} %x_hbm.1, f32[1,8192]{1,0:T(1,128)} %bitcast.29, bf16[8192,1024]{1,0:T(8,128)(2,1)} %weight_hbm.1, f32[1,1024]{1,0:T(1,128)} %bitcast.30), custom_call_target="tpu_custom_call" | custom-call | flops 8589934592 | bytes 25165824 | tf_op jit(solution)/shard_map/project/pallas_call | solution.py:88
  20.1 0.0 copy-done
  20.1 1.0 %choose.1.refs_2_ = bf16[16,32,1024]{2,1,0:T(8,128)(2,1)S(1)} custom-call(s32[1,512]{1,0:T(1,128)S(1)} %bitcast.23, bf16[512,1024]{1,0:T(8,128)(2,1)S(1)} %project.1.rows_ref), custom_call_target="tpu_custom_call" | custom-call | flops 805306368 | bytes 2097152 | tf_op jit(solution)/shard_map/choose/pallas_call | solution.py:195
  21.1 0.0 collective-permute-done.1.refs_2_
  21.1 0.0 collective-permute-done.3.refs_4_
  21.1 0.5 collective-permute-done.5.refs_6_
  21.7 0.0 collective-permute-start.6
  21.7 0.5 collective-permute-start.4
  22.2 0.0 collective-permute-start.2
  22.2 0.0 collective-permute-done.refs_1_
  22.2 0.9 %collective-permute-done.6.refs_7_ = bf16[784,128]{1,0:T(8,128)(2,1)S(1)} collective-permute-done((bf16[784,128]{1,0:T(8,128)(2,1)S(1)}, bf16[784,128]{1,0:T(8,128)(2,1)S(1)}, u32[]{:S(2)}, u32[]{:S(2)}) %collective-permute-start.6) | collective-permute-done | bytes 200736 | tf_op jit(solution)/shard_map/ppermute | solution.py:391
  23.1 0.3 collective-permute-done.4.refs_5_
  23.4 0.3 collective-permute-done.2.refs_3_
  23.7 1.6 %collective-permute-start.8 = (s32[1,128]{1,0:T(1,128)S(1)}, s32[1,128]{1,0:T(1,128)S(1)}, u32[]{:S(2)}, u32[]{:S(2)}) collective-permute-start(s32[1,128]{1,0:T(1,128)S(1)} %get-tuple-element.30.refs_0_), channel_id=1, source_target_pairs={{0,2},{1,3},{2,0},{3,1},{4,6},{5,7},{6,4},{7,5},{8,10},{9,11},{10,... | collective-permute-start | bytes 1544 | tf_op jit(solution)/shard_map/ppermute | solution.py:391
  25.4 0.5 collective-permute-start.7
  25.8 1.5 %collective-permute-done.8.refs_1_ = s32[1,128]{1,0:T(1,128)S(1)} collective-permute-done((s32[1,128]{1,0:T(1,128)S(1)}, s32[1,128]{1,0:T(1,128)S(1)}, u32[]{:S(2)}, u32[]{:S(2)}) %collective-permute-start.8) | collective-permute-done | bytes 544 | tf_op jit(solution)/shard_map/ppermute | solution.py:391
  27.3 1.3 %deal.1.refs_8_ = bf16[16,32,1024]{2,1,0:T(8,128)(2,1)} custom-call(s32[1]{0:T(128)} %bitcast.me_ref, s32[1,128]{1,0:T(1,128)S(1)} %get-tuple-element.30.refs_0_, s32[1,128]{1,0:T(1,128)S(1)} %collective-permute-done.8.refs_1_, bf16[16,32,1024]{2,1,0:T(8,128)(2,1)S(1)} %choose.1.refs_2_), custom_call_target="tpu_custom_call" | custom-call | flops 20000000000 | bytes 2097152 | tf_op jit(solution)/shard_map/deal/pallas_call | solution.py:220
  28.6 7.9 %all-to-all-start = ((bf16[16,32,1024]{2,1,0:T(8,128)(2,1)}), bf16[16,32,1024]{2,1,0:T(8,128)(2,1)S(1)}, u32[]{:S(2)}, u32[]{:S(2)}) async-start(bf16[16,32,1024]{2,1,0:T(8,128)(2,1)} %deal.1.refs_8_), calls=%async_computation | async-start | bytes 2097152 | tf_op jit(solution)/shard_map/all_to_all | solution.py:411
  36.5 0.0 collective-permute-done.7.q_ref
  36.5 5.2 %score.2 = (bf16[4096,1024]{1,0:T(8,128)(2,1)S(1)}, f32[16,1024]{1,0:T(8,128)S(1)}, f32[1,1024]{1,0:T(1,128)S(1)}) custom-call(bf16[1024,128]{1,0:T(8,128)(2,1)S(1)} %collective-permute-done.7.q_ref, bf16[784,128]{1,0:T(8,128)(2,1)S(1)} %get-tuple-element.20.refs_0_, bf16[784,128]{1,0:T(8,128)(2,1)S(1)} %collective-permute-done.refs_1_, ...), custom_call_target="tpu_custom_call" | custom-call | flops 8589934592 | bytes 8388608 | tf_op jit(solution)/shard_map/score/pallas_call | solution.py:299
  41.8 2.0 %collective-permute-start.10 = (f32[1,1024]{1,0:T(1,128)S(1)}, f32[1,1024]{1,0:T(1,128)S(1)}, u32[]{:S(2)}, u32[]{:S(2)}) collective-permute-start(f32[1,1024]{1,0:T(1,128)S(1)} %get-tuple-element.34.refs_8_.lse_ref), channel_id=1, source_target_pairs={{0,2},{1,3},{2,0},{3,1},{4,6},{5,7},{6,4},{7,5},{8,10},{9,11},{10,... | collective-permute-start | bytes 12296 | tf_op jit(solution)/shard_map/ppermute | solution.py:391
  43.8 5.2 %score.3 = (bf16[4096,1024]{1,0:T(8,128)(2,1)S(1)}, f32[16,1024]{1,0:T(8,128)S(1)}, f32[1,1024]{1,0:T(1,128)S(1)}) custom-call(bf16[1024,128]{1,0:T(8,128)(2,1)S(1)} %get-tuple-element.29.q_ref, bf16[784,128]{1,0:T(8,128)(2,1)S(1)} %get-tuple-element.20.refs_0_, bf16[784,128]{1,0:T(8,128)(2,1)S(1)} %collective-permute-done.refs_1_, ...), custom_call_target="tpu_custom_call" | custom-call | flops 8589934592 | bytes 8388608 | tf_op jit(solution)/shard_map/score/pallas_call | solution.py:299
  49.0 0.2 collective-permute-start.9
  49.2 0.0 collective-permute-done.10.rest_0_
  49.2 1.8 %weigh.2.rest_1_ = f32[16,256]{1,0:T(8,128)S(1)} custom-call(bf16[4096,1024]{1,0:T(8,128)(2,1)S(1)} %get-tuple-element.36.prob_ref, f32[16,1024]{1,0:T(8,128)S(1)} %get-tuple-element.37.top_ref, f32[1,1024]{1,0:T(1,128)S(1)} %get-tuple-element.35.lse_ref, f32[1,1024]{1,0:T(1,128)S(1)} %collective-permute-done.10.rest_0_), custom_call_target="tpu_custom_call" | custom-call | flops 16777216 | bytes 8388608 | tf_op jit(solution)/shard_map/weigh/pallas_call | solution.py:355
  51.0 1.7 %collective-permute-done.9.rest_0_ = f32[1,1024]{1,0:T(1,128)S(1)} collective-permute-done((f32[1,1024]{1,0:T(1,128)S(1)}, f32[1,1024]{1,0:T(1,128)S(1)}, u32[]{:S(2)}, u32[]{:S(2)}) %collective-permute-start.9) | collective-permute-done | bytes 4128 | tf_op jit(solution)/shard_map/ppermute | solution.py:391
  52.7 1.9 %weigh.3 = f32[16,256]{1,0:T(8,128)S(1)} custom-call(bf16[4096,1024]{1,0:T(8,128)(2,1)S(1)} %get-tuple-element.32.prob_ref, f32[16,1024]{1,0:T(8,128)S(1)} %get-tuple-element.33.top_ref, f32[1,1024]{1,0:T(1,128)S(1)} %get-tuple-element.34.refs_8_.lse_ref, f32[1,1024]{1,0:T(1,128)S(1)} %collective-permute-done.9.rest_0_, f32[16,256]{1,0:T(8,128)S(1)} %weigh.2.rest_1_), custom_call_target="tpu_custom_call" | custom-call | flops 16777216 | bytes 8388608 | tf_op jit(solution)/shard_map/weigh/pallas_call | solution.py:355
  54.6 0.1 collective-permute-start.11
  54.7 1.2 %collective-permute-done.11 = f32[4,512]{1,0:T(4,128)S(1)} collective-permute-done((f32[4,512]{1,0:T(4,128)S(1)}, f32[4,512]{1,0:T(4,128)S(1)}, u32[]{:S(2)}, u32[]{:S(2)}) %collective-permute-start.11) | collective-permute-done | bytes 8224 | tf_op jit(solution)/shard_map/ppermute | solution.py:391
  55.9 3.4 %collective-permute-start.13 = (f32[512]{0:T(512)S(1)}, f32[512]{0:T(512)S(1)}, u32[]{:S(2)}, u32[]{:S(2)}) collective-permute-start(f32[512]{0:T(512)S(1)} %bitcast.28), channel_id=1, source_target_pairs={{0,12},{1,13},{2,14},{3,15},{4,8},{5,9},{6,10},{7,11},{8,4},{9,5},... | collective-permute-start | bytes 6152 | tf_op jit(solution)/shard_map/ppermute | solution.py:391
  59.3 0.0 collective-permute-start.14
  59.3 1.1 %collective-permute-start.12 = (f32[512]{0:T(512)S(1)}, f32[512]{0:T(512)S(1)}, u32[]{:S(2)}, u32[]{:S(2)}) collective-permute-start(f32[512]{0:T(512)S(1)} %bitcast.26), channel_id=1, source_target_pairs={{0,8},{1,9},{2,10},{3,11},{4,12},{5,13},{6,14},{7,15},{8,0},{9,1},... | collective-permute-start | bytes 6152 | tf_op jit(solution)/shard_map/ppermute | solution.py:391
  60.4 0.0 all-to-all-done
  60.4 1.4 %place.1.refs_4_ = bf16[256,1024]{1,0:T(8,128)(2,1)} custom-call(s32[1]{0:T(128)} %bitcast.me_ref, s32[1,128]{1,0:T(1,128)S(1)} %get-tuple-element.30.refs_0_, s32[1,128]{1,0:T(1,128)S(1)} %collective-permute-done.8.refs_1_, bf16[512,1024]{1,0:T(8,128)(2,1)S(1)} %bitcast.19), custom_call_target="tpu_custom_call" | custom-call | flops 268435456 | bytes 1572864 | tf_op jit(solution)/shard_map/place/pallas_call | solution.py:254
  61.7 0.0 collective-permute-done.13
  61.7 1.1 %collective-permute-done.14 = f32[512]{0:T(512)S(1)} collective-permute-done((f32[512]{0:T(512)S(1)}, f32[512]{0:T(512)S(1)}, u32[]{:S(2)}, u32[]{:S(2)}) %collective-permute-start.14) | collective-permute-done | bytes 2080 | tf_op jit(solution)/shard_map/ppermute | solution.py:391
  62.9 0.9 %collective-permute-done.12 = f32[512]{0:T(512)S(1)} collective-permute-done((f32[512]{0:T(512)S(1)}, f32[512]{0:T(512)S(1)}, u32[]{:S(2)}, u32[]{:S(2)}) %collective-permute-start.12) | collective-permute-done | bytes 2080 | tf_op jit(solution)/shard_map/ppermute | solution.py:391
  63.8 0.6 finish.1
  (6 shorter events, 0.1 us)
Async XLA Ops:
  2.6 18.6 %collective-permute-start.1 = (bf16[784,128]{1,0:T(8,128)(2,1)S(1)}, bf16[784,128]{1,0:T(8,128)(2,1)S(1)}, u32[]{:S(2)}, u32[]{:S(2)}) collective-permute-start(bf16[784,128]{1,0:T(8,128)(2,1)S(1)} %get-tuple-element.21), channel_id=1, source_target_pairs={{0,8},{1,9},{2,10},{3,11},{4,12},{5,13},{6,14},{7,15},{8,0},{9,1},... | collective-permute-start | bytes 602120 | tf_op jit(solution)/shard_map/ppermute | solution.py:391
  6.7 14.5 %collective-permute-start.3 = (bf16[784,128]{1,0:T(8,128)(2,1)S(1)}, bf16[784,128]{1,0:T(8,128)(2,1)S(1)}, u32[]{:S(2)}, u32[]{:S(2)}) collective-permute-start(bf16[784,128]{1,0:T(8,128)(2,1)S(1)} %get-tuple-element.23), channel_id=1, source_target_pairs={{0,12},{1,13},{2,14},{3,15},{4,8},{5,9},{6,10},{7,11},{8,4},{9,5},... | collective-permute-start | bytes 602120 | tf_op jit(solution)/shard_map/ppermute | solution.py:391
  8.0 13.6 %collective-permute-start.5 = (bf16[784,128]{1,0:T(8,128)(2,1)S(1)}, bf16[784,128]{1,0:T(8,128)(2,1)S(1)}, u32[]{:S(2)}, u32[]{:S(2)}) collective-permute-start(bf16[784,128]{1,0:T(8,128)(2,1)S(1)} %get-tuple-element.26), channel_id=1, source_target_pairs={{0,4},{1,5},{2,6},{3,7},{4,0},{5,1},{6,2},{7,3},{8,12},{9,13},{10,... | collective-permute-start | bytes 602120 | tf_op jit(solution)/shard_map/ppermute | solution.py:391
  8.3 14.0 %collective-permute-start = (bf16[784,128]{1,0:T(8,128)(2,1)S(1)}, bf16[784,128]{1,0:T(8,128)(2,1)S(1)}, u32[]{:S(2)}, u32[]{:S(2)}) collective-permute-start(bf16[784,128]{1,0:T(8,128)(2,1)S(1)} %get-tuple-element.20.refs_0_), channel_id=1, source_target_pairs={{0,1},{1,0},{2,3},{3,2},{4,5},{5,4},{6,7},{7,6},{8,9},{9,8},{10,11... | collective-permute-start | bytes 602120 | tf_op jit(solution)/shard_map/ppermute | solution.py:391
  8.3 11.8 %copy-start = (s32[512]{0:T(512)S(1)}, s32[512]{0:T(512)}, u32[]{:S(2)}) copy-start(s32[512]{0:T(512)} %param.12) | copy-start | bytes 6148
  21.7 1.4 %collective-permute-start.6 = (bf16[784,128]{1,0:T(8,128)(2,1)S(1)}, bf16[784,128]{1,0:T(8,128)(2,1)S(1)}, u32[]{:S(2)}, u32[]{:S(2)}) collective-permute-start(bf16[784,128]{1,0:T(8,128)(2,1)S(1)} %collective-permute-done.5.refs_6_), channel_id=1, source_target_pairs={{0,1},{1,0},{2,3},{3,2},{4,5},{5,4},{6,7},{7,6},{8,9},{9,8},{10,11... | collective-permute-start | bytes 602120 | tf_op jit(solution)/shard_map/ppermute | solution.py:391
  21.7 1.7 %collective-permute-start.4 = (bf16[784,128]{1,0:T(8,128)(2,1)S(1)}, bf16[784,128]{1,0:T(8,128)(2,1)S(1)}, u32[]{:S(2)}, u32[]{:S(2)}) collective-permute-start(bf16[784,128]{1,0:T(8,128)(2,1)S(1)} %collective-permute-done.3.refs_4_), channel_id=1, source_target_pairs={{0,1},{1,0},{2,3},{3,2},{4,5},{5,4},{6,7},{7,6},{8,9},{9,8},{10,11... | collective-permute-start | bytes 602120 | tf_op jit(solution)/shard_map/ppermute | solution.py:391
  22.2 1.5 %collective-permute-start.2 = (bf16[784,128]{1,0:T(8,128)(2,1)S(1)}, bf16[784,128]{1,0:T(8,128)(2,1)S(1)}, u32[]{:S(2)}, u32[]{:S(2)}) collective-permute-start(bf16[784,128]{1,0:T(8,128)(2,1)S(1)} %collective-permute-done.1.refs_2_), channel_id=1, source_target_pairs={{0,1},{1,0},{2,3},{3,2},{4,5},{5,4},{6,7},{7,6},{8,9},{9,8},{10,11... | collective-permute-start | bytes 602120 | tf_op jit(solution)/shard_map/ppermute | solution.py:391
  23.7 3.6 %collective-permute-start.8 = (s32[1,128]{1,0:T(1,128)S(1)}, s32[1,128]{1,0:T(1,128)S(1)}, u32[]{:S(2)}, u32[]{:S(2)}) collective-permute-start(s32[1,128]{1,0:T(1,128)S(1)} %get-tuple-element.30.refs_0_), channel_id=1, source_target_pairs={{0,2},{1,3},{2,0},{3,1},{4,6},{5,7},{6,4},{7,5},{8,10},{9,11},{10,... | collective-permute-start | bytes 1544 | tf_op jit(solution)/shard_map/ppermute | solution.py:391
  25.4 11.2 %collective-permute-start.7 = (bf16[1024,128]{1,0:T(8,128)(2,1)S(1)}, bf16[1024,128]{1,0:T(8,128)(2,1)S(1)}, u32[]{:S(2)}, u32[]{:S(2)}) collective-permute-start(bf16[1024,128]{1,0:T(8,128)(2,1)S(1)} %get-tuple-element.29.q_ref), channel_id=1, source_target_pairs={{0,2},{1,3},{2,0},{3,1},{4,6},{5,7},{6,4},{7,5},{8,10},{9,11},{10,... | collective-permute-start | bytes 786440 | tf_op jit(solution)/shard_map/ppermute | solution.py:391
  28.6 31.8 %all-to-all-start = ((bf16[16,32,1024]{2,1,0:T(8,128)(2,1)}), bf16[16,32,1024]{2,1,0:T(8,128)(2,1)S(1)}, u32[]{:S(2)}, u32[]{:S(2)}) async-start(bf16[16,32,1024]{2,1,0:T(8,128)(2,1)} %deal.1.refs_8_), calls=%async_computation | async-start | bytes 2097152 | tf_op jit(solution)/shard_map/all_to_all | solution.py:411
  41.8 7.4 %collective-permute-start.10 = (f32[1,1024]{1,0:T(1,128)S(1)}, f32[1,1024]{1,0:T(1,128)S(1)}, u32[]{:S(2)}, u32[]{:S(2)}) collective-permute-start(f32[1,1024]{1,0:T(1,128)S(1)} %get-tuple-element.34.refs_8_.lse_ref), channel_id=1, source_target_pairs={{0,2},{1,3},{2,0},{3,1},{4,6},{5,7},{6,4},{7,5},{8,10},{9,11},{10,... | collective-permute-start | bytes 12296 | tf_op jit(solution)/shard_map/ppermute | solution.py:391
  49.0 3.7 %collective-permute-start.9 = (f32[1,1024]{1,0:T(1,128)S(1)}, f32[1,1024]{1,0:T(1,128)S(1)}, u32[]{:S(2)}, u32[]{:S(2)}) collective-permute-start(f32[1,1024]{1,0:T(1,128)S(1)} %get-tuple-element.35.lse_ref), channel_id=1, source_target_pairs={{0,2},{1,3},{2,0},{3,1},{4,6},{5,7},{6,4},{7,5},{8,10},{9,11},{10,... | collective-permute-start | bytes 12296 | tf_op jit(solution)/shard_map/ppermute | solution.py:391
  54.6 1.2 %collective-permute-start.11 = (f32[4,512]{1,0:T(4,128)S(1)}, f32[4,512]{1,0:T(4,128)S(1)}, u32[]{:S(2)}, u32[]{:S(2)}) collective-permute-start(f32[4,512]{1,0:T(4,128)S(1)} %bitcast.24), channel_id=1, source_target_pairs={{0,1},{1,0},{2,3},{3,2},{4,5},{5,4},{6,7},{7,6},{8,9},{9,8},{10,11... | collective-permute-start | bytes 24584 | tf_op jit(solution)/shard_map/ppermute | solution.py:391
  55.9 5.8 %collective-permute-start.13 = (f32[512]{0:T(512)S(1)}, f32[512]{0:T(512)S(1)}, u32[]{:S(2)}, u32[]{:S(2)}) collective-permute-start(f32[512]{0:T(512)S(1)} %bitcast.28), channel_id=1, source_target_pairs={{0,12},{1,13},{2,14},{3,15},{4,8},{5,9},{6,10},{7,11},{8,4},{9,5},... | collective-permute-start | bytes 6152 | tf_op jit(solution)/shard_map/ppermute | solution.py:391
  59.3 3.6 %collective-permute-start.14 = (f32[512]{0:T(512)S(1)}, f32[512]{0:T(512)S(1)}, u32[]{:S(2)}, u32[]{:S(2)}) collective-permute-start(f32[512]{0:T(512)S(1)} %bitcast.27), channel_id=1, source_target_pairs={{0,4},{1,5},{2,6},{3,7},{4,0},{5,1},{6,2},{7,3},{8,12},{9,13},{10,... | collective-permute-start | bytes 6152 | tf_op jit(solution)/shard_map/ppermute | solution.py:391
  59.3 4.5 %collective-permute-start.12 = (f32[512]{0:T(512)S(1)}, f32[512]{0:T(512)S(1)}, u32[]{:S(2)}, u32[]{:S(2)}) collective-permute-start(f32[512]{0:T(512)S(1)} %bitcast.26), channel_id=1, source_target_pairs={{0,8},{1,9},{2,10},{3,11},{4,12},{5,13},{6,14},{7,15},{8,0},{9,1},... | collective-permute-start | bytes 6152 | tf_op jit(solution)/shard_map/ppermute | solution.py:391

commit v9 on v8

--- a/solution.py
+++ b/solution.py
@@ -187,7 +187,9 @@
         chooses, listed, (((1,), (1,)), ((), ())), preferred_element_type=F32
     ).astype(BF16)
     rows = jnp.dot(select, rows_ref[...], preferred_element_type=F32).astype(BF16)
-    out_ref[...] = rows.reshape(out_ref.shape)
+    rows = rows.reshape(size, cap, rows.shape[1])
+    out_ref[:size] = rows
+    out_ref[size:] = rows
 
 
 def choose(keep_index, rows, size):
@@ -196,7 +198,7 @@
         functools.partial(choose_kernel, size),
         in_specs=[VMEM] * 2,
         out_specs=VMEM,
-        out_shape=jax.ShapeDtypeStruct((size, n // size, width), BF16),
+        out_shape=jax.ShapeDtypeStruct((2 * size, n // size, width), BF16),
         compiler_params=params(32),
         cost_estimate=cost(2 * n * n * (n + width), 4 * rows.size),
         name="choose",
@@ -204,24 +206,27 @@
 
 
 def deal_kernel(me_ref, *refs):
-    count_refs, (rows_ref, out_ref) = refs[:-2], refs[-2:]
+    count_refs, (rows_ref, out_ref, sem) = refs[:-3], refs[-3:]
     me = me_ref[0]
-    size = rows_ref.shape[0]
+    size = out_ref.shape[0]
     start = jnp.zeros((1, 1), jnp.int32)
     for cross, ref in zip(cross_steps(size), count_refs):
         for lane, step in enumerate(cell_steps(size)):
             start += jnp.where((me ^ cross ^ step) < me, ref[:, lane : lane + 1], 0)
     start = jnp.sum(start)
-    for owner in range(size):
-        out_ref[owner] = rows_ref[(owner - start) & (size - 1)]
+    first = (-start) & (size - 1)
+    copy = pltpu.make_async_copy(rows_ref.at[pl.ds(first, size)], out_ref, sem)
+    copy.start()
+    copy.wait()
 
 
 def deal(me, counts, rows):
     return pl.pallas_call(
         deal_kernel,
         in_specs=[SMEM] + [VMEM] * (len(counts) + 1),
-        out_specs=VMEM,
-        out_shape=jax.ShapeDtypeStruct(rows.shape, BF16),
+        out_specs=ANY,
+        out_shape=jax.ShapeDtypeStruct((rows.shape[0] // 2, *rows.shape[1:]), BF16),
+        scratch_shapes=[pltpu.SemaphoreType.DMA],
         compiler_params=params(16),
         cost_estimate=cost(2e10, 4 * rows.size),
         name="deal",

time: 64.6 us -> 64.5 us (level)
  no operation moved by 1% of the time
where the time goes in v9:
time: 64.5 us; the launch traced here: 64.3 us
  Pallas kernels  31.5 us (49%)
  starting transfers between devices  23 us (36%)
  waiting for transfers between devices  8.39 us (13%)
  between operations  1.41 us (2%)
    ppermute x15, starting transfers between devices, swap(): return lax.ppermute(x, 'seq', [(i, i ^ r) for i in range(size)])  15 us
    pallas_call x1, Pallas kernels, project(): pl.pallas_call(functools.partial(project_kernel, cuts), in_specs=[ANY] *...  11.8 us
    pallas_call x2, Pallas kernels, score(): pl.pallas_call(functools.partial(score_kernel, keys, chunk, tile), in_spe...  10.5 us
    ppermute x15, waiting for transfers between devices, swap(): return lax.ppermute(x, 'seq', [(i, i ^ r) for i in range(size)])  8.39 us
    all_to_all x1, starting transfers between devices, shards(): lax.all_to_all(picked, 'seq', split_axis=0, concat_axis=0, tiled=True)  7.96 us
    pallas_call x2, Pallas kernels, weigh(): pl.pallas_call(functools.partial(weigh_kernel, factor, 1 + len(others), v...  3.7 us
    pallas_call x1, Pallas kernels, place(): pl.pallas_call(functools.partial(place_kernel, size), in_specs=[SMEM] + [...  1.35 us
    pallas_call x1, Pallas kernels, front(): pl.pallas_call(functools.partial(front_kernel, size, keys.shape[0]), in_s...  1.29 us
  transfers between devices with their start and end apart: 16, of which 9 were waited for; matrix products, arithmetic and copies ran while one was open for 0% of the time, Pallas kernels for 46%

profile of v9, /device:TPU:0, one launch (start us, length us, event | category | flops | bytes accessed | tf_op | source)
XLA Modules:
  0.0 64.3 jit_solution(9112190248552829795)
XLA Ops:
  1.3 1.3 %front.1 = (bf16[784,128]{1,0:T(8,128)(2,1)S(1)}, bf16[784,128]{1,0:T(8,128)(2,1)S(1)}, bf16[784,128]{1,0:T(8,128)(2,1)S(1)}, bf16[784,128]{1,0:T(8,128)(2,1)S(1)}) custom-call(s32[1]{0:T(128)} %bitcast.me_ref, s32[1]{0:T(128)S(6)} %copy.19.count_ref, bf16[512,512]{1,0:T(8,128)(2,1)} %keys_ref.1, bf16[32,4096]{1,0:T(8,128)(2,1)} %q_ref.1), custom_call_target="tpu_custom_call" | custom-call | bytes 1572864 | tf_op jit(solution)/shard_map/front/pallas_call | solution.py:139
  2.6 4.1 %collective-permute-start.1 = (bf16[784,128]{1,0:T(8,128)(2,1)S(1)}, bf16[784,128]{1,0:T(8,128)(2,1)S(1)}, u32[]{:S(2)}, u32[]{:S(2)}) collective-permute-start(bf16[784,128]{1,0:T(8,128)(2,1)S(1)} %get-tuple-element.21), channel_id=1, source_target_pairs={{0,8},{1,9},{2,10},{3,11},{4,12},{5,13},{6,14},{7,15},{8,0},{9,1},... | collective-permute-start | bytes 602120 | tf_op jit(solution)/shard_map/ppermute | solution.py:396
  6.7 1.3 %collective-permute-start.3 = (bf16[784,128]{1,0:T(8,128)(2,1)S(1)}, bf16[784,128]{1,0:T(8,128)(2,1)S(1)}, u32[]{:S(2)}, u32[]{:S(2)}) collective-permute-start(bf16[784,128]{1,0:T(8,128)(2,1)S(1)} %get-tuple-element.23), channel_id=1, source_target_pairs={{0,12},{1,13},{2,14},{3,15},{4,8},{5,9},{6,10},{7,11},{8,4},{9,5},... | collective-permute-start | bytes 602120 | tf_op jit(solution)/shard_map/ppermute | solution.py:396
  8.0 0.2 collective-permute-start.5
  8.3 0.0 collective-permute-start
  8.3 0.0 copy-start
  8.3 11.8 %project.1.rows_ref = bf16[512,1024]{1,0:T(8,128)(2,1)S(1)} custom-call(bf16[512,8192]{1,0:T(8,128)(2,1)} %x_hbm.1, f32[1,8192]{1,0:T(1,128)} %bitcast.29, bf16[8192,1024]{1,0:T(8,128)(2,1)} %weight_hbm.1, f32[1,1024]{1,0:T(1,128)} %bitcast.30), custom_call_target="tpu_custom_call" | custom-call | flops 8589934592 | bytes 25165824 | tf_op jit(solution)/shard_map/project/pallas_call | solution.py:88
  20.1 0.0 copy-done
  20.1 1.0 %choose.1.refs_2_ = bf16[32,32,1024]{2,1,0:T(8,128)(2,1)S(1)} custom-call(s32[1,512]{1,0:T(1,128)S(1)} %bitcast.23, bf16[512,1024]{1,0:T(8,128)(2,1)S(1)} %project.1.rows_ref), custom_call_target="tpu_custom_call" | custom-call | flops 805306368 | bytes 2097152 | tf_op jit(solution)/shard_map/choose/pallas_call | solution.py:197
  21.1 0.0 collective-permute-done.1.refs_2_
  21.1 0.0 collective-permute-done.3.refs_4_
  21.1 0.5 collective-permute-done.5.refs_6_
  21.7 0.0 collective-permute-start.6
  21.7 0.5 collective-permute-start.4
  22.2 0.0 collective-permute-start.2
  22.2 0.0 collective-permute-done.refs_1_
  22.2 0.9 %collective-permute-done.6.refs_7_ = bf16[784,128]{1,0:T(8,128)(2,1)S(1)} collective-permute-done((bf16[784,128]{1,0:T(8,128)(2,1)S(1)}, bf16[784,128]{1,0:T(8,128)(2,1)S(1)}, u32[]{:S(2)}, u32[]{:S(2)}) %collective-permute-start.6) | collective-permute-done | bytes 200736 | tf_op jit(solution)/shard_map/ppermute | solution.py:396
  23.1 0.3 collective-permute-done.4.refs_5_
  23.4 0.3 collective-permute-done.2.refs_3_
  23.7 1.6 %collective-permute-start.8 = (s32[1,128]{1,0:T(1,128)S(1)}, s32[1,128]{1,0:T(1,128)S(1)}, u32[]{:S(2)}, u32[]{:S(2)}) collective-permute-start(s32[1,128]{1,0:T(1,128)S(1)} %get-tuple-element.30.refs_0_), channel_id=1, source_target_pairs={{0,2},{1,3},{2,0},{3,1},{4,6},{5,7},{6,4},{7,5},{8,10},{9,11},{10,... | collective-permute-start | bytes 1544 | tf_op jit(solution)/shard_map/ppermute | solution.py:396
  25.4 0.5 collective-permute-start.7
  25.8 1.5 %collective-permute-done.8.refs_1_ = s32[1,128]{1,0:T(1,128)S(1)} collective-permute-done((s32[1,128]{1,0:T(1,128)S(1)}, s32[1,128]{1,0:T(1,128)S(1)}, u32[]{:S(2)}, u32[]{:S(2)}) %collective-permute-start.8) | collective-permute-done | bytes 544 | tf_op jit(solution)/shard_map/ppermute | solution.py:396
  27.3 1.2 %deal.1.refs_8_ = bf16[16,32,1024]{2,1,0:T(8,128)(2,1)} custom-call(s32[1]{0:T(128)} %bitcast.me_ref, s32[1,128]{1,0:T(1,128)S(1)} %get-tuple-element.30.refs_0_, s32[1,128]{1,0:T(1,128)S(1)} %collective-permute-done.8.refs_1_, bf16[32,32,1024]{2,1,0:T(8,128)(2,1)S(1)} %choose.1.refs_2_), custom_call_target="tpu_custom_call" | custom-call | flops 20000000000 | bytes 4194304 | tf_op jit(solution)/shard_map/deal/pallas_call | solution.py:224
  28.5 8.0 %all-to-all-start = ((bf16[16,32,1024]{2,1,0:T(8,128)(2,1)}), bf16[16,32,1024]{2,1,0:T(8,128)(2,1)S(1)}, u32[]{:S(2)}, u32[]{:S(2)}) async-start(bf16[16,32,1024]{2,1,0:T(8,128)(2,1)} %deal.1.refs_8_), calls=%async_computation | async-start | bytes 2097152 | tf_op jit(solution)/shard_map/all_to_all | solution.py:416
  36.5 0.0 collective-permute-done.7.q_ref
  36.5 5.2 %score.2 = (bf16[4096,1024]{1,0:T(8,128)(2,1)S(1)}, f32[16,1024]{1,0:T(8,128)S(1)}, f32[1,1024]{1,0:T(1,128)S(1)}) custom-call(bf16[1024,128]{1,0:T(8,128)(2,1)S(1)} %collective-permute-done.7.q_ref, bf16[784,128]{1,0:T(8,128)(2,1)S(1)} %get-tuple-element.20.refs_0_, bf16[784,128]{1,0:T(8,128)(2,1)S(1)} %collective-permute-done.refs_1_, ...), custom_call_target="tpu_custom_call" | custom-call | flops 8589934592 | bytes 8388608 | tf_op jit(solution)/shard_map/score/pallas_call | solution.py:304
  41.8 2.0 %collective-permute-start.10 = (f32[1,1024]{1,0:T(1,128)S(1)}, f32[1,1024]{1,0:T(1,128)S(1)}, u32[]{:S(2)}, u32[]{:S(2)}) collective-permute-start(f32[1,1024]{1,0:T(1,128)S(1)} %get-tuple-element.34.refs_8_.lse_ref), channel_id=1, source_target_pairs={{0,2},{1,3},{2,0},{3,1},{4,6},{5,7},{6,4},{7,5},{8,10},{9,11},{10,... | collective-permute-start | bytes 12296 | tf_op jit(solution)/shard_map/ppermute | solution.py:396
  43.7 5.2 %score.3 = (bf16[4096,1024]{1,0:T(8,128)(2,1)S(1)}, f32[16,1024]{1,0:T(8,128)S(1)}, f32[1,1024]{1,0:T(1,128)S(1)}) custom-call(bf16[1024,128]{1,0:T(8,128)(2,1)S(1)} %get-tuple-element.29.q_ref, bf16[784,128]{1,0:T(8,128)(2,1)S(1)} %get-tuple-element.20.refs_0_, bf16[784,128]{1,0:T(8,128)(2,1)S(1)} %collective-permute-done.refs_1_, ...), custom_call_target="tpu_custom_call" | custom-call | flops 8589934592 | bytes 8388608 | tf_op jit(solution)/shard_map/score/pallas_call | solution.py:304
  49.0 0.2 collective-permute-start.9
  49.2 0.0 collective-permute-done.10.rest_0_
  49.2 1.8 %weigh.2.rest_1_ = f32[16,256]{1,0:T(8,128)S(1)} custom-call(bf16[4096,1024]{1,0:T(8,128)(2,1)S(1)} %get-tuple-element.36.prob_ref, f32[16,1024]{1,0:T(8,128)S(1)} %get-tuple-element.37.top_ref, f32[1,1024]{1,0:T(1,128)S(1)} %get-tuple-element.35.lse_ref, f32[1,1024]{1,0:T(1,128)S(1)} %collective-permute-done.10.rest_0_), custom_call_target="tpu_custom_call" | custom-call | flops 16777216 | bytes 8388608 | tf_op jit(solution)/shard_map/weigh/pallas_call | solution.py:360
  51.0 1.7 %collective-permute-done.9.rest_0_ = f32[1,1024]{1,0:T(1,128)S(1)} collective-permute-done((f32[1,1024]{1,0:T(1,128)S(1)}, f32[1,1024]{1,0:T(1,128)S(1)}, u32[]{:S(2)}, u32[]{:S(2)}) %collective-permute-start.9) | collective-permute-done | bytes 4128 | tf_op jit(solution)/shard_map/ppermute | solution.py:396
  52.6 1.9 %weigh.3 = f32[16,256]{1,0:T(8,128)S(1)} custom-call(bf16[4096,1024]{1,0:T(8,128)(2,1)S(1)} %get-tuple-element.32.prob_ref, f32[16,1024]{1,0:T(8,128)S(1)} %get-tuple-element.33.top_ref, f32[1,1024]{1,0:T(1,128)S(1)} %get-tuple-element.34.refs_8_.lse_ref, f32[1,1024]{1,0:T(1,128)S(1)} %collective-permute-done.9.rest_0_, f32[16,256]{1,0:T(8,128)S(1)} %weigh.2.rest_1_), custom_call_target="tpu_custom_call" | custom-call | flops 16777216 | bytes 8388608 | tf_op jit(solution)/shard_map/weigh/pallas_call | solution.py:360
  54.6 0.1 collective-permute-start.11
  54.7 1.2 %collective-permute-done.11 = f32[4,512]{1,0:T(4,128)S(1)} collective-permute-done((f32[4,512]{1,0:T(4,128)S(1)}, f32[4,512]{1,0:T(4,128)S(1)}, u32[]{:S(2)}, u32[]{:S(2)}) %collective-permute-start.11) | collective-permute-done | bytes 8224 | tf_op jit(solution)/shard_map/ppermute | solution.py:396
  55.9 3.4 %collective-permute-start.13 = (f32[512]{0:T(512)S(1)}, f32[512]{0:T(512)S(1)}, u32[]{:S(2)}, u32[]{:S(2)}) collective-permute-start(f32[512]{0:T(512)S(1)} %bitcast.28), channel_id=1, source_target_pairs={{0,12},{1,13},{2,14},{3,15},{4,8},{5,9},{6,10},{7,11},{8,4},{9,5},... | collective-permute-start | bytes 6152 | tf_op jit(solution)/shard_map/ppermute | solution.py:396
  59.2 0.0 collective-permute-start.14
  59.2 1.1 %collective-permute-start.12 = (f32[512]{0:T(512)S(1)}, f32[512]{0:T(512)S(1)}, u32[]{:S(2)}, u32[]{:S(2)}) collective-permute-start(f32[512]{0:T(512)S(1)} %bitcast.26), channel_id=1, source_target_pairs={{0,8},{1,9},{2,10},{3,11},{4,12},{5,13},{6,14},{7,15},{8,0},{9,1},... | collective-permute-start | bytes 6152 | tf_op jit(solution)/shard_map/ppermute | solution.py:396
  60.3 0.0 all-to-all-done
  60.3 1.4 %place.1.refs_4_ = bf16[256,1024]{1,0:T(8,128)(2,1)} custom-call(s32[1]{0:T(128)} %bitcast.me_ref, s32[1,128]{1,0:T(1,128)S(1)} %get-tuple-element.30.refs_0_, s32[1,128]{1,0:T(1,128)S(1)} %collective-permute-done.8.refs_1_, bf16[512,1024]{1,0:T(8,128)(2,1)S(1)} %bitcast.19), custom_call_target="tpu_custom_call" | custom-call | flops 268435456 | bytes 1572864 | tf_op jit(solution)/shard_map/place/pallas_call | solution.py:259
  61.7 0.0 collective-permute-done.13
  61.7 1.1 %collective-permute-done.14 = f32[512]{0:T(512)S(1)} collective-permute-done((f32[512]{0:T(512)S(1)}, f32[512]{0:T(512)S(1)}, u32[]{:S(2)}, u32[]{:S(2)}) %collective-permute-start.14) | collective-permute-done | bytes 2080 | tf_op jit(solution)/shard_map/ppermute | solution.py:396
  62.8 0.9 %collective-permute-done.12 = f32[512]{0:T(512)S(1)} collective-permute-done((f32[512]{0:T(512)S(1)}, f32[512]{0:T(512)S(1)}, u32[]{:S(2)}, u32[]{:S(2)}) %collective-permute-start.12) | collective-permute-done | bytes 2080 | tf_op jit(solution)/shard_map/ppermute | solution.py:396
  63.7 0.6 finish.1
  (6 shorter events, 0.1 us)
Async XLA Ops:
  2.6 18.6 %collective-permute-start.1 = (bf16[784,128]{1,0:T(8,128)(2,1)S(1)}, bf16[784,128]{1,0:T(8,128)(2,1)S(1)}, u32[]{:S(2)}, u32[]{:S(2)}) collective-permute-start(bf16[784,128]{1,0:T(8,128)(2,1)S(1)} %get-tuple-element.21), channel_id=1, source_target_pairs={{0,8},{1,9},{2,10},{3,11},{4,12},{5,13},{6,14},{7,15},{8,0},{9,1},... | collective-permute-start | bytes 602120 | tf_op jit(solution)/shard_map/ppermute | solution.py:396
  6.7 14.5 %collective-permute-start.3 = (bf16[784,128]{1,0:T(8,128)(2,1)S(1)}, bf16[784,128]{1,0:T(8,128)(2,1)S(1)}, u32[]{:S(2)}, u32[]{:S(2)}) collective-permute-start(bf16[784,128]{1,0:T(8,128)(2,1)S(1)} %get-tuple-element.23), channel_id=1, source_target_pairs={{0,12},{1,13},{2,14},{3,15},{4,8},{5,9},{6,10},{7,11},{8,4},{9,5},... | collective-permute-start | bytes 602120 | tf_op jit(solution)/shard_map/ppermute | solution.py:396
  8.0 13.6 %collective-permute-start.5 = (bf16[784,128]{1,0:T(8,128)(2,1)S(1)}, bf16[784,128]{1,0:T(8,128)(2,1)S(1)}, u32[]{:S(2)}, u32[]{:S(2)}) collective-permute-start(bf16[784,128]{1,0:T(8,128)(2,1)S(1)} %get-tuple-element.26), channel_id=1, source_target_pairs={{0,4},{1,5},{2,6},{3,7},{4,0},{5,1},{6,2},{7,3},{8,12},{9,13},{10,... | collective-permute-start | bytes 602120 | tf_op jit(solution)/shard_map/ppermute | solution.py:396
  8.3 14.0 %collective-permute-start = (bf16[784,128]{1,0:T(8,128)(2,1)S(1)}, bf16[784,128]{1,0:T(8,128)(2,1)S(1)}, u32[]{:S(2)}, u32[]{:S(2)}) collective-permute-start(bf16[784,128]{1,0:T(8,128)(2,1)S(1)} %get-tuple-element.20.refs_0_), channel_id=1, source_target_pairs={{0,1},{1,0},{2,3},{3,2},{4,5},{5,4},{6,7},{7,6},{8,9},{9,8},{10,11... | collective-permute-start | bytes 602120 | tf_op jit(solution)/shard_map/ppermute | solution.py:396
  8.3 11.8 %copy-start = (s32[512]{0:T(512)S(1)}, s32[512]{0:T(512)}, u32[]{:S(2)}) copy-start(s32[512]{0:T(512)} %param.12) | copy-start | bytes 6148
  21.7 1.4 %collective-permute-start.6 = (bf16[784,128]{1,0:T(8,128)(2,1)S(1)}, bf16[784,128]{1,0:T(8,128)(2,1)S(1)}, u32[]{:S(2)}, u32[]{:S(2)}) collective-permute-start(bf16[784,128]{1,0:T(8,128)(2,1)S(1)} %collective-permute-done.5.refs_6_), channel_id=1, source_target_pairs={{0,1},{1,0},{2,3},{3,2},{4,5},{5,4},{6,7},{7,6},{8,9},{9,8},{10,11... | collective-permute-start | bytes 602120 | tf_op jit(solution)/shard_map/ppermute | solution.py:396
  21.7 1.7 %collective-permute-start.4 = (bf16[784,128]{1,0:T(8,128)(2,1)S(1)}, bf16[784,128]{1,0:T(8,128)(2,1)S(1)}, u32[]{:S(2)}, u32[]{:S(2)}) collective-permute-start(bf16[784,128]{1,0:T(8,128)(2,1)S(1)} %collective-permute-done.3.refs_4_), channel_id=1, source_target_pairs={{0,1},{1,0},{2,3},{3,2},{4,5},{5,4},{6,7},{7,6},{8,9},{9,8},{10,11... | collective-permute-start | bytes 602120 | tf_op jit(solution)/shard_map/ppermute | solution.py:396
  22.2 1.5 %collective-permute-start.2 = (bf16[784,128]{1,0:T(8,128)(2,1)S(1)}, bf16[784,128]{1,0:T(8,128)(2,1)S(1)}, u32[]{:S(2)}, u32[]{:S(2)}) collective-permute-start(bf16[784,128]{1,0:T(8,128)(2,1)S(1)} %collective-permute-done.1.refs_2_), channel_id=1, source_target_pairs={{0,1},{1,0},{2,3},{3,2},{4,5},{5,4},{6,7},{7,6},{8,9},{9,8},{10,11... | collective-permute-start | bytes 602120 | tf_op jit(solution)/shard_map/ppermute | solution.py:396
  23.7 3.6 %collective-permute-start.8 = (s32[1,128]{1,0:T(1,128)S(1)}, s32[1,128]{1,0:T(1,128)S(1)}, u32[]{:S(2)}, u32[]{:S(2)}) collective-permute-start(s32[1,128]{1,0:T(1,128)S(1)} %get-tuple-element.30.refs_0_), channel_id=1, source_target_pairs={{0,2},{1,3},{2,0},{3,1},{4,6},{5,7},{6,4},{7,5},{8,10},{9,11},{10,... | collective-permute-start | bytes 1544 | tf_op jit(solution)/shard_map/ppermute | solution.py:396
  25.4 11.1 %collective-permute-start.7 = (bf16[1024,128]{1,0:T(8,128)(2,1)S(1)}, bf16[1024,128]{1,0:T(8,128)(2,1)S(1)}, u32[]{:S(2)}, u32[]{:S(2)}) collective-permute-start(bf16[1024,128]{1,0:T(8,128)(2,1)S(1)} %get-tuple-element.29.q_ref), channel_id=1, source_target_pairs={{0,2},{1,3},{2,0},{3,1},{4,6},{5,7},{6,4},{7,5},{8,10},{9,11},{10,... | collective-permute-start | bytes 786440 | tf_op jit(solution)/shard_map/ppermute | solution.py:396
  28.5 31.8 %all-to-all-start = ((bf16[16,32,1024]{2,1,0:T(8,128)(2,1)}), bf16[16,32,1024]{2,1,0:T(8,128)(2,1)S(1)}, u32[]{:S(2)}, u32[]{:S(2)}) async-start(bf16[16,32,1024]{2,1,0:T(8,128)(2,1)} %deal.1.refs_8_), calls=%async_computation | async-start | bytes 2097152 | tf_op jit(solution)/shard_map/all_to_all | solution.py:416
  41.8 7.4 %collective-permute-start.10 = (f32[1,1024]{1,0:T(1,128)S(1)}, f32[1,1024]{1,0:T(1,128)S(1)}, u32[]{:S(2)}, u32[]{:S(2)}) collective-permute-start(f32[1,1024]{1,0:T(1,128)S(1)} %get-tuple-element.34.refs_8_.lse_ref), channel_id=1, source_target_pairs={{0,2},{1,3},{2,0},{3,1},{4,6},{5,7},{6,4},{7,5},{8,10},{9,11},{10,... | collective-permute-start | bytes 12296 | tf_op jit(solution)/shard_map/ppermute | solution.py:396
  49.0 3.7 %collective-permute-start.9 = (f32[1,1024]{1,0:T(1,128)S(1)}, f32[1,1024]{1,0:T(1,128)S(1)}, u32[]{:S(2)}, u32[]{:S(2)}) collective-permute-start(f32[1,1024]{1,0:T(1,128)S(1)} %get-tuple-element.35.lse_ref), channel_id=1, source_target_pairs={{0,2},{1,3},{2,0},{3,1},{4,6},{5,7},{6,4},{7,5},{8,10},{9,11},{10,... | collective-permute-start | bytes 12296 | tf_op jit(solution)/shard_map/ppermute | solution.py:396
  54.6 1.2 %collective-permute-start.11 = (f32[4,512]{1,0:T(4,128)S(1)}, f32[4,512]{1,0:T(4,128)S(1)}, u32[]{:S(2)}, u32[]{:S(2)}) collective-permute-start(f32[4,512]{1,0:T(4,128)S(1)} %bitcast.24), channel_id=1, source_target_pairs={{0,1},{1,0},{2,3},{3,2},{4,5},{5,4},{6,7},{7,6},{8,9},{9,8},{10,11... | collective-permute-start | bytes 24584 | tf_op jit(solution)/shard_map/ppermute | solution.py:396
  55.9 5.8 %collective-permute-start.13 = (f32[512]{0:T(512)S(1)}, f32[512]{0:T(512)S(1)}, u32[]{:S(2)}, u32[]{:S(2)}) collective-permute-start(f32[512]{0:T(512)S(1)} %bitcast.28), channel_id=1, source_target_pairs={{0,12},{1,13},{2,14},{3,15},{4,8},{5,9},{6,10},{7,11},{8,4},{9,5},... | collective-permute-start | bytes 6152 | tf_op jit(solution)/shard_map/ppermute | solution.py:396
  59.2 3.6 %collective-permute-start.14 = (f32[512]{0:T(512)S(1)}, f32[512]{0:T(512)S(1)}, u32[]{:S(2)}, u32[]{:S(2)}) collective-permute-start(f32[512]{0:T(512)S(1)} %bitcast.27), channel_id=1, source_target_pairs={{0,4},{1,5},{2,6},{3,7},{4,0},{5,1},{6,2},{7,3},{8,12},{9,13},{10,... | collective-permute-start | bytes 6152 | tf_op jit(solution)/shard_map/ppermute | solution.py:396
  59.2 4.5 %collective-permute-start.12 = (f32[512]{0:T(512)S(1)}, f32[512]{0:T(512)S(1)}, u32[]{:S(2)}, u32[]{:S(2)}) collective-permute-start(f32[512]{0:T(512)S(1)} %bitcast.26), channel_id=1, source_target_pairs={{0,8},{1,9},{2,10},{3,11},{4,12},{5,13},{6,14},{7,15},{8,0},{9,1},... | collective-permute-start | bytes 6152 | tf_op jit(solution)/shard_map/ppermute | solution.py:396

commit v10 on v8

--- a/solution.py
+++ b/solution.py
@@ -426,7 +426,7 @@
         partial = weigh(prob, tops, lse, others, factor, partial)
     partial = partial.reshape(CHIPS, 2, own_keys)
     chips = partial[:, 0] + swap(partial[:, 1], 1)
-    parts = [chips[0]] + [swap(chip, r) for chip, r in zip(chips[1:], far)]
+    parts = [chips[0]] + [swap(chip, r) for chip, r in zip(chips[:0:-1], far[::-1])]
     return (finish(parts, layer_kv), layer_kv)
 
 

time: 64.6 us -> 64.6 us (level)
  transfers between devices with their start and end apart: 16 -> 16, of which waited for: 9 -> 8; matrix products, arithmetic and copies ran while one was open for 0% -> 0% of each run, Pallas kernels for 46% -> 46%
where the time goes in v10:
time: 64.6 us; the launch traced here: 64.3 us
  Pallas kernels  31.5 us (49%)
  starting transfers between devices  23 us (36%)
  waiting for transfers between devices  8.43 us (13%)
  between operations  1.4 us (2%)
    ppermute x15, starting transfers between devices, swap(): return lax.ppermute(x, 'seq', [(i, i ^ r) for i in range(size)])  15 us
    pallas_call x1, Pallas kernels, project(): pl.pallas_call(functools.partial(project_kernel, cuts), in_specs=[ANY] *...  11.8 us
    pallas_call x2, Pallas kernels, score(): pl.pallas_call(functools.partial(score_kernel, keys, chunk, tile), in_spe...  10.5 us
    ppermute x15, waiting for transfers between devices, swap(): return lax.ppermute(x, 'seq', [(i, i ^ r) for i in range(size)])  8.42 us
    all_to_all x1, starting transfers between devices, shards(): lax.all_to_all(picked, 'seq', split_axis=0, concat_axis=0, tiled=True)  7.95 us
    pallas_call x2, Pallas kernels, weigh(): pl.pallas_call(functools.partial(weigh_kernel, factor, 1 + len(others), v...  3.7 us
    pallas_call x1, Pallas kernels, place(): pl.pallas_call(functools.partial(place_kernel, size), in_specs=[SMEM] + [...  1.35 us
    pallas_call x1, Pallas kernels, front(): pl.pallas_call(functools.partial(front_kernel, size, keys.shape[0]), in_s...  1.29 us
  transfers between devices with their start and end apart: 16, of which 8 were waited for; matrix products, arithmetic and copies ran while one was open for 0% of the time, Pallas kernels for 46%

profile of v10, /device:TPU:0, one launch (start us, length us, event | category | flops | bytes accessed | tf_op | source)
XLA Modules:
  0.0 64.3 jit_solution(18000835662282374594)
XLA Ops:
  1.3 1.3 %front.1 = (bf16[784,128]{1,0:T(8,128)(2,1)S(1)}, bf16[784,128]{1,0:T(8,128)(2,1)S(1)}, bf16[784,128]{1,0:T(8,128)(2,1)S(1)}, bf16[784,128]{1,0:T(8,128)(2,1)S(1)}) custom-call(s32[1]{0:T(128)} %bitcast.me_ref, s32[1]{0:T(128)S(6)} %copy.19.count_ref, bf16[512,512]{1,0:T(8,128)(2,1)} %keys_ref.1, bf16[32,4096]{1,0:T(8,128)(2,1)} %q_ref.1), custom_call_target="tpu_custom_call" | custom-call | bytes 1572864 | tf_op jit(solution)/shard_map/front/pallas_call | solution.py:139
  2.6 4.1 %collective-permute-start.1 = (bf16[784,128]{1,0:T(8,128)(2,1)S(1)}, bf16[784,128]{1,0:T(8,128)(2,1)S(1)}, u32[]{:S(2)}, u32[]{:S(2)}) collective-permute-start(bf16[784,128]{1,0:T(8,128)(2,1)S(1)} %get-tuple-element.21), channel_id=1, source_target_pairs={{0,8},{1,9},{2,10},{3,11},{4,12},{5,13},{6,14},{7,15},{8,0},{9,1},... | collective-permute-start | bytes 602120 | tf_op jit(solution)/shard_map/ppermute | solution.py:391
  6.7 1.3 %collective-permute-start.3 = (bf16[784,128]{1,0:T(8,128)(2,1)S(1)}, bf16[784,128]{1,0:T(8,128)(2,1)S(1)}, u32[]{:S(2)}, u32[]{:S(2)}) collective-permute-start(bf16[784,128]{1,0:T(8,128)(2,1)S(1)} %get-tuple-element.23), channel_id=1, source_target_pairs={{0,12},{1,13},{2,14},{3,15},{4,8},{5,9},{6,10},{7,11},{8,4},{9,5},... | collective-permute-start | bytes 602120 | tf_op jit(solution)/shard_map/ppermute | solution.py:391
  8.0 0.2 collective-permute-start.5
  8.3 0.0 collective-permute-start
  8.3 0.0 copy-start
  8.3 11.8 %project.1.rows_ref = bf16[512,1024]{1,0:T(8,128)(2,1)S(1)} custom-call(bf16[512,8192]{1,0:T(8,128)(2,1)} %x_hbm.1, f32[1,8192]{1,0:T(1,128)} %bitcast.29, bf16[8192,1024]{1,0:T(8,128)(2,1)} %weight_hbm.1, f32[1,1024]{1,0:T(1,128)} %bitcast.30), custom_call_target="tpu_custom_call" | custom-call | flops 8589934592 | bytes 25165824 | tf_op jit(solution)/shard_map/project/pallas_call | solution.py:88
  20.1 0.0 copy-done
  20.1 1.0 %choose.1.refs_2_ = bf16[16,32,1024]{2,1,0:T(8,128)(2,1)S(1)} custom-call(s32[1,512]{1,0:T(1,128)S(1)} %bitcast.23, bf16[512,1024]{1,0:T(8,128)(2,1)S(1)} %project.1.rows_ref), custom_call_target="tpu_custom_call" | custom-call | flops 805306368 | bytes 2097152 | tf_op jit(solution)/shard_map/choose/pallas_call | solution.py:195
  21.1 0.0 collective-permute-done.1.refs_2_
  21.1 0.0 collective-permute-done.3.refs_4_
  21.1 0.5 collective-permute-done.5.refs_6_
  21.7 0.0 collective-permute-start.6
  21.7 0.5 collective-permute-start.4
  22.2 0.0 collective-permute-start.2
  22.2 0.0 collective-permute-done.refs_1_
  22.2 0.9 %collective-permute-done.6.refs_7_ = bf16[784,128]{1,0:T(8,128)(2,1)S(1)} collective-permute-done((bf16[784,128]{1,0:T(8,128)(2,1)S(1)}, bf16[784,128]{1,0:T(8,128)(2,1)S(1)}, u32[]{:S(2)}, u32[]{:S(2)}) %collective-permute-start.6) | collective-permute-done | bytes 200736 | tf_op jit(solution)/shard_map/ppermute | solution.py:391
  23.1 0.3 collective-permute-done.4.refs_5_
  23.4 0.3 collective-permute-done.2.refs_3_
  23.7 1.6 %collective-permute-start.8 = (s32[1,128]{1,0:T(1,128)S(1)}, s32[1,128]{1,0:T(1,128)S(1)}, u32[]{:S(2)}, u32[]{:S(2)}) collective-permute-start(s32[1,128]{1,0:T(1,128)S(1)} %get-tuple-element.30.refs_0_), channel_id=1, source_target_pairs={{0,2},{1,3},{2,0},{3,1},{4,6},{5,7},{6,4},{7,5},{8,10},{9,11},{10,... | collective-permute-start | bytes 1544 | tf_op jit(solution)/shard_map/ppermute | solution.py:391
  25.4 0.5 collective-permute-start.7
  25.8 1.5 %collective-permute-done.8.refs_1_ = s32[1,128]{1,0:T(1,128)S(1)} collective-permute-done((s32[1,128]{1,0:T(1,128)S(1)}, s32[1,128]{1,0:T(1,128)S(1)}, u32[]{:S(2)}, u32[]{:S(2)}) %collective-permute-start.8) | collective-permute-done | bytes 544 | tf_op jit(solution)/shard_map/ppermute | solution.py:391
  27.3 1.3 %deal.1.refs_8_ = bf16[16,32,1024]{2,1,0:T(8,128)(2,1)} custom-call(s32[1]{0:T(128)} %bitcast.me_ref, s32[1,128]{1,0:T(1,128)S(1)} %get-tuple-element.30.refs_0_, s32[1,128]{1,0:T(1,128)S(1)} %collective-permute-done.8.refs_1_, bf16[16,32,1024]{2,1,0:T(8,128)(2,1)S(1)} %choose.1.refs_2_), custom_call_target="tpu_custom_call" | custom-call | flops 20000000000 | bytes 2097152 | tf_op jit(solution)/shard_map/deal/pallas_call | solution.py:220
  28.6 7.9 %all-to-all-start = ((bf16[16,32,1024]{2,1,0:T(8,128)(2,1)}), bf16[16,32,1024]{2,1,0:T(8,128)(2,1)S(1)}, u32[]{:S(2)}, u32[]{:S(2)}) async-start(bf16[16,32,1024]{2,1,0:T(8,128)(2,1)} %deal.1.refs_8_), calls=%async_computation | async-start | bytes 2097152 | tf_op jit(solution)/shard_map/all_to_all | solution.py:411
  36.5 0.0 collective-permute-done.7.q_ref
  36.5 5.2 %score.2 = (bf16[4096,1024]{1,0:T(8,128)(2,1)S(1)}, f32[16,1024]{1,0:T(8,128)S(1)}, f32[1,1024]{1,0:T(1,128)S(1)}) custom-call(bf16[1024,128]{1,0:T(8,128)(2,1)S(1)} %collective-permute-done.7.q_ref, bf16[784,128]{1,0:T(8,128)(2,1)S(1)} %get-tuple-element.20.refs_0_, bf16[784,128]{1,0:T(8,128)(2,1)S(1)} %collective-permute-done.refs_1_, ...), custom_call_target="tpu_custom_call" | custom-call | flops 8589934592 | bytes 8388608 | tf_op jit(solution)/shard_map/score/pallas_call | solution.py:299
  41.8 2.0 %collective-permute-start.10 = (f32[1,1024]{1,0:T(1,128)S(1)}, f32[1,1024]{1,0:T(1,128)S(1)}, u32[]{:S(2)}, u32[]{:S(2)}) collective-permute-start(f32[1,1024]{1,0:T(1,128)S(1)} %get-tuple-element.34.refs_8_.lse_ref), channel_id=1, source_target_pairs={{0,2},{1,3},{2,0},{3,1},{4,6},{5,7},{6,4},{7,5},{8,10},{9,11},{10,... | collective-permute-start | bytes 12296 | tf_op jit(solution)/shard_map/ppermute | solution.py:391
  43.8 5.2 %score.3 = (bf16[4096,1024]{1,0:T(8,128)(2,1)S(1)}, f32[16,1024]{1,0:T(8,128)S(1)}, f32[1,1024]{1,0:T(1,128)S(1)}) custom-call(bf16[1024,128]{1,0:T(8,128)(2,1)S(1)} %get-tuple-element.29.q_ref, bf16[784,128]{1,0:T(8,128)(2,1)S(1)} %get-tuple-element.20.refs_0_, bf16[784,128]{1,0:T(8,128)(2,1)S(1)} %collective-permute-done.refs_1_, ...), custom_call_target="tpu_custom_call" | custom-call | flops 8589934592 | bytes 8388608 | tf_op jit(solution)/shard_map/score/pallas_call | solution.py:299
  49.0 0.2 collective-permute-start.9
  49.2 0.0 collective-permute-done.10.rest_0_
  49.2 1.8 %weigh.2.rest_1_ = f32[16,256]{1,0:T(8,128)S(1)} custom-call(bf16[4096,1024]{1,0:T(8,128)(2,1)S(1)} %get-tuple-element.36.prob_ref, f32[16,1024]{1,0:T(8,128)S(1)} %get-tuple-element.37.top_ref, f32[1,1024]{1,0:T(1,128)S(1)} %get-tuple-element.35.lse_ref, f32[1,1024]{1,0:T(1,128)S(1)} %collective-permute-done.10.rest_0_), custom_call_target="tpu_custom_call" | custom-call | flops 16777216 | bytes 8388608 | tf_op jit(solution)/shard_map/weigh/pallas_call | solution.py:355
  51.0 1.7 %collective-permute-done.9.rest_0_ = f32[1,1024]{1,0:T(1,128)S(1)} collective-permute-done((f32[1,1024]{1,0:T(1,128)S(1)}, f32[1,1024]{1,0:T(1,128)S(1)}, u32[]{:S(2)}, u32[]{:S(2)}) %collective-permute-start.9) | collective-permute-done | bytes 4128 | tf_op jit(solution)/shard_map/ppermute | solution.py:391
  52.7 1.9 %weigh.3 = f32[16,256]{1,0:T(8,128)S(1)} custom-call(bf16[4096,1024]{1,0:T(8,128)(2,1)S(1)} %get-tuple-element.32.prob_ref, f32[16,1024]{1,0:T(8,128)S(1)} %get-tuple-element.33.top_ref, f32[1,1024]{1,0:T(1,128)S(1)} %get-tuple-element.34.refs_8_.lse_ref, f32[1,1024]{1,0:T(1,128)S(1)} %collective-permute-done.9.rest_0_, f32[16,256]{1,0:T(8,128)S(1)} %weigh.2.rest_1_), custom_call_target="tpu_custom_call" | custom-call | flops 16777216 | bytes 8388608 | tf_op jit(solution)/shard_map/weigh/pallas_call | solution.py:355
  54.6 0.1 collective-permute-start.11
  54.7 1.2 %collective-permute-done.11 = f32[4,512]{1,0:T(4,128)S(1)} collective-permute-done((f32[4,512]{1,0:T(4,128)S(1)}, f32[4,512]{1,0:T(4,128)S(1)}, u32[]{:S(2)}, u32[]{:S(2)}) %collective-permute-start.11) | collective-permute-done | bytes 8224 | tf_op jit(solution)/shard_map/ppermute | solution.py:391
  55.9 3.4 %collective-permute-start.13 = (f32[512]{0:T(512)S(1)}, f32[512]{0:T(512)S(1)}, u32[]{:S(2)}, u32[]{:S(2)}) collective-permute-start(f32[512]{0:T(512)S(1)} %bitcast.28), channel_id=1, source_target_pairs={{0,12},{1,13},{2,14},{3,15},{4,8},{5,9},{6,10},{7,11},{8,4},{9,5},... | collective-permute-start | bytes 6152 | tf_op jit(solution)/shard_map/ppermute | solution.py:391
  59.3 0.0 collective-permute-start.14
  59.3 1.1 %collective-permute-start.12 = (f32[512]{0:T(512)S(1)}, f32[512]{0:T(512)S(1)}, u32[]{:S(2)}, u32[]{:S(2)}) collective-permute-start(f32[512]{0:T(512)S(1)} %bitcast.26), channel_id=1, source_target_pairs={{0,4},{1,5},{2,6},{3,7},{4,0},{5,1},{6,2},{7,3},{8,12},{9,13},{10,... | collective-permute-start | bytes 6152 | tf_op jit(solution)/shard_map/ppermute | solution.py:391
  60.4 0.0 all-to-all-done
  60.4 1.4 %place.1.refs_4_ = bf16[256,1024]{1,0:T(8,128)(2,1)} custom-call(s32[1]{0:T(128)} %bitcast.me_ref, s32[1,128]{1,0:T(1,128)S(1)} %get-tuple-element.30.refs_0_, s32[1,128]{1,0:T(1,128)S(1)} %collective-permute-done.8.refs_1_, bf16[512,1024]{1,0:T(8,128)(2,1)S(1)} %bitcast.19), custom_call_target="tpu_custom_call" | custom-call | flops 268435456 | bytes 1572864 | tf_op jit(solution)/shard_map/place/pallas_call | solution.py:254
  61.7 0.0 collective-permute-done.13
  61.7 2.0 %collective-permute-done.14 = f32[512]{0:T(512)S(1)} collective-permute-done((f32[512]{0:T(512)S(1)}, f32[512]{0:T(512)S(1)}, u32[]{:S(2)}, u32[]{:S(2)}) %collective-permute-start.14) | collective-permute-done | bytes 2080 | tf_op jit(solution)/shard_map/ppermute | solution.py:391
  63.8 0.0 collective-permute-done.12
  63.8 0.6 finish.1
  (6 shorter events, 0.1 us)
Async XLA Ops:
  2.6 18.6 %collective-permute-start.1 = (bf16[784,128]{1,0:T(8,128)(2,1)S(1)}, bf16[784,128]{1,0:T(8,128)(2,1)S(1)}, u32[]{:S(2)}, u32[]{:S(2)}) collective-permute-start(bf16[784,128]{1,0:T(8,128)(2,1)S(1)} %get-tuple-element.21), channel_id=1, source_target_pairs={{0,8},{1,9},{2,10},{3,11},{4,12},{5,13},{6,14},{7,15},{8,0},{9,1},... | collective-permute-start | bytes 602120 | tf_op jit(solution)/shard_map/ppermute | solution.py:391
  6.7 14.5 %collective-permute-start.3 = (bf16[784,128]{1,0:T(8,128)(2,1)S(1)}, bf16[784,128]{1,0:T(8,128)(2,1)S(1)}, u32[]{:S(2)}, u32[]{:S(2)}) collective-permute-start(bf16[784,128]{1,0:T(8,128)(2,1)S(1)} %get-tuple-element.23), channel_id=1, source_target_pairs={{0,12},{1,13},{2,14},{3,15},{4,8},{5,9},{6,10},{7,11},{8,4},{9,5},... | collective-permute-start | bytes 602120 | tf_op jit(solution)/shard_map/ppermute | solution.py:391
  8.0 13.6 %collective-permute-start.5 = (bf16[784,128]{1,0:T(8,128)(2,1)S(1)}, bf16[784,128]{1,0:T(8,128)(2,1)S(1)}, u32[]{:S(2)}, u32[]{:S(2)}) collective-permute-start(bf16[784,128]{1,0:T(8,128)(2,1)S(1)} %get-tuple-element.26), channel_id=1, source_target_pairs={{0,4},{1,5},{2,6},{3,7},{4,0},{5,1},{6,2},{7,3},{8,12},{9,13},{10,... | collective-permute-start | bytes 602120 | tf_op jit(solution)/shard_map/ppermute | solution.py:391
  8.3 14.0 %collective-permute-start = (bf16[784,128]{1,0:T(8,128)(2,1)S(1)}, bf16[784,128]{1,0:T(8,128)(2,1)S(1)}, u32[]{:S(2)}, u32[]{:S(2)}) collective-permute-start(bf16[784,128]{1,0:T(8,128)(2,1)S(1)} %get-tuple-element.20.refs_0_), channel_id=1, source_target_pairs={{0,1},{1,0},{2,3},{3,2},{4,5},{5,4},{6,7},{7,6},{8,9},{9,8},{10,11... | collective-permute-start | bytes 602120 | tf_op jit(solution)/shard_map/ppermute | solution.py:391
  8.3 11.8 %copy-start = (s32[512]{0:T(512)S(1)}, s32[512]{0:T(512)}, u32[]{:S(2)}) copy-start(s32[512]{0:T(512)} %param.12) | copy-start | bytes 6148
  21.7 1.4 %collective-permute-start.6 = (bf16[784,128]{1,0:T(8,128)(2,1)S(1)}, bf16[784,128]{1,0:T(8,128)(2,1)S(1)}, u32[]{:S(2)}, u32[]{:S(2)}) collective-permute-start(bf16[784,128]{1,0:T(8,128)(2,1)S(1)} %collective-permute-done.5.refs_6_), channel_id=1, source_target_pairs={{0,1},{1,0},{2,3},{3,2},{4,5},{5,4},{6,7},{7,6},{8,9},{9,8},{10,11... | collective-permute-start | bytes 602120 | tf_op jit(solution)/shard_map/ppermute | solution.py:391
  21.7 1.7 %collective-permute-start.4 = (bf16[784,128]{1,0:T(8,128)(2,1)S(1)}, bf16[784,128]{1,0:T(8,128)(2,1)S(1)}, u32[]{:S(2)}, u32[]{:S(2)}) collective-permute-start(bf16[784,128]{1,0:T(8,128)(2,1)S(1)} %collective-permute-done.3.refs_4_), channel_id=1, source_target_pairs={{0,1},{1,0},{2,3},{3,2},{4,5},{5,4},{6,7},{7,6},{8,9},{9,8},{10,11... | collective-permute-start | bytes 602120 | tf_op jit(solution)/shard_map/ppermute | solution.py:391
  22.2 1.5 %collective-permute-start.2 = (bf16[784,128]{1,0:T(8,128)(2,1)S(1)}, bf16[784,128]{1,0:T(8,128)(2,1)S(1)}, u32[]{:S(2)}, u32[]{:S(2)}) collective-permute-start(bf16[784,128]{1,0:T(8,128)(2,1)S(1)} %collective-permute-done.1.refs_2_), channel_id=1, source_target_pairs={{0,1},{1,0},{2,3},{3,2},{4,5},{5,4},{6,7},{7,6},{8,9},{9,8},{10,11... | collective-permute-start | bytes 602120 | tf_op jit(solution)/shard_map/ppermute | solution.py:391
  23.7 3.6 %collective-permute-start.8 = (s32[1,128]{1,0:T(1,128)S(1)}, s32[1,128]{1,0:T(1,128)S(1)}, u32[]{:S(2)}, u32[]{:S(2)}) collective-permute-start(s32[1,128]{1,0:T(1,128)S(1)} %get-tuple-element.30.refs_0_), channel_id=1, source_target_pairs={{0,2},{1,3},{2,0},{3,1},{4,6},{5,7},{6,4},{7,5},{8,10},{9,11},{10,... | collective-permute-start | bytes 1544 | tf_op jit(solution)/shard_map/ppermute | solution.py:391
  25.4 11.2 %collective-permute-start.7 = (bf16[1024,128]{1,0:T(8,128)(2,1)S(1)}, bf16[1024,128]{1,0:T(8,128)(2,1)S(1)}, u32[]{:S(2)}, u32[]{:S(2)}) collective-permute-start(bf16[1024,128]{1,0:T(8,128)(2,1)S(1)} %get-tuple-element.29.q_ref), channel_id=1, source_target_pairs={{0,2},{1,3},{2,0},{3,1},{4,6},{5,7},{6,4},{7,5},{8,10},{9,11},{10,... | collective-permute-start | bytes 786440 | tf_op jit(solution)/shard_map/ppermute | solution.py:391
  28.6 31.8 %all-to-all-start = ((bf16[16,32,1024]{2,1,0:T(8,128)(2,1)}), bf16[16,32,1024]{2,1,0:T(8,128)(2,1)S(1)}, u32[]{:S(2)}, u32[]{:S(2)}) async-start(bf16[16,32,1024]{2,1,0:T(8,128)(2,1)} %deal.1.refs_8_), calls=%async_computation | async-start | bytes 2097152 | tf_op jit(solution)/shard_map/all_to_all | solution.py:411
  41.8 7.4 %collective-permute-start.10 = (f32[1,1024]{1,0:T(1,128)S(1)}, f32[1,1024]{1,0:T(1,128)S(1)}, u32[]{:S(2)}, u32[]{:S(2)}) collective-permute-start(f32[1,1024]{1,0:T(1,128)S(1)} %get-tuple-element.34.refs_8_.lse_ref), channel_id=1, source_target_pairs={{0,2},{1,3},{2,0},{3,1},{4,6},{5,7},{6,4},{7,5},{8,10},{9,11},{10,... | collective-permute-start | bytes 12296 | tf_op jit(solution)/shard_map/ppermute | solution.py:391
  49.0 3.7 %collective-permute-start.9 = (f32[1,1024]{1,0:T(1,128)S(1)}, f32[1,1024]{1,0:T(1,128)S(1)}, u32[]{:S(2)}, u32[]{:S(2)}) collective-permute-start(f32[1,1024]{1,0:T(1,128)S(1)} %get-tuple-element.35.lse_ref), channel_id=1, source_target_pairs={{0,2},{1,3},{2,0},{3,1},{4,6},{5,7},{6,4},{7,5},{8,10},{9,11},{10,... | collective-permute-start | bytes 12296 | tf_op jit(solution)/shard_map/ppermute | solution.py:391
  54.6 1.2 %collective-permute-start.11 = (f32[4,512]{1,0:T(4,128)S(1)}, f32[4,512]{1,0:T(4,128)S(1)}, u32[]{:S(2)}, u32[]{:S(2)}) collective-permute-start(f32[4,512]{1,0:T(4,128)S(1)} %bitcast.24), channel_id=1, source_target_pairs={{0,1},{1,0},{2,3},{3,2},{4,5},{5,4},{6,7},{7,6},{8,9},{9,8},{10,11... | collective-permute-start | bytes 24584 | tf_op jit(solution)/shard_map/ppermute | solution.py:391
  55.9 5.8 %collective-permute-start.13 = (f32[512]{0:T(512)S(1)}, f32[512]{0:T(512)S(1)}, u32[]{:S(2)}, u32[]{:S(2)}) collective-permute-start(f32[512]{0:T(512)S(1)} %bitcast.28), channel_id=1, source_target_pairs={{0,12},{1,13},{2,14},{3,15},{4,8},{5,9},{6,10},{7,11},{8,4},{9,5},... | collective-permute-start | bytes 6152 | tf_op jit(solution)/shard_map/ppermute | solution.py:391
  59.3 4.5 %collective-permute-start.14 = (f32[512]{0:T(512)S(1)}, f32[512]{0:T(512)S(1)}, u32[]{:S(2)}, u32[]{:S(2)}) collective-permute-start(f32[512]{0:T(512)S(1)} %bitcast.27), channel_id=1, source_target_pairs={{0,8},{1,9},{2,10},{3,11},{4,12},{5,13},{6,14},{7,15},{8,0},{9,1},... | collective-permute-start | bytes 6152 | tf_op jit(solution)/shard_map/ppermute | solution.py:391
  59.3 4.5 %collective-permute-start.12 = (f32[512]{0:T(512)S(1)}, f32[512]{0:T(512)S(1)}, u32[]{:S(2)}, u32[]{:S(2)}) collective-permute-start(f32[512]{0:T(512)S(1)} %bitcast.26), channel_id=1, source_target_pairs={{0,4},{1,5},{2,6},{3,7},{4,0},{5,1},{6,2},{7,3},{8,12},{9,13},{10,... | collective-permute-start | bytes 6152 | tf_op jit(solution)/shard_map/ppermute | solution.py:391
